TPU v7x, 32 devices: a whole 2x2x4 slice. The times are simulated.
32 devices in a mesh: ex: 8 (over y, x, core), feat: 4 (over z).
Axes of the slice: x: 2, y: 2, z: 4, core: 2. Of those that a mesh axis runs over, the one named last changes fastest.
Arguments:
- features: bfloat16 [16384, 2048], P('ex', 'feat'), may hold values from -0.125 to 0.125
- weights: float32 [2048], P('feat'), may hold values from -6 to 6
- labels: int32 [16384], P('ex'), may hold values 0 or 1
- signs: int32 [16384], P('ex'), may hold values from -1 to 1, as said below
- samples: int32 [2048], replicated, may hold values from 0 to 16383
- radius: float32 [1], replicated, may hold values from 0.1 to 0.25
Outputs:
- new_weights: float32 [2048], P('feat')
Inputs may be any that keep to these rules, and one draw needn't show every extreme that they name: `signs`: each entry is -1 or +1.
All inputs are finite; a program needn't handle non-finite values. No bound on the sum of `labels` on one device may be relied on, other than what follows from the above.
Results may differ from a plain program's by a relative error of at most 0.00067.
Values may be sent and summed in bfloat16 or wider, within the bound.
No kernel may reach another device: no remote copies, remote signals or barrier semaphores. Data moves between devices by JAX's collectives and lax.ppermute only.
A program may use at most 192 MiB of HBM per device.

v0:
```python
import functools
import math

import jax
import jax.numpy as jnp
from jax import lax
from jax.experimental import pallas as pl
from jax.experimental.pallas import tpu as pltpu
from jax.sharding import PartitionSpec as P

D = 2048
ITERS = 4
REG = 0.02
BLOCK = 128
PIVOTS = 8
CHUNK = 256
GROUP = 4


def split(value):
    high = value.astype(jnp.bfloat16)
    low = (value - high.astype(jnp.float32)).astype(jnp.bfloat16)
    return high, low


def invert_block(block, pieces=()):
    tiles = BLOCK // PIVOTS
    lane = lax.broadcasted_iota(jnp.int32, (PIVOTS, BLOCK), 1)
    sub = lax.broadcasted_iota(jnp.int32, (PIVOTS, BLOCK), 0)
    shape = (PIVOTS, BLOCK)
    held = [block[t * PIVOTS : (t + 1) * PIVOTS, :] for t in range(tiles)]
    plain, scaled_rows = [], []
    for step in range(tiles):
        first = step * PIVOTS
        rows = held[step]
        inside = (lane >= first) & (lane < first + PIVOTS)
        before = lane < first + PIVOTS
        last = step + 1 == tiles

        def columns(tile):
            return [
                jnp.broadcast_to(tile[:, first + j : first + j + 1], shape) for j in range(PIVOTS)
            ]

        wide = columns(rows)
        cell = {}
        for j in range(PIVOTS):
            for i in range(j, PIVOTS):
                cell[i, j] = jnp.broadcast_to(wide[j][i : i + 1, :], shape)
        rows = jnp.where(inside, (lane - first == sub).astype(jnp.float32), rows)
        line = [jnp.broadcast_to(rows[i : i + 1, :], shape) for i in range(PIVOTS)]
        if not last:
            ahead = columns(held[step + 1])
            total = jnp.where(inside, 0.0, held[step + 1])
        scaled = {}
        pairs = []
        for j in range(0, PIVOTS, 2):
            a, b, d = cell[j, j], cell[j + 1, j], cell[j + 1, j + 1]
            inverse = 1.0 / (a * d - b * b)
            pairs.append((a * inverse, b * inverse, d * inverse))
            for i in range(j + 2, PIVOTS):
                one, two = cell[i, j], cell[i, j + 1]
                scaled[i, j] = one * d - two * b
                scaled[i, j + 1] = two * a - one * b
            for i in range(j + 2, PIVOTS):
                for m in range(j + 2, i + 1):
                    product = scaled[i, j] * cell[m, j] + scaled[i, j + 1] * cell[m, j + 1]
                    cell[i, m] = cell[i, m] - product * inverse
            if not last:
                one = ahead[j] * d - ahead[j + 1] * b
                two = ahead[j + 1] * a - ahead[j] * b
                for m in range(j + 2, PIVOTS):
                    product = one * cell[m, j] + two * cell[m, j + 1]
                    ahead[m] = ahead[m] - product * inverse
                total = total - (one * line[j] + two * line[j + 1]) * inverse
            for i in range(j + 2, PIVOTS):
                scaled[i, j] = scaled[i, j] * inverse
                scaled[i, j + 1] = scaled[i, j + 1] * inverse
                line[i] = line[i] - (scaled[i, j] * line[j] + scaled[i, j + 1] * line[j + 1])
        if not last:
            held[step + 1] = total
        for j in range(PIVOTS - 2, -1, -2):
            a, b, d = pairs[j // 2]
            one = line[j] * d - line[j + 1] * b
            two = line[j + 1] * a - line[j] * b
            for i in range(j + 2, PIVOTS):
                one = one - scaled[i, j] * line[i]
                two = two - scaled[i, j + 1] * line[i]
            line[j], line[j + 1] = one, two
        for t in range(step + 2, tiles):
            total = jnp.where(inside, 0.0, held[t])
            for j, column in enumerate(columns(held[t])):
                total = total - column * line[j]
            held[t] = total
        plain.append(jnp.where(before, rows, 0.0))
        rows = line[0]
        for j in range(1, PIVOTS):
            rows = jnp.where(sub == j, line[j], rows)
        scaled_rows.append(jnp.where(before, rows, 0.0))
        for piece in pieces[step * len(pieces) // tiles : (step + 1) * len(pieces) // tiles]:
            piece()
    high, low = split(jnp.concatenate(plain, axis=0))
    left = jnp.concatenate([high, low, high, low], axis=0)
    high, low = split(jnp.concatenate(scaled_rows, axis=0))
    right = jnp.concatenate([high, high, low, low], axis=0)
    return lax.dot_general(
        left, right, (((0,), (0,)), ((), ())), preferred_element_type=jnp.float32
    )


def factor_kernel(pieces, work, inv_ref, sketch, right, left, sem):
    size = work.shape[0]
    blocks = size // BLOCK
    feat_count = pieces.shape[1]
    width = size // feat_count
    copies = [
        pltpu.make_async_copy(
            pieces.at[:, f], sketch.at[:, :, f * width : (f + 1) * width], sem.at[f]
        )
        for f in range(feat_count)
    ]
    for copy in copies:
        copy.start()
    for copy in copies:
        copy.wait()
    samples = sketch.shape[0] * sketch.shape[1]

    chunks = size // CHUNK

    def chunk(c):
        return slice(c * CHUNK, (c + 1) * CHUNK)

    def gram(m, _):
        start = pl.multiple_of(m * CHUNK, CHUNK)
        here = pl.ds(start, CHUNK)
        for c in range(chunks):

            @pl.when(c >= m)
            def _():
                product = lax.dot_general(
                    sketch[:, :, here].reshape(samples, CHUNK),
                    sketch[:, :, chunk(c)].reshape(samples, CHUNK),
                    (((0,), (0,)), ((), ())),
                    preferred_element_type=jnp.float32,
                )
                row = start + lax.broadcasted_iota(jnp.int32, product.shape, 0)
                col = c * CHUNK + lax.broadcasted_iota(jnp.int32, product.shape, 1)
                work[here, chunk(c)] = jnp.where(row == col, product + REG / D, product)

        return 0

    lax.fori_loop(0, chunks, gram, 0)
    eye = (
        lax.broadcasted_iota(jnp.int32, (BLOCK, BLOCK), 0)
        == lax.broadcasted_iota(jnp.int32, (BLOCK, BLOCK), 1)
    ).astype(jnp.float32)

    def prepare(k, inverse, lowest):
        here = pl.ds(pl.multiple_of(k * BLOCK, BLOCK), BLOCK)
        inv_ref[here, :] = inverse
        high, low = split(inverse)
        diag = jnp.concatenate([high, high, low, low], axis=0)
        work[here, here] = eye
        for c in range(chunks):
            panel = work[here, chunk(c)]
            high, low = split(panel)
            right[0:BLOCK, chunk(c)] = high
            right[BLOCK : 2 * BLOCK, chunk(c)] = high
            right[2 * BLOCK : 3 * BLOCK, chunk(c)] = low
            right[3 * BLOCK : 4 * BLOCK, chunk(c)] = low
            if c >= lowest:
                high, low = split(panel.T)
                wide = jnp.concatenate([high, low, high, low], axis=1)
                scaled = jnp.dot(wide, diag, preferred_element_type=jnp.float32)
                place = c * CHUNK + lax.broadcasted_iota(jnp.int32, (CHUNK, BLOCK), 0)
                high, low = split(jnp.where(place >= (k + 1) * BLOCK, scaled, 0.0))
                left[chunk(c), :] = jnp.concatenate([high, low, high, low], axis=1)

    def update(k, m, c, lowest):
        product = jnp.dot(
            left[chunk(m), :], right[:, chunk(c)], preferred_element_type=jnp.float32
        )
        value = work[chunk(m), chunk(c)]
        if lowest <= c < lowest + GROUP * BLOCK // CHUNK:
            row = m * CHUNK + lax.broadcasted_iota(jnp.int32, value.shape, 0)
            col = c * CHUNK + lax.broadcasted_iota(jnp.int32, value.shape, 1)
            fresh = (col >= k * BLOCK) & (col < (k + 1) * BLOCK) & (row >= (k + 1) * BLOCK)
            value = jnp.where(fresh, 0.0, value)
        work[chunk(m), chunk(c)] = value - product

    prepare(0, invert_block(work[0:BLOCK, 0:BLOCK]), 0)
    for first in range(0, blocks, GROUP):
        lowest = first * BLOCK // CHUNK
        settled = lowest + GROUP * BLOCK // CHUNK
        wanted = [
            (m, c) for m in range(lowest, chunks) for c in range(chunks) if c < settled or c >= m
        ]

        def outer(k, _):
            following = pl.ds(pl.multiple_of((k + 1) * BLOCK, BLOCK), BLOCK)
            block = work[following, following] - jnp.dot(
                left[following, :], right[:, following], preferred_element_type=jnp.float32
            )
            inverse = invert_block(
                block, [functools.partial(update, k, m, c, lowest) for m, c in wanted]
            )
            prepare(k + 1, inverse, lowest)
            return 0

        lax.fori_loop(first, min(first + GROUP, blocks - 1), outer, 0)
    for k in range(blocks):
        last = k // GROUP * GROUP + GROUP
        if k + 1 < last:
            work[k * BLOCK : (k + 1) * BLOCK, (k + 1) * BLOCK : last * BLOCK] = jnp.zeros(
                (BLOCK, (last - k - 1) * BLOCK), jnp.float32
            )


VMEM = pl.BlockSpec(memory_space=pltpu.VMEM)


def factor(pieces, interpret=False):
    ex_count, feat_count, rows, width = pieces.shape
    size = feat_count * width
    return pl.pallas_call(
        factor_kernel,
        in_specs=[pl.BlockSpec(memory_space=pl.ANY)],
        out_specs=[VMEM, VMEM],
        out_shape=[
            pltpu.VMEM((size, size), jnp.float32),
            pltpu.VMEM((size, BLOCK), jnp.float32),
        ],
        scratch_shapes=[
            pltpu.VMEM((ex_count, rows, size), jnp.bfloat16),
            pltpu.VMEM((4 * BLOCK, size), jnp.bfloat16),
            pltpu.VMEM((size, 4 * BLOCK), jnp.bfloat16),
            pltpu.SemaphoreType.DMA((feat_count,)),
        ],
        compiler_params=pltpu.CompilerParams(vmem_limit_bytes=36 * 2**20),
        interpret=interpret,
    )(pieces)


def apply_inverse(lower, inverses, residual, column):
    size = residual.shape[1]
    blocks = size // BLOCK
    eye = lax.broadcasted_iota(jnp.int32, (BLOCK, BLOCK), 0) == lax.broadcasted_iota(
        jnp.int32, (BLOCK, BLOCK), 1
    )
    for group in range(0, blocks, GROUP):
        used = group + GROUP

        def down(k, _):
            here = pl.ds(pl.multiple_of(k * BLOCK, BLOCK), BLOCK)
            sums = jnp.zeros((BLOCK, BLOCK), jnp.float32)
            for c in range(used):
                cols = slice(c * BLOCK, (c + 1) * BLOCK)
                sums = sums + lower[here, cols] * residual[:, cols]
            middle = jnp.sum(sums, axis=1, keepdims=True)
            row = jnp.sum(inverses[here, :] * middle, axis=0, keepdims=True)
            middle = jnp.sum(jnp.where(eye, row, 0.0), axis=1, keepdims=True)
            column[here, :] = jnp.broadcast_to(middle, (BLOCK, BLOCK))
            return 0

        lax.fori_loop(group, used, down, 0, unroll=True)
    total = tuple(jnp.zeros((8, BLOCK), jnp.float32) for _ in range(blocks))
    for group in range(0, blocks, GROUP):
        used = group + GROUP

        def up(t, total):
            here = pl.ds(pl.multiple_of(t * 32, 32), 32)
            middle = column[here, :]
            fresh = list(total)
            for c in range(used):
                cols = slice(c * BLOCK, (c + 1) * BLOCK)
                product = lower[here, cols] * middle
                fresh[c] = fresh[c] + jnp.sum(product.reshape(4, 8, BLOCK), axis=0)
            return tuple(fresh)

        total = lax.fori_loop(group * BLOCK // 32, used * BLOCK // 32, up, total)
    return jnp.concatenate([jnp.sum(t, axis=0, keepdims=True) for t in total], axis=1)


def curve(rows_ref, direction):
    count, size = rows_ref.shape
    blocks = size // BLOCK
    high = 16

    def step(i, total):
        here = pl.ds(pl.multiple_of(i * high, high), high)
        tile = rows_ref[here, :].astype(jnp.float32)
        sums = jnp.zeros((high, BLOCK), jnp.float32)
        for c in range(blocks):
            cols = slice(c * BLOCK, (c + 1) * BLOCK)
            sums = sums + tile[:, cols] * direction[:, cols]
        column = jnp.sum(sums, axis=1, keepdims=True)
        fresh = list(total)
        for c in range(blocks):
            product = tile[:, c * BLOCK : (c + 1) * BLOCK] * column
            fresh[c] = fresh[c] + (product[:8] + product[8:])
        return tuple(fresh)

    total = tuple(jnp.zeros((8, BLOCK), jnp.float32) for _ in range(blocks))
    total = lax.fori_loop(0, count // high, step, total, unroll=4)
    return jnp.concatenate([jnp.sum(t, axis=0, keepdims=True) for t in total], axis=1)


def dot(left, right):
    return jnp.sum(left * right, axis=1, keepdims=True)


def first_kernel(lower, inverses, rows, residual, direction, inner, curved, column):
    solved = apply_inverse(lower, inverses, residual[...], column)
    inner[...] = dot(residual[...], solved)
    direction[...] = solved
    curved[...] = curve(rows, direction)


def next_kernel(
    total_rows, lower, inverses, rows, sums, solution, residual, direction, inner,
    solution_out, residual_out, direction_out, inner_out, curved_out, column,
):
    ahead = direction[...]
    curved = sums[...] / total_rows + (REG / D) * ahead
    size = inner[...] / dot(ahead, curved)
    solution_out[...] = solution[...] + size * ahead
    left = residual[...] - size * curved
    residual_out[...] = left
    solved = apply_inverse(lower, inverses, left, column)
    fresh = dot(left, solved)
    inner_out[...] = fresh
    direction_out[...] = solved + fresh / inner[...] * ahead
    curved_out[...] = curve(rows, direction_out)


def last_kernel(total_rows, sums, solution, direction, inner, radius, out):
    ahead = direction[...]
    curved = sums[...] / total_rows + (REG / D) * ahead
    size = inner[...] / dot(ahead, curved)
    full = solution[...] + size * ahead
    length_sq = dot(full, full)
    scale = jnp.minimum(1.0, radius[...] * math.sqrt(D) / jnp.sqrt(length_sq + 1e-06))
    out[...] = scale * full


def call(kernel, shapes, args, scratch=()):
    args = list(args)
    for place, value in enumerate(args):
        if value.size >= BLOCK * D:
            args[place] = pltpu.with_memory_space_constraint(value, pltpu.VMEM)
    return pl.pallas_call(
        kernel,
        in_specs=[VMEM] * len(args),
        out_specs=[VMEM] * len(shapes),
        out_shape=[jax.ShapeDtypeStruct(shape, jnp.float32) for shape in shapes],
        scratch_shapes=scratch,
        compiler_params=pltpu.CompilerParams(vmem_limit_bytes=8 * 2**20),
    )(*args)


def exchange(value, axis):
    count = lax.axis_size(axis)
    pieces = [value]
    for mask in range(1, count):
        pieces.append(lax.ppermute(value, axis, [(s, s ^ mask) for s in range(count)]))
    return pieces


def swap(value, axis, bit):
    mask = 2**bit
    return lax.ppermute(value, axis, [(s, s ^ mask) for s in range(lax.axis_size(axis))])


def bit_places(order):
    places = [0]
    for bit in reversed(order):
        places = places + [place | 2**bit for place in places]
    return places


def sampled_mix(samples, places, signed):
    count = lax.axis_size("ex")
    grid = samples.reshape(count * 2, -1)
    upward = list(range(1, count.bit_length() - 1))
    downward = upward[::-1]
    wanted = [(q, 0) for q in bit_places(upward)] + [(q, 1) for q in bit_places(downward)]
    numbers = jnp.array([[q ^ 1, half] for q, half in wanted] + [[q, half] for q, half in wanted])
    rows = grid[(numbers[:, 0] ^ lax.axis_index("ex")) * 2 + numbers[:, 1]].reshape(2, -1)

    def mix(chosen):
        odd = lax.population_count(chosen[:, None] & places[None, :]) & 1
        table = (1 - 2 * odd).astype(jnp.bfloat16)
        return jnp.dot(table, signed, preferred_element_type=jnp.float32)

    total = swap(mix(rows[0]), "ex", 0) + mix(rows[1])
    parts = list(jnp.split(total, 2))
    for bits in zip(upward, downward):
        halves = [jnp.split(part, 2) for part in parts]
        got = [swap(half[1], "ex", bit) for half, bit in zip(halves, bits)]
        got = lax.optimization_barrier(got)
        parts = [half[0] + other for half, other in zip(halves, got)]
    return jnp.concatenate(parts)


def butterfly(value):
    for axis in ("ex", "feat"):
        count = lax.axis_size(axis)
        mask = 1
        while mask < count:
            value = value + lax.ppermute(value, axis, [(s, s ^ mask) for s in range(count)])
            mask = mask * 2
    return value


def local(features, weights, labels, signs, samples, radius):
    highest = lax.Precision.HIGHEST
    row_count, feat_width = features.shape
    ex_count = lax.axis_size("ex")
    ex_index = lax.axis_index("ex")
    feat_count = lax.axis_size("feat")
    feat_index = lax.axis_index("feat")
    total_rows = row_count * ex_count
    sample_count = samples.shape[0]
    dense = features.astype(jnp.float32)
    margins = sum(exchange(jnp.dot(dense, weights, precision=highest), "feat"))
    probability = 1.0 / (1.0 + jnp.exp(-margins))
    curvature = probability * (1.0 - probability)
    weighted = (jnp.sqrt(curvature)[:, None] * dense).astype(jnp.bfloat16)
    signed = weighted * signs.astype(jnp.bfloat16)[:, None]
    places = ex_index * row_count + lax.iota(jnp.int32, row_count)
    total = sampled_mix(samples, places, signed)
    sketch = (total * (1.0 / math.sqrt(total_rows * sample_count))).astype(jnp.bfloat16)
    pieces = lax.all_gather(lax.all_gather(sketch, "feat", axis=0), "ex", axis=0)
    lower, inverses = factor(pieces)

    grad_part = jnp.dot(probability - labels.astype(jnp.float32), dense, precision=highest)
    gradient = lax.psum(grad_part, "ex") / total_rows + (REG / D) * weights
    own_rows = lax.all_to_all(weighted, "feat", split_axis=0, concat_axis=1, tiled=True)
    residual = -lax.all_gather(gradient, "feat", axis=0, tiled=True)[None, :]

    row, one = (1, D), (1, 1)
    scratch = [pltpu.VMEM((D, BLOCK), jnp.float32)]
    direction, inner, curved = call(
        first_kernel, [row, one, row], [lower, inverses, own_rows, residual], scratch
    )
    solution = jnp.zeros(row, jnp.float32)
    following = functools.partial(next_kernel, total_rows)
    for _ in range(ITERS - 1):
        solution, residual, direction, inner, curved = call(
            following,
            [row, row, row, one, row],
            [lower, inverses, own_rows, butterfly(curved), solution, residual, direction, inner],
            scratch,
        )
    (step,) = call(
        functools.partial(last_kernel, total_rows),
        [row],
        [butterfly(curved), solution, direction, inner, radius[None, :]],
    )
    own = lax.dynamic_slice_in_dim(step[0], feat_index * feat_width, feat_width, 0)
    return weights + own


def solution(mesh):
    in_specs = (P("ex", "feat"), P("feat"), P("ex"), P("ex"), P(), P())
    out_specs = P("feat")
    return jax.shard_map(local, mesh=mesh, in_specs=in_specs, out_specs=out_specs, check_vma=False)
```

profile of v0, /device:TPU:0, one launch (start us, length us, event | category | flops | bytes accessed | tf_op | source)
XLA Modules:
  0.0 355.8 jit_solution(2231835697968704282)
XLA Ops:
  6.6 3.5 fusion.27
  10.1 3.0 collective-permute-start
  13.1 2.6 collective-permute-start.1
  15.7 0.6 gather_fusion
  16.4 1.3 collective-permute-done.1
  17.7 3.5 collective-permute-done.2
  21.2 0.5 multiply_convert_fusion
  21.7 2.4 fusion
  24.2 4.1 %collective-permute-done.3 = f32[1024,512]{1,0:T(8,128)S(1)} collective-permute-done((f32[1024,512]{1,0:T(8,128)S(1)}, f32[1024,512]{1,0:T(8,128)S(1)}, u32[]{:S(2)}, u32[]{:S(2)}) %collective-permute-start.3) | collective-permute-done | bytes 2097184 | tf_op jit(solution)/shard_map/ppermute | solution.py:371
  28.3 2.4 fusion.12
  30.8 1.5 collective-permute-start.4
  32.4 1.5 collective-permute-start.5
  33.9 11.0 %collective-permute-done.4 = f32[256,512]{1,0:T(8,128)S(1)} collective-permute-done((f32[256,512]{1,0:T(8,128)S(1)}, f32[256,512]{1,0:T(8,128)S(1)}, u32[]{:S(2)}, u32[]{:S(2)}) %collective-permute-start.4) | collective-permute-done | bytes 524320 | tf_op jit(solution)/shard_map/ppermute | solution.py:371
  44.9 1.2 collective-permute-done.5
  46.1 0.2 slice_add_fusion
  46.3 1.6 collective-permute-start.6
  47.9 0.6 collective-permute-start.7
  48.5 5.1 %collective-permute-done.6 = f32[128,512]{1,0:T(8,128)S(1)} collective-permute-done((f32[128,512]{1,0:T(8,128)S(1)}, f32[128,512]{1,0:T(8,128)S(1)}, u32[]{:S(2)}, u32[]{:S(2)}) %collective-permute-start.6) | collective-permute-done | bytes 262176 | tf_op jit(solution)/shard_map/ppermute | solution.py:371
  53.6 1.3 collective-permute-done.7
  54.9 0.1 fusion.18
  55.0 0.7 fusion.17
  55.8 24.4 %all-gather.5.cloned.1.call-done = bf16[4,256,512]{2,1,0:T(8,128)(2,1)} async-done(((bf16[1,256,512]{2,1,0:T(8,128)(2,1)}), bf16[4,256,512]{2,1,0:T(8,128)(2,1)}) %all-gather.5.cloned.1.call-update) | async-done | bytes 1048592 | tf_op jit(solution)/shard_map/all_gather | solution.py:433
  80.2 4.4 %all-to-all-start = ((bf16[4,512,512]{2,1,0:T(8,128)(2,1)}), bf16[4,512,512]{2,1,0:T(8,128)(2,1)}, u32[]{:S(2)}, u32[]{:S(2)}) async-start(bf16[4,512,512]{2,1,0:T(8,128)(2,1)} %bitcast.37), calls=%async_computation | async-start | bytes 4194304 | tf_op jit(solution)/shard_map/all_to_all | solution.py:438
  84.7 0.9 fusion.28
  85.6 14.5 %psum.7 = f32[512]{0:T(512)S(1)} all-reduce(f32[512]{0:T(512)S(1)} %bitcast.44), channel_id=1, replica_groups=mesh['ex'=8,'feat'=4] {'ex'}, use_global_device_ids=true, to_apply=%region_0.0 | all-reduce | flops 512 | bytes 4096 | tf_op jit(solution)/shard_map/psum | solution.py:437
  100.1 38.2 %all-gather.1 = f32[4,1,512]{2,1,0:T(1,128)S(1)} all-gather(f32[1,1,512]{2,1,0:T(1,128)S(1)} %bitcast.45), channel_id=1, replica_groups=mesh['ex'=8,'feat'=4] {'feat'}, dimensions={0}, use_global_device_ids=true | all-gather | bytes 10240 | tf_op jit(solution)/shard_map/all_gather | solution.py:439
  138.3 1.9 copy.10
  140.2 118.7 %shard_map.73 = (f32[2048,2048]{1,0:T(8,128)S(1)}, f32[2048,128]{1,0:T(8,128)S(1)}) custom-call(bf16[8,4,256,512]{3,2,1,0:T(8,128)(2,1)} %bitcast.36), custom_call_target="tpu_custom_call" | custom-call | tf_op jit(solution)/shard_map/pallas_call | solution.py:225
  259.0 4.5 %shard_map.74 = (f32[1,2048]{1,0:T(1,128)S(1)}, f32[1,1]{1,0:T(1,128)}, f32[1,2048]{1,0:T(1,128)S(1)}) custom-call(f32[2048,2048]{1,0:T(8,128)S(1)} %get-tuple-element.32.lower, f32[2048,128]{1,0:T(8,128)S(1)} %get-tuple-element.33.inverses, bf16[512,2048]{1,0:T(8,128)(2,1)S(1)} %bitcast.30, f32[1,2048]{1,0:T(1,128)S(1)} %bitcast.34), custom_call_target="tpu_custom_call" | custom-call | tf_op jit(solution)/shard_map/pallas_call | solution.py:351
  263.5 1.2 collective-permute-done.8
  264.7 1.6 collective-permute-start.9
  266.3 2.1 collective-permute-done.9
  268.4 1.6 collective-permute-start.10
  270.0 2.2 collective-permute-done.10
  272.2 3.6 %collective-permute-done.11 = f32[1,2048]{1,0:T(1,128)S(1)} collective-permute-done((f32[1,2048]{1,0:T(1,128)S(1)}, f32[1,2048]{1,0:T(1,128)S(1)}, u32[]{:S(2)}, u32[]{:S(2)}) %collective-permute-start.11) | collective-permute-done | bytes 8224 | tf_op jit(solution)/shard_map/ppermute | solution.py:410
  275.9 0.1 collective-permute-start.12
  276.0 4.5 %collective-permute-done.12 = f32[1,2048]{1,0:T(1,128)S(1)} collective-permute-done((f32[1,2048]{1,0:T(1,128)S(1)}, f32[1,2048]{1,0:T(1,128)S(1)}, u32[]{:S(2)}, u32[]{:S(2)}) %collective-permute-start.12) | collective-permute-done | bytes 8224 | tf_op jit(solution)/shard_map/ppermute | solution.py:410
  280.5 5.3 %shard_map.75 = (f32[1,2048]{1,0:T(1,128)S(1)}, f32[1,2048]{1,0:T(1,128)S(1)}, f32[1,2048]{1,0:T(1,128)S(1)}, f32[1,1]{1,0:T(1,128)}, f32[1,2048]{1,0:T(1,128)S(1)}) custom-call(f32[2048,2048]{1,0:T(8,128)S(1)} %get-tuple-element.32.lower, f32[2048,128]{1,0:T(8,128)S(1)} %get-tuple-element.33.inverses, bf16[512,2048]{1,0:T(8,128)(2,1)S(1)} %bitcast.31, ...), custom_call_target="tpu_custom_call" | custom-call | tf_op jit(solution)/shard_map/pallas_call | solution.py:351
  285.8 1.2 collective-permute-done.13
  287.0 1.6 collective-permute-start.14
  288.7 2.1 collective-permute-done.14
  290.7 1.6 collective-permute-start.15
  292.3 2.2 collective-permute-done.15
  294.6 3.6 %collective-permute-done.16 = f32[1,2048]{1,0:T(1,128)S(1)} collective-permute-done((f32[1,2048]{1,0:T(1,128)S(1)}, f32[1,2048]{1,0:T(1,128)S(1)}, u32[]{:S(2)}, u32[]{:S(2)}) %collective-permute-start.16) | collective-permute-done | bytes 8224 | tf_op jit(solution)/shard_map/ppermute | solution.py:410
  298.3 4.5 %collective-permute-done.17 = f32[1,2048]{1,0:T(1,128)S(1)} collective-permute-done((f32[1,2048]{1,0:T(1,128)S(1)}, f32[1,2048]{1,0:T(1,128)S(1)}, u32[]{:S(2)}, u32[]{:S(2)}) %collective-permute-start.17) | collective-permute-done | bytes 8224 | tf_op jit(solution)/shard_map/ppermute | solution.py:410
  302.8 5.0 %shard_map.76 = (f32[1,2048]{1,0:T(1,128)S(1)}, f32[1,2048]{1,0:T(1,128)S(1)}, f32[1,2048]{1,0:T(1,128)S(1)}, f32[1,1]{1,0:T(1,128)}, f32[1,2048]{1,0:T(1,128)S(1)}) custom-call(f32[2048,2048]{1,0:T(8,128)S(1)} %get-tuple-element.32.lower, f32[2048,128]{1,0:T(8,128)S(1)} %get-tuple-element.33.inverses, bf16[512,2048]{1,0:T(8,128)(2,1)S(1)} %bitcast.32, ...), custom_call_target="tpu_custom_call" | custom-call | tf_op jit(solution)/shard_map/pallas_call | solution.py:351
  307.8 1.2 collective-permute-done.18
  309.0 1.6 collective-permute-start.19
  310.6 2.1 collective-permute-done.19
  312.7 1.6 collective-permute-start.20
  314.3 2.2 collective-permute-done.20
  316.5 3.6 %collective-permute-done.21 = f32[1,2048]{1,0:T(1,128)S(1)} collective-permute-done((f32[1,2048]{1,0:T(1,128)S(1)}, f32[1,2048]{1,0:T(1,128)S(1)}, u32[]{:S(2)}, u32[]{:S(2)}) %collective-permute-start.21) | collective-permute-done | bytes 8224 | tf_op jit(solution)/shard_map/ppermute | solution.py:410
  320.2 0.1 collective-permute-start.22
  320.3 4.5 %collective-permute-done.22 = f32[1,2048]{1,0:T(1,128)S(1)} collective-permute-done((f32[1,2048]{1,0:T(1,128)S(1)}, f32[1,2048]{1,0:T(1,128)S(1)}, u32[]{:S(2)}, u32[]{:S(2)}) %collective-permute-start.22) | collective-permute-done | bytes 8224 | tf_op jit(solution)/shard_map/ppermute | solution.py:410
  324.8 5.1 %shard_map.77 = (f32[1,2048]{1,0:T(1,128)S(1)}, f32[1,2048]{1,0:T(1,128)}, f32[1,2048]{1,0:T(1,128)S(1)}, f32[1,1]{1,0:T(1,128)}, f32[1,2048]{1,0:T(1,128)S(1)}) custom-call(f32[2048,2048]{1,0:T(8,128)S(1)} %get-tuple-element.32.lower, f32[2048,128]{1,0:T(8,128)S(1)} %get-tuple-element.33.inverses, bf16[512,2048]{1,0:T(8,128)(2,1)S(1)} %bitcast.33, ...), custom_call_target="tpu_custom_call" | custom-call | tf_op jit(solution)/shard_map/pallas_call | solution.py:351
  329.9 1.2 collective-permute-done.23
  331.1 1.6 collective-permute-start.24
  332.7 2.1 collective-permute-done.24
  334.8 1.6 collective-permute-start.25
  336.4 2.2 collective-permute-done.25
  338.6 3.6 %collective-permute-done.26 = f32[1,2048]{1,0:T(1,128)S(1)} collective-permute-done((f32[1,2048]{1,0:T(1,128)S(1)}, f32[1,2048]{1,0:T(1,128)S(1)}, u32[]{:S(2)}, u32[]{:S(2)}) %collective-permute-start.26) | collective-permute-done | bytes 8224 | tf_op jit(solution)/shard_map/ppermute | solution.py:410
  343.0 3.9 %collective-permute-done.27 = f32[1,2048]{1,0:T(1,128)S(1)} collective-permute-done((f32[1,2048]{1,0:T(1,128)S(1)}, f32[1,2048]{1,0:T(1,128)S(1)}, u32[]{:S(2)}, u32[]{:S(2)}) %collective-permute-start.27) | collective-permute-done | bytes 8224 | tf_op jit(solution)/shard_map/ppermute | solution.py:410
  346.9 1.0 shard_map.78
  347.9 0.6 add.151
  (69 shorter events, 1.1 us)
Async XLA Ops:
  6.5 9.2 %copy-start = (s32[2048]{0:T(1024)S(1)}, s32[2048]{0:T(1024)}, u32[]{:S(2)}) copy-start(s32[2048]{0:T(1024)} %param.11) | copy-start | bytes 24580
  6.5 9.2 %copy-start.6 = (s32[16,1]{0,1:T(1,128)S(1)}, s32[16,1]{0,1:T(1,128)}, u32[]{:S(2)}) copy-start(s32[16,1]{0,1:T(1,128)} %constant.38) | copy-start | bytes 196
  6.5 9.2 %copy-start.7 = (s32[16,1]{0,1:T(1,128)S(1)}, s32[16,1]{0,1:T(1,128)}, u32[]{:S(2)}) copy-start(s32[16,1]{0,1:T(1,128)} %constant.39) | copy-start | bytes 196
  6.5 14.6 %copy-start.1 = (bf16[2048,512]{1,0:T(8,128)(2,1)S(1)}, bf16[2048,512]{1,0:T(8,128)(2,1)}, u32[]{:S(2)}) copy-start(bf16[2048,512]{1,0:T(8,128)(2,1)} %param.7) | copy-start | bytes 6291460
  6.5 9.8 %copy-start.5 = (s32[2048]{0:T(1024)S(1)}, s32[2048]{0:T(1024)}, u32[]{:S(2)}) copy-start(s32[2048]{0:T(1024)} %param.10) | copy-start | bytes 24580
  6.5 14.6 %copy-start.4 = (s32[2048]{0:T(1024)S(1)}, s32[2048]{0:T(1024)}, u32[]{:S(2)}) copy-start(s32[2048]{0:T(1024)} %param.9) | copy-start | bytes 24580
  6.6 73.6 %all-gather.5.cloned.1.call-start = ((), (), s32[]{:S(2)}) async-start(), calls=%async_computation.1 | async-start | bytes 1310720 | tf_op jit(solution)/shard_map/all_gather | solution.py:433
  10.1 6.3 %collective-permute-start = (f32[2048]{0:T(1024)S(1)}, f32[2048]{0:T(1024)S(1)}, u32[]{:S(2)}, u32[]{:S(2)}) collective-permute-start(f32[2048]{0:T(1024)S(1)} %bitcast.39), channel_id=1, source_target_pairs={{0,1},{1,0},{2,3},{3,2},{4,5},{5,4},{6,7},{7,6},{8,9},{9,8},{10,11... | collective-permute-start | bytes 24584 | tf_op jit(solution)/shard_map/ppermute | solution.py:365
  13.1 4.5 %collective-permute-start.1 = (f32[2048]{0:T(1024)S(1)}, f32[2048]{0:T(1024)S(1)}, u32[]{:S(2)}, u32[]{:S(2)}) collective-permute-start(f32[2048]{0:T(1024)S(1)} %bitcast.40), channel_id=1, source_target_pairs={{0,2},{1,3},{2,0},{3,1},{4,6},{5,7},{6,4},{7,5},{8,10},{9,11},{10,... | collective-permute-start | bytes 24584 | tf_op jit(solution)/shard_map/ppermute | solution.py:365
  15.7 5.4 %collective-permute-start.2 = (f32[2048]{0:T(1024)S(1)}, f32[2048]{0:T(1024)S(1)}, u32[]{:S(2)}, u32[]{:S(2)}) collective-permute-start(f32[2048]{0:T(1024)S(1)} %bitcast.41), channel_id=1, source_target_pairs={{0,3},{1,2},{2,1},{3,0},{4,7},{5,6},{6,5},{7,4},{8,11},{9,10},{10,... | collective-permute-start | bytes 24584 | tf_op jit(solution)/shard_map/ppermute | solution.py:365
  21.6 6.7 %copy-start.2 = (bf16[2048,512]{1,0:T(8,128)(2,1)}, bf16[2048,512]{1,0:T(8,128)(2,1)S(1)}, u32[]{:S(2)}) copy-start(bf16[2048,512]{1,0:T(8,128)(2,1)S(1)} %multiply_convert_fusion) | copy-start | bytes 6291460
  24.1 4.2 %collective-permute-start.3 = (f32[1024,512]{1,0:T(8,128)S(1)}, f32[1024,512]{1,0:T(8,128)S(1)}, u32[]{:S(2)}, u32[]{:S(2)}) collective-permute-start(f32[1024,512]{1,0:T(8,128)S(1)} %fusion), channel_id=1, source_target_pairs={{0,4},{4,0},{8,12},{12,8},{16,20},{20,16},{24,28},{28,24},{1,5},{5... | collective-permute-start | bytes 6291464 | tf_op jit(solution)/shard_map/ppermute | solution.py:371
  30.8 14.0 %collective-permute-start.4 = (f32[256,512]{1,0:T(8,128)S(1)}, f32[256,512]{1,0:T(8,128)S(1)}, u32[]{:S(2)}, u32[]{:S(2)}) collective-permute-start(f32[256,512]{1,0:T(8,128)S(1)} %get-tuple-element.56), channel_id=1, source_target_pairs={{0,8},{4,12},{8,0},{12,4},{16,24},{20,28},{24,16},{28,20},{1,9},{5... | collective-permute-start | bytes 1572872 | tf_op jit(solution)/shard_map/ppermute | solution.py:371
  32.4 13.7 %collective-permute-start.5 = (f32[256,512]{1,0:T(8,128)S(1)}, f32[256,512]{1,0:T(8,128)S(1)}, u32[]{:S(2)}, u32[]{:S(2)}) collective-permute-start(f32[256,512]{1,0:T(8,128)S(1)} %get-tuple-element.55), channel_id=1, source_target_pairs={{0,16},{4,20},{8,24},{12,28},{16,0},{20,4},{24,8},{28,12},{1,17},{... | collective-permute-start | bytes 1572872 | tf_op jit(solution)/shard_map/ppermute | solution.py:371
  46.3 7.3 %collective-permute-start.6 = (f32[128,512]{1,0:T(8,128)S(1)}, f32[128,512]{1,0:T(8,128)S(1)}, u32[]{:S(2)}, u32[]{:S(2)}) collective-permute-start(f32[128,512]{1,0:T(8,128)S(1)} %split.38), channel_id=1, source_target_pairs={{0,16},{4,20},{8,24},{12,28},{16,0},{20,4},{24,8},{28,12},{1,17},{... | collective-permute-start | bytes 786440 | tf_op jit(solution)/shard_map/ppermute | solution.py:371
  47.9 7.0 %collective-permute-start.7 = (f32[128,512]{1,0:T(8,128)S(1)}, f32[128,512]{1,0:T(8,128)S(1)}, u32[]{:S(2)}, u32[]{:S(2)}) collective-permute-start(f32[128,512]{1,0:T(8,128)S(1)} %split.40), channel_id=1, source_target_pairs={{0,8},{4,12},{8,0},{12,4},{16,24},{20,28},{24,16},{28,20},{1,9},{5... | collective-permute-start | bytes 786440 | tf_op jit(solution)/shard_map/ppermute | solution.py:371
  55.7 84.5 %all-gather.7.cloned.1.call-start = ((), (), s32[]{:S(2)}) async-start(), calls=%async_computation.2 | async-start | bytes 9437184 | tf_op jit(solution)/shard_map/all_gather | solution.py:433
  80.2 58.1 %all-to-all-start = ((bf16[4,512,512]{2,1,0:T(8,128)(2,1)}), bf16[4,512,512]{2,1,0:T(8,128)(2,1)}, u32[]{:S(2)}, u32[]{:S(2)}) async-start(bf16[4,512,512]{2,1,0:T(8,128)(2,1)} %bitcast.37), calls=%async_computation | async-start | bytes 4194304 | tf_op jit(solution)/shard_map/all_to_all | solution.py:438
  84.7 15.5 %copy-start.3 = (f32[512]{0:T(512)S(1)}, f32[512]{0:T(512)}, u32[]{:S(2)}) copy-start(f32[512]{0:T(512)} %param.8) | copy-start | bytes 6148
  263.5 1.2 collective-permute-start.8
  264.7 3.7 %collective-permute-start.9 = (f32[1,2048]{1,0:T(1,128)S(1)}, f32[1,2048]{1,0:T(1,128)S(1)}, u32[]{:S(2)}, u32[]{:S(2)}) collective-permute-start(f32[1,2048]{1,0:T(1,128)S(1)} %add.130), channel_id=1, source_target_pairs={{0,8},{4,12},{8,0},{12,4},{16,24},{20,28},{24,16},{28,20},{1,9},{5... | collective-permute-start | bytes 24584 | tf_op jit(solution)/shard_map/ppermute | solution.py:410
  268.4 3.7 %collective-permute-start.10 = (f32[1,2048]{1,0:T(1,128)S(1)}, f32[1,2048]{1,0:T(1,128)S(1)}, u32[]{:S(2)}, u32[]{:S(2)}) collective-permute-start(f32[1,2048]{1,0:T(1,128)S(1)} %add.131), channel_id=1, source_target_pairs={{0,16},{4,20},{8,24},{12,28},{16,0},{20,4},{24,8},{28,12},{1,17},{... | collective-permute-start | bytes 24584 | tf_op jit(solution)/shard_map/ppermute | solution.py:410
  272.2 3.7 %collective-permute-start.11 = (f32[1,2048]{1,0:T(1,128)S(1)}, f32[1,2048]{1,0:T(1,128)S(1)}, u32[]{:S(2)}, u32[]{:S(2)}) collective-permute-start(f32[1,2048]{1,0:T(1,128)S(1)} %add.132), channel_id=1, source_target_pairs={{0,1},{1,0},{2,3},{3,2},{4,5},{5,4},{6,7},{7,6},{8,9},{9,8},{10,11... | collective-permute-start | bytes 24584 | tf_op jit(solution)/shard_map/ppermute | solution.py:410
  275.9 4.6 %collective-permute-start.12 = (f32[1,2048]{1,0:T(1,128)S(1)}, f32[1,2048]{1,0:T(1,128)S(1)}, u32[]{:S(2)}, u32[]{:S(2)}) collective-permute-start(f32[1,2048]{1,0:T(1,128)S(1)} %add.133), channel_id=1, source_target_pairs={{0,2},{1,3},{2,0},{3,1},{4,6},{5,7},{6,4},{7,5},{8,10},{9,11},{10,... | collective-permute-start | bytes 24584 | tf_op jit(solution)/shard_map/ppermute | solution.py:410
  285.8 1.2 collective-permute-start.13
  287.0 3.7 %collective-permute-start.14 = (f32[1,2048]{1,0:T(1,128)S(1)}, f32[1,2048]{1,0:T(1,128)S(1)}, u32[]{:S(2)}, u32[]{:S(2)}) collective-permute-start(f32[1,2048]{1,0:T(1,128)S(1)} %add.135), channel_id=1, source_target_pairs={{0,8},{4,12},{8,0},{12,4},{16,24},{20,28},{24,16},{28,20},{1,9},{5... | collective-permute-start | bytes 24584 | tf_op jit(solution)/shard_map/ppermute | solution.py:410
  290.7 3.7 %collective-permute-start.15 = (f32[1,2048]{1,0:T(1,128)S(1)}, f32[1,2048]{1,0:T(1,128)S(1)}, u32[]{:S(2)}, u32[]{:S(2)}) collective-permute-start(f32[1,2048]{1,0:T(1,128)S(1)} %add.136), channel_id=1, source_target_pairs={{0,16},{4,20},{8,24},{12,28},{16,0},{20,4},{24,8},{28,12},{1,17},{... | collective-permute-start | bytes 24584 | tf_op jit(solution)/shard_map/ppermute | solution.py:410
  294.5 3.7 %collective-permute-start.16 = (f32[1,2048]{1,0:T(1,128)S(1)}, f32[1,2048]{1,0:T(1,128)S(1)}, u32[]{:S(2)}, u32[]{:S(2)}) collective-permute-start(f32[1,2048]{1,0:T(1,128)S(1)} %add.137), channel_id=1, source_target_pairs={{0,1},{1,0},{2,3},{3,2},{4,5},{5,4},{6,7},{7,6},{8,9},{9,8},{10,11... | collective-permute-start | bytes 24584 | tf_op jit(solution)/shard_map/ppermute | solution.py:410
  298.2 4.6 %collective-permute-start.17 = (f32[1,2048]{1,0:T(1,128)S(1)}, f32[1,2048]{1,0:T(1,128)S(1)}, u32[]{:S(2)}, u32[]{:S(2)}) collective-permute-start(f32[1,2048]{1,0:T(1,128)S(1)} %add.138), channel_id=1, source_target_pairs={{0,2},{1,3},{2,0},{3,1},{4,6},{5,7},{6,4},{7,5},{8,10},{9,11},{10,... | collective-permute-start | bytes 24584 | tf_op jit(solution)/shard_map/ppermute | solution.py:410
  307.8 1.2 collective-permute-start.18
  309.0 3.7 %collective-permute-start.19 = (f32[1,2048]{1,0:T(1,128)S(1)}, f32[1,2048]{1,0:T(1,128)S(1)}, u32[]{:S(2)}, u32[]{:S(2)}) collective-permute-start(f32[1,2048]{1,0:T(1,128)S(1)} %add.140), channel_id=1, source_target_pairs={{0,8},{4,12},{8,0},{12,4},{16,24},{20,28},{24,16},{28,20},{1,9},{5... | collective-permute-start | bytes 24584 | tf_op jit(solution)/shard_map/ppermute | solution.py:410
  312.7 3.7 %collective-permute-start.20 = (f32[1,2048]{1,0:T(1,128)S(1)}, f32[1,2048]{1,0:T(1,128)S(1)}, u32[]{:S(2)}, u32[]{:S(2)}) collective-permute-start(f32[1,2048]{1,0:T(1,128)S(1)} %add.141), channel_id=1, source_target_pairs={{0,16},{4,20},{8,24},{12,28},{16,0},{20,4},{24,8},{28,12},{1,17},{... | collective-permute-start | bytes 24584 | tf_op jit(solution)/shard_map/ppermute | solution.py:410
  316.5 3.7 %collective-permute-start.21 = (f32[1,2048]{1,0:T(1,128)S(1)}, f32[1,2048]{1,0:T(1,128)S(1)}, u32[]{:S(2)}, u32[]{:S(2)}) collective-permute-start(f32[1,2048]{1,0:T(1,128)S(1)} %add.142), channel_id=1, source_target_pairs={{0,1},{1,0},{2,3},{3,2},{4,5},{5,4},{6,7},{7,6},{8,9},{9,8},{10,11... | collective-permute-start | bytes 24584 | tf_op jit(solution)/shard_map/ppermute | solution.py:410
  320.2 4.6 %collective-permute-start.22 = (f32[1,2048]{1,0:T(1,128)S(1)}, f32[1,2048]{1,0:T(1,128)S(1)}, u32[]{:S(2)}, u32[]{:S(2)}) collective-permute-start(f32[1,2048]{1,0:T(1,128)S(1)} %add.143), channel_id=1, source_target_pairs={{0,2},{1,3},{2,0},{3,1},{4,6},{5,7},{6,4},{7,5},{8,10},{9,11},{10,... | collective-permute-start | bytes 24584 | tf_op jit(solution)/shard_map/ppermute | solution.py:410
  329.9 1.2 collective-permute-start.23
  331.1 3.7 %collective-permute-start.24 = (f32[1,2048]{1,0:T(1,128)S(1)}, f32[1,2048]{1,0:T(1,128)S(1)}, u32[]{:S(2)}, u32[]{:S(2)}) collective-permute-start(f32[1,2048]{1,0:T(1,128)S(1)} %add.145), channel_id=1, source_target_pairs={{0,8},{4,12},{8,0},{12,4},{16,24},{20,28},{24,16},{28,20},{1,9},{5... | collective-permute-start | bytes 24584 | tf_op jit(solution)/shard_map/ppermute | solution.py:410
  334.8 3.7 %collective-permute-start.25 = (f32[1,2048]{1,0:T(1,128)S(1)}, f32[1,2048]{1,0:T(1,128)S(1)}, u32[]{:S(2)}, u32[]{:S(2)}) collective-permute-start(f32[1,2048]{1,0:T(1,128)S(1)} %add.146), channel_id=1, source_target_pairs={{0,16},{4,20},{8,24},{12,28},{16,0},{20,4},{24,8},{28,12},{1,17},{... | collective-permute-start | bytes 24584 | tf_op jit(solution)/shard_map/ppermute | solution.py:410
  338.6 3.7 %collective-permute-start.26 = (f32[1,2048]{1,0:T(1,128)S(1)}, f32[1,2048]{1,0:T(1,128)S(1)}, u32[]{:S(2)}, u32[]{:S(2)}) collective-permute-start(f32[1,2048]{1,0:T(1,128)S(1)} %add.147), channel_id=1, source_target_pairs={{0,1},{1,0},{2,3},{3,2},{4,5},{5,4},{6,7},{7,6},{8,9},{9,8},{10,11... | collective-permute-start | bytes 24584 | tf_op jit(solution)/shard_map/ppermute | solution.py:410
  342.3 4.6 %collective-permute-start.27 = (f32[1,2048]{1,0:T(1,128)S(1)}, f32[1,2048]{1,0:T(1,128)S(1)}, u32[]{:S(2)}, u32[]{:S(2)}) collective-permute-start(f32[1,2048]{1,0:T(1,128)S(1)} %add.148), channel_id=1, source_target_pairs={{0,2},{1,3},{2,0},{3,1},{4,6},{5,7},{6,4},{7,5},{8,10},{9,11},{10,... | collective-permute-start | bytes 24584 | tf_op jit(solution)/shard_map/ppermute | solution.py:410
Sparse Core Ops, SparseCore 0:
  55.9 24.2 all-gather.4
  82.1 53.9 all-gather.6
where the time goes:
time: 362 us; the launch traced here: 356 us
  Pallas kernels  140 us (39%)
  waiting for transfers between devices  106 us (29%)
  blocking collectives  52.7 us (15%)
  starting transfers between devices  28.8 us (8%)
  between operations  14.9 us (4%)
  matrix products  9.24 us (3%)
    pallas_call x1, Pallas kernels, factor(): pl.pallas_call(factor_kernel, in_specs=[pl.BlockSpec(memory_space=pl.ANY)...  119 us
    ppermute x20, waiting for transfers between devices, butterfly(): lax.ppermute(value, axis, [(s, s ^ mask) for s in range(count)])  53.7 us
    all_gather x1, blocking collectives, local(): residual = -lax.all_gather(gradient, 'feat', axis=0, tiled=True)[None, :]  38.2 us
    all_gather x1, waiting for transfers between devices, local(): lax.all_gather(sketch, 'feat', axis=0)  24.4 us
    ppermute x5, waiting for transfers between devices, swap(): lax.ppermute(value, axis, [(s, s ^ mask) for s in range(lax.axis_size(axi...  22.7 us
    pallas_call x5, Pallas kernels, call(): pl.pallas_call(kernel, in_specs=[VMEM] * len(args), out_specs=[VMEM] * le...  20.8 us
    psum x1, blocking collectives, local(): gradient = lax.psum(grad_part, 'ex') / total_rows + REG / D * weights  14.5 us
    ppermute x20, starting transfers between devices, butterfly(): lax.ppermute(value, axis, [(s, s ^ mask) for s in range(count)])  13.4 us
  transfers between devices with their start and end apart: 31, of which 28 were waited for; matrix products, arithmetic and copies ran while one was open for 1% of the time, Pallas kernels for 0%

commit v1 on v0

--- a/solution.py
+++ b/solution.py
@@ -21,6 +21,12 @@
     high = value.astype(jnp.bfloat16)
     low = (value - high.astype(jnp.float32)).astype(jnp.bfloat16)
     return high, low
+
+
+def reciprocal(value):
+    guess = pl.reciprocal(value, approx=True)
+    guess = guess * (2.0 - value * guess)
+    return guess * (2.0 - value * guess)
 
 
 def invert_block(block, pieces=()):
@@ -56,7 +62,7 @@
         pairs = []
         for j in range(0, PIVOTS, 2):
             a, b, d = cell[j, j], cell[j + 1, j], cell[j + 1, j + 1]
-            inverse = 1.0 / (a * d - b * b)
+            inverse = reciprocal(a * d - b * b)
             pairs.append((a * inverse, b * inverse, d * inverse))
             for i in range(j + 2, PIVOTS):
                 one, two = cell[i, j], cell[i, j + 1]
@@ -108,23 +114,27 @@
     )
 
 
-def factor_kernel(pieces, work, inv_ref, sketch, right, left, sem):
+def factor_kernel(feat, upper, lower, work, inv_ref, sketch, right, wide, left, sem):
     size = work.shape[0]
     blocks = size // BLOCK
-    feat_count = pieces.shape[1]
+    feat_count = upper.shape[1]
     width = size // feat_count
-    copies = [
-        pltpu.make_async_copy(
-            pieces.at[:, f], sketch.at[:, :, f * width : (f + 1) * width], sem.at[f]
-        )
-        for f in range(feat_count)
-    ]
+    copies = []
+    for group, pieces in enumerate((upper, lower)):
+        for mask in range(feat_count):
+            start = pl.multiple_of((feat[0] ^ mask) * width, width)
+            copies.append(
+                pltpu.make_async_copy(
+                    pieces.at[:, mask],
+                    sketch.at[group, :, :, pl.ds(start, width)],
+                    sem.at[group, mask],
+                )
+            )
     for copy in copies:
         copy.start()
     for copy in copies:
         copy.wait()
-    samples = sketch.shape[0] * sketch.shape[1]
-
+    samples = sketch.shape[0] * sketch.shape[1] * sketch.shape[2]
     chunks = size // CHUNK
 
     def chunk(c):
@@ -138,8 +148,8 @@
             @pl.when(c >= m)
             def _():
                 product = lax.dot_general(
-                    sketch[:, :, here].reshape(samples, CHUNK),
-                    sketch[:, :, chunk(c)].reshape(samples, CHUNK),
+                    sketch[:, :, :, here].reshape(samples, CHUNK),
+                    sketch[:, :, :, chunk(c)].reshape(samples, CHUNK),
                     (((0,), (0,)), ((), ())),
                     preferred_element_type=jnp.float32,
                 )
@@ -150,31 +160,34 @@
         return 0
 
     lax.fori_loop(0, chunks, gram, 0)
-    eye = (
-        lax.broadcasted_iota(jnp.int32, (BLOCK, BLOCK), 0)
-        == lax.broadcasted_iota(jnp.int32, (BLOCK, BLOCK), 1)
-    ).astype(jnp.float32)
-
-    def prepare(k, inverse, lowest):
+
+    def stage(k, c, lowest):
         here = pl.ds(pl.multiple_of(k * BLOCK, BLOCK), BLOCK)
-        inv_ref[here, :] = inverse
+        panel = work[here, chunk(c)]
+        if lowest <= c <= lowest + GROUP * BLOCK // CHUNK:
+            row = lax.broadcasted_iota(jnp.int32, panel.shape, 0)
+            col = c * CHUNK - k * BLOCK + lax.broadcasted_iota(jnp.int32, panel.shape, 1)
+            unit = jnp.where(row == col, 1.0, 0.0)
+            panel = jnp.where((col >= 0) & (col < BLOCK), unit, panel)
+            work[here, chunk(c)] = panel
+        high, low = split(panel)
+        right[0:BLOCK, chunk(c)] = high
+        right[BLOCK : 2 * BLOCK, chunk(c)] = high
+        right[2 * BLOCK : 3 * BLOCK, chunk(c)] = low
+        right[3 * BLOCK : 4 * BLOCK, chunk(c)] = low
+        if c >= lowest:
+            high, low = split(panel.T)
+            wide[chunk(c), :] = jnp.concatenate([high, low, high, low], axis=1)
+
+    def finish(k, inverse, lowest):
+        inv_ref[pl.ds(pl.multiple_of(k * BLOCK, BLOCK), BLOCK), :] = inverse
         high, low = split(inverse)
         diag = jnp.concatenate([high, high, low, low], axis=0)
-        work[here, here] = eye
-        for c in range(chunks):
-            panel = work[here, chunk(c)]
-            high, low = split(panel)
-            right[0:BLOCK, chunk(c)] = high
-            right[BLOCK : 2 * BLOCK, chunk(c)] = high
-            right[2 * BLOCK : 3 * BLOCK, chunk(c)] = low
-            right[3 * BLOCK : 4 * BLOCK, chunk(c)] = low
-            if c >= lowest:
-                high, low = split(panel.T)
-                wide = jnp.concatenate([high, low, high, low], axis=1)
-                scaled = jnp.dot(wide, diag, preferred_element_type=jnp.float32)
-                place = c * CHUNK + lax.broadcasted_iota(jnp.int32, (CHUNK, BLOCK), 0)
-                high, low = split(jnp.where(place >= (k + 1) * BLOCK, scaled, 0.0))
-                left[chunk(c), :] = jnp.concatenate([high, low, high, low], axis=1)
+        for c in range(lowest, chunks):
+            scaled = jnp.dot(wide[chunk(c), :], diag, preferred_element_type=jnp.float32)
+            place = c * CHUNK + lax.broadcasted_iota(jnp.int32, (CHUNK, BLOCK), 0)
+            high, low = split(jnp.where(place >= (k + 1) * BLOCK, scaled, 0.0))
+            left[chunk(c), :] = jnp.concatenate([high, low, high, low], axis=1)
 
     def update(k, m, c, lowest):
         product = jnp.dot(
@@ -188,23 +201,26 @@
             value = jnp.where(fresh, 0.0, value)
         work[chunk(m), chunk(c)] = value - product
 
-    prepare(0, invert_block(work[0:BLOCK, 0:BLOCK]), 0)
+    inverse = invert_block(work[0:BLOCK, 0:BLOCK])
+    for c in range(chunks):
+        stage(0, c, 0)
+    finish(0, inverse, 0)
     for first in range(0, blocks, GROUP):
         lowest = first * BLOCK // CHUNK
         settled = lowest + GROUP * BLOCK // CHUNK
-        wanted = [
-            (m, c) for m in range(lowest, chunks) for c in range(chunks) if c < settled or c >= m
-        ]
 
         def outer(k, _):
             following = pl.ds(pl.multiple_of((k + 1) * BLOCK, BLOCK), BLOCK)
             block = work[following, following] - jnp.dot(
                 left[following, :], right[:, following], preferred_element_type=jnp.float32
             )
-            inverse = invert_block(
-                block, [functools.partial(update, k, m, c, lowest) for m, c in wanted]
-            )
-            prepare(k + 1, inverse, lowest)
+            pieces = []
+            for c in range(chunks):
+                for m in range(lowest, chunks):
+                    if c < settled or c >= m:
+                        pieces.append(functools.partial(update, k, m, c, lowest))
+                pieces.append(functools.partial(stage, k + 1, c, lowest))
+            finish(k + 1, invert_block(block, pieces), lowest)
             return 0
 
         lax.fori_loop(first, min(first + GROUP, blocks - 1), outer, 0)
@@ -219,26 +235,31 @@
 VMEM = pl.BlockSpec(memory_space=pltpu.VMEM)
 
 
-def factor(pieces, interpret=False):
-    ex_count, feat_count, rows, width = pieces.shape
+def factor(feat, upper, lower, interpret=False):
+    ex_count, feat_count, rows, width = upper.shape
     size = feat_count * width
     return pl.pallas_call(
         factor_kernel,
-        in_specs=[pl.BlockSpec(memory_space=pl.ANY)],
+        in_specs=[
+            pl.BlockSpec(memory_space=pltpu.SMEM),
+            pl.BlockSpec(memory_space=pl.ANY),
+            pl.BlockSpec(memory_space=pl.ANY),
+        ],
         out_specs=[VMEM, VMEM],
         out_shape=[
             pltpu.VMEM((size, size), jnp.float32),
             pltpu.VMEM((size, BLOCK), jnp.float32),
         ],
         scratch_shapes=[
-            pltpu.VMEM((ex_count, rows, size), jnp.bfloat16),
+            pltpu.VMEM((2, ex_count, rows, size), jnp.bfloat16),
             pltpu.VMEM((4 * BLOCK, size), jnp.bfloat16),
             pltpu.VMEM((size, 4 * BLOCK), jnp.bfloat16),
-            pltpu.SemaphoreType.DMA((feat_count,)),
+            pltpu.VMEM((size, 4 * BLOCK), jnp.bfloat16),
+            pltpu.SemaphoreType.DMA((2, feat_count)),
         ],
         compiler_params=pltpu.CompilerParams(vmem_limit_bytes=36 * 2**20),
         interpret=interpret,
-    )(pieces)
+    )(feat, upper, lower)
 
 
 def apply_inverse(lower, inverses, residual, column):
@@ -392,14 +413,16 @@
         table = (1 - 2 * odd).astype(jnp.bfloat16)
         return jnp.dot(table, signed, preferred_element_type=jnp.float32)
 
-    total = swap(mix(rows[0]), "ex", 0) + mix(rows[1])
+    total = swap(mix(rows[0]).astype(jnp.float16), "ex", 0).astype(jnp.float32) + mix(rows[1])
     parts = list(jnp.split(total, 2))
     for bits in zip(upward, downward):
         halves = [jnp.split(part, 2) for part in parts]
-        got = [swap(half[1], "ex", bit) for half, bit in zip(halves, bits)]
+        got = [
+            swap(half[1].astype(jnp.float16), "ex", bit) for half, bit in zip(halves, bits)
+        ]
         got = lax.optimization_barrier(got)
-        parts = [half[0] + other for half, other in zip(halves, got)]
-    return jnp.concatenate(parts)
+        parts = [half[0] + other.astype(jnp.float32) for half, other in zip(halves, got)]
+    return parts
 
 
 def butterfly(value):
@@ -428,15 +451,24 @@
     weighted = (jnp.sqrt(curvature)[:, None] * dense).astype(jnp.bfloat16)
     signed = weighted * signs.astype(jnp.bfloat16)[:, None]
     places = ex_index * row_count + lax.iota(jnp.int32, row_count)
-    total = sampled_mix(samples, places, signed)
-    sketch = (total * (1.0 / math.sqrt(total_rows * sample_count))).astype(jnp.bfloat16)
-    pieces = lax.all_gather(lax.all_gather(sketch, "feat", axis=0), "ex", axis=0)
-    lower, inverses = factor(pieces)
+    scale = 1.0 / math.sqrt(total_rows * sample_count)
+    upper, lower = [
+        (part * scale).astype(jnp.bfloat16) for part in sampled_mix(samples, places, signed)
+    ]
+    upper = jnp.stack(exchange(upper, "feat"))
+    upper, lower = lax.optimization_barrier((upper, lower))
+    lower = jnp.stack(exchange(lower, "feat"))
+    upper, lower = [lax.all_gather(value, "ex", axis=0) for value in (upper, lower)]
+    lower, inverses = factor(feat_index.astype(jnp.int32)[None], upper, lower)
 
     grad_part = jnp.dot(probability - labels.astype(jnp.float32), dense, precision=highest)
-    gradient = lax.psum(grad_part, "ex") / total_rows + (REG / D) * weights
+    own_weights = jnp.where(ex_index == 0, REG / D, 0.0) * weights
+    wide = jnp.zeros((feat_count, feat_width), jnp.float32)
+    wide = lax.dynamic_update_slice_in_dim(
+        wide, (grad_part / total_rows + own_weights)[None], feat_index, 0
+    )
+    residual = -butterfly(wide.reshape(1, D))
     own_rows = lax.all_to_all(weighted, "feat", split_axis=0, concat_axis=1, tiled=True)
-    residual = -lax.all_gather(gradient, "feat", axis=0, tiled=True)[None, :]
 
     row, one = (1, D), (1, 1)
     scratch = [pltpu.VMEM((D, BLOCK), jnp.float32)]

time: 362 us -> 360 us (level)
  blocking collectives: 52.7 us -> 0 us
  starting transfers between devices: 28.8 us -> 59.4 us
  waiting for transfers between devices: 106 us -> 115 us
  Pallas kernels: 140 us -> 145 us
  other arithmetic: 2.35 us -> 7.07 us
    all_gather x1 -> x0, blocking collectives: 38.2 us -> none  [local(): residual = -lax.all_gather(gradient, 'feat', axis=0, tiled=True)[None, :]]
    ppermute x20 -> x25, waiting for transfers between devices: 53.7 us -> 78.8 us  [butterfly(): lax.ppermute(value, axis, [(s, s ^ mask) for s in range(count)])]
    ppermute x20 -> x25, starting transfers between devices: 13.4 us -> 35.1 us  [butterfly(): lax.ppermute(value, axis, [(s, s ^ mask) for s in range(count)])]
    all_gather x2, waiting for transfers between devices: 24.4 us -> 5.29 us  [local(): lax.all_gather(value, 'ex', axis=0)]
    psum x1 -> x0, blocking collectives: 14.5 us -> none  [local(): gradient = lax.psum(grad_part, 'ex') / total_rows + REG / D * weights]
    ppermute x3 -> x9, waiting for transfers between devices: 4.78 us -> 17.7 us  [exchange(): lax.ppermute(value, axis, [(s, s ^ mask) for s in range(count)])]
    ppermute x5, waiting for transfers between devices: 22.7 us -> 13.6 us  [swap(): lax.ppermute(value, axis, [(s, s ^ mask) for s in range(lax.axis_size(axi...]
    ppermute x3 -> x9, starting transfers between devices: 5.63 us -> 14.5 us  [exchange(): lax.ppermute(value, axis, [(s, s ^ mask) for s in range(count)])]
  transfers between devices with their start and end apart: 31 -> 42, of which waited for: 28 -> 36; matrix products, arithmetic and copies ran while one was open for 1% -> 2% of each run, Pallas kernels for 0% -> 0%
where the time goes in v1:
time: 360 us; the launch traced here: 353 us
  Pallas kernels  145 us (40%)
  waiting for transfers between devices  115 us (32%)
  starting transfers between devices  59.4 us (16%)
  between operations  14.6 us (4%)
  matrix products  9.08 us (3%)
  other arithmetic  7.07 us (2%)
    pallas_call x1, Pallas kernels, factor(): pl.pallas_call(factor_kernel, in_specs=[pl.BlockSpec(memory_space=pltpu.S...  124 us
    ppermute x25, waiting for transfers between devices, butterfly(): lax.ppermute(value, axis, [(s, s ^ mask) for s in range(count)])  78.8 us
    ppermute x25, starting transfers between devices, butterfly(): lax.ppermute(value, axis, [(s, s ^ mask) for s in range(count)])  35.1 us
    pallas_call x5, Pallas kernels, call(): pl.pallas_call(kernel, in_specs=[VMEM] * len(args), out_specs=[VMEM] * le...  20.3 us
    ppermute x9, waiting for transfers between devices, exchange(): lax.ppermute(value, axis, [(s, s ^ mask) for s in range(count)])  17.7 us
    ppermute x9, starting transfers between devices, exchange(): lax.ppermute(value, axis, [(s, s ^ mask) for s in range(count)])  14.5 us
    ppermute x5, waiting for transfers between devices, swap(): lax.ppermute(value, axis, [(s, s ^ mask) for s in range(lax.axis_size(axi...  13.6 us
  transfers between devices with their start and end apart: 42, of which 36 were waited for; matrix products, arithmetic and copies ran while one was open for 2% of the time, Pallas kernels for 0%

profile of v1, /device:TPU:0, one launch (start us, length us, event | category | flops | bytes accessed | tf_op | source)
XLA Modules:
  0.0 353.2 jit_solution(14914197851359826932)
XLA Ops:
  6.5 3.3 fusion.31
  9.9 3.0 collective-permute-start
  12.9 2.6 collective-permute-start.1
  17.5 3.5 collective-permute-done.2
  21.7 2.0 multiply_convert_fusion
  23.7 2.4 fusion.14
  26.2 2.6 collective-permute-done.3
  28.9 2.4 fusion.30
  31.4 1.6 collective-permute-start.4
  33.0 1.5 collective-permute-start.5
  34.5 5.3 %collective-permute-done.4 = f16[256,512]{1,0:T(8,128)(2,1)S(1)} collective-permute-done((f16[256,512]{1,0:T(8,128)(2,1)S(1)}, f16[256,512]{1,0:T(8,128)(2,1)S(1)}, u32[]{:S(2)}, u32[]{:S(2)}) %collective-permute-start.4) | collective-permute-done | bytes 262176 | tf_op jit(solution)/shard_map/ppermute | solution.py:392
  41.3 1.6 collective-permute-start.6
  43.5 2.8 collective-permute-done.6
  46.3 1.6 collective-permute-done.7
  48.4 4.0 %collective-permute-start.9 = (bf16[128,512]{1,0:T(8,128)(2,1)S(1)}, bf16[128,512]{1,0:T(8,128)(2,1)S(1)}, u32[]{:S(2)}, u32[]{:S(2)}) collective-permute-start(bf16[128,512]{1,0:T(8,128)(2,1)S(1)} %fusion.22), channel_id=1, source_target_pairs={{0,2},{1,3},{2,0},{3,1},{4,6},{5,7},{6,4},{7,5},{8,10},{9,11},{10,... | collective-permute-start | bytes 393224 | tf_op jit(solution)/shard_map/ppermute | solution.py:386
  52.5 3.6 %collective-permute-done.10 = bf16[128,512]{1,0:T(8,128)(2,1)S(1)} collective-permute-done((bf16[128,512]{1,0:T(8,128)(2,1)S(1)}, bf16[128,512]{1,0:T(8,128)(2,1)S(1)}, u32[]{:S(2)}, u32[]{:S(2)}) %collective-permute-start.10) | collective-permute-done | bytes 131104 | tf_op jit(solution)/shard_map/ppermute | solution.py:386
  56.0 3.5 collective-permute-done.9
  60.5 1.5 collective-permute-start.12
  62.1 2.9 collective-permute-start.13
  65.6 6.5 %collective-permute-done.12 = bf16[128,512]{1,0:T(8,128)(2,1)S(1)} collective-permute-done((bf16[128,512]{1,0:T(8,128)(2,1)S(1)}, bf16[128,512]{1,0:T(8,128)(2,1)S(1)}, u32[]{:S(2)}, u32[]{:S(2)}) %collective-permute-start.12) | collective-permute-done | bytes 131104 | tf_op jit(solution)/shard_map/ppermute | solution.py:386
  73.0 4.5 %all-to-all-start = ((bf16[4,512,512]{2,1,0:T(8,128)(2,1)}), bf16[4,512,512]{2,1,0:T(8,128)(2,1)}, u32[]{:S(2)}, u32[]{:S(2)}) async-start(bf16[4,512,512]{2,1,0:T(8,128)(2,1)} %bitcast.42), calls=%async_computation | async-start | bytes 4194304 | tf_op jit(solution)/shard_map/all_to_all | solution.py:471
  80.6 3.2 collective-permute-done.15
  83.9 3.8 %collective-permute-done.16 = f32[1,2048]{1,0:T(1,128)S(1)} collective-permute-done((f32[1,2048]{1,0:T(1,128)S(1)}, f32[1,2048]{1,0:T(1,128)S(1)}, u32[]{:S(2)}, u32[]{:S(2)}) %collective-permute-start.16) | collective-permute-done | bytes 8224 | tf_op jit(solution)/shard_map/ppermute | solution.py:433
  87.7 2.0 collective-permute-start.17
  89.8 20.6 %collective-permute-done.17 = f32[1,2048]{1,0:T(1,128)S(1)} collective-permute-done((f32[1,2048]{1,0:T(1,128)S(1)}, f32[1,2048]{1,0:T(1,128)S(1)}, u32[]{:S(2)}, u32[]{:S(2)}) %collective-permute-start.17) | collective-permute-done | bytes 8224 | tf_op jit(solution)/shard_map/ppermute | solution.py:433
  110.3 4.7 %collective-permute-start.18 = (f32[1,2048]{1,0:T(1,128)S(1)}, f32[1,2048]{1,0:T(1,128)S(1)}, u32[]{:S(2)}, u32[]{:S(2)}) collective-permute-start(f32[1,2048]{1,0:T(1,128)S(1)} %add.150), channel_id=1, source_target_pairs={{0,2},{1,3},{2,0},{3,1},{4,6},{5,7},{6,4},{7,5},{8,10},{9,11},{10,... | collective-permute-start | bytes 24584 | tf_op jit(solution)/shard_map/ppermute | solution.py:433
  115.1 10.5 %collective-permute-done.18 = f32[1,2048]{1,0:T(1,128)S(1)} collective-permute-done((f32[1,2048]{1,0:T(1,128)S(1)}, f32[1,2048]{1,0:T(1,128)S(1)}, u32[]{:S(2)}, u32[]{:S(2)}) %collective-permute-start.18) | collective-permute-done | bytes 8224 | tf_op jit(solution)/shard_map/ppermute | solution.py:433
  125.6 1.9 copy.10
  127.6 5.3 %all-gather.7.cloned.1.call-done = bf16[32,128,512]{2,1,0:T(8,128)(2,1)} async-done(((bf16[4,128,512]{2,1,0:T(8,128)(2,1)}), bf16[32,128,512]{2,1,0:T(8,128)(2,1)}) %all-gather.7.cloned.1.call-update) | async-done | bytes 4194320 | tf_op jit(solution)/shard_map/all_gather | solution.py:461
  132.9 124.2 %shard_map.73 = (f32[2048,2048]{1,0:T(8,128)S(1)}, f32[2048,128]{1,0:T(8,128)S(1)}) custom-call(s32[1]{0:T(128)} %bitcast.feat, bf16[8,4,128,512]{3,2,1,0:T(8,128)(2,1)} %bitcast.43, bf16[8,4,128,512]{3,2,1,0:T(8,128)(2,1)} %bitcast.44), custom_call_target="tpu_custom_call" | custom-call | tf_op jit(solution)/shard_map/pallas_call | solution.py:241
  257.1 4.5 %shard_map.74 = (f32[1,2048]{1,0:T(1,128)S(1)}, f32[1,1]{1,0:T(1,128)}, f32[1,2048]{1,0:T(1,128)S(1)}) custom-call(f32[2048,2048]{1,0:T(8,128)S(1)} %get-tuple-element.36.lower, f32[2048,128]{1,0:T(8,128)S(1)} %get-tuple-element.37.inverses, bf16[512,2048]{1,0:T(8,128)(2,1)S(1)} %bitcast.38, f32[1,2048]{1,0:T(1,128)S(1)} %add_negate_fusion.residual), custom_call_target="tpu_custom_call" | custom-call | tf_op jit(solution)/shard_map/pallas_call | solution.py:372
  262.8 1.5 collective-permute-start.20
  264.3 2.2 collective-permute-done.20
  266.6 1.3 collective-permute-start.21
  267.9 2.4 collective-permute-done.21
  270.3 1.6 collective-permute-start.22
  271.8 2.2 collective-permute-done.22
  274.0 2.5 collective-permute-start.23
  276.5 2.1 collective-permute-done.23
  278.7 4.9 %shard_map.75 = (f32[1,2048]{1,0:T(1,128)S(1)}, f32[1,2048]{1,0:T(1,128)S(1)}, f32[1,2048]{1,0:T(1,128)S(1)}, f32[1,1]{1,0:T(1,128)}, f32[1,2048]{1,0:T(1,128)S(1)}) custom-call(f32[2048,2048]{1,0:T(8,128)S(1)} %get-tuple-element.36.lower, f32[2048,128]{1,0:T(8,128)S(1)} %get-tuple-element.37.inverses, bf16[512,2048]{1,0:T(8,128)(2,1)S(1)} %bitcast.39, ...), custom_call_target="tpu_custom_call" | custom-call | tf_op jit(solution)/shard_map/pallas_call | solution.py:372
  284.7 1.5 collective-permute-start.25
  286.2 2.2 collective-permute-done.25
  288.5 1.3 collective-permute-start.26
  289.8 2.4 collective-permute-done.26
  292.2 1.6 collective-permute-start.27
  293.7 2.2 collective-permute-done.27
  295.9 2.5 collective-permute-start.28
  298.4 2.1 collective-permute-done.28
  300.6 4.9 %shard_map.76 = (f32[1,2048]{1,0:T(1,128)S(1)}, f32[1,2048]{1,0:T(1,128)S(1)}, f32[1,2048]{1,0:T(1,128)S(1)}, f32[1,1]{1,0:T(1,128)}, f32[1,2048]{1,0:T(1,128)S(1)}) custom-call(f32[2048,2048]{1,0:T(8,128)S(1)} %get-tuple-element.36.lower, f32[2048,128]{1,0:T(8,128)S(1)} %get-tuple-element.37.inverses, bf16[512,2048]{1,0:T(8,128)(2,1)S(1)} %bitcast.40, ...), custom_call_target="tpu_custom_call" | custom-call | tf_op jit(solution)/shard_map/pallas_call | solution.py:372
  306.6 1.5 collective-permute-start.30
  308.1 2.2 collective-permute-done.30
  311.7 2.4 collective-permute-done.31
  314.1 1.6 collective-permute-start.32
  315.6 2.2 collective-permute-done.32
  317.8 2.5 collective-permute-start.33
  320.3 2.1 collective-permute-done.33
  322.5 5.0 %shard_map.77 = (f32[1,2048]{1,0:T(1,128)S(1)}, f32[1,2048]{1,0:T(1,128)}, f32[1,2048]{1,0:T(1,128)S(1)}, f32[1,1]{1,0:T(1,128)}, f32[1,2048]{1,0:T(1,128)S(1)}) custom-call(f32[2048,2048]{1,0:T(8,128)S(1)} %get-tuple-element.36.lower, f32[2048,128]{1,0:T(8,128)S(1)} %get-tuple-element.37.inverses, bf16[512,2048]{1,0:T(8,128)(2,1)S(1)} %bitcast.41, ...), custom_call_target="tpu_custom_call" | custom-call | tf_op jit(solution)/shard_map/pallas_call | solution.py:372
  328.7 1.5 collective-permute-start.35
  330.1 2.2 collective-permute-done.35
  333.7 2.4 collective-permute-done.36
  336.1 1.6 collective-permute-start.37
  337.7 2.2 collective-permute-done.37
  339.8 2.5 collective-permute-start.38
  343.0 1.5 collective-permute-done.38
  (90 shorter events, 20.4 us)
Async XLA Ops:
  6.5 9.6 %copy-start = (s32[2048]{0:T(1024)S(1)}, s32[2048]{0:T(1024)}, u32[]{:S(2)}) copy-start(s32[2048]{0:T(1024)} %param.11) | copy-start | bytes 24580
  6.5 121.1 %all-gather.5.cloned.1.call-start = ((), (), s32[]{:S(2)}) async-start(), calls=%async_computation.1 | async-start | bytes 4718592 | tf_op jit(solution)/shard_map/all_gather | solution.py:461
  9.9 7.6 %collective-permute-start = (f32[2048]{0:T(1024)S(1)}, f32[2048]{0:T(1024)S(1)}, u32[]{:S(2)}, u32[]{:S(2)}) collective-permute-start(f32[2048]{0:T(1024)S(1)} %bitcast.54), channel_id=1, source_target_pairs={{0,1},{1,0},{2,3},{3,2},{4,5},{5,4},{6,7},{7,6},{8,9},{9,8},{10,11... | collective-permute-start | bytes 24584 | tf_op jit(solution)/shard_map/ppermute | solution.py:386
  12.9 4.6 %collective-permute-start.1 = (f32[2048]{0:T(1024)S(1)}, f32[2048]{0:T(1024)S(1)}, u32[]{:S(2)}, u32[]{:S(2)}) collective-permute-start(f32[2048]{0:T(1024)S(1)} %bitcast.55), channel_id=1, source_target_pairs={{0,2},{1,3},{2,0},{3,1},{4,6},{5,7},{6,4},{7,5},{8,10},{9,11},{10,... | collective-permute-start | bytes 24584 | tf_op jit(solution)/shard_map/ppermute | solution.py:386
  15.5 5.4 %collective-permute-start.2 = (f32[2048]{0:T(1024)S(1)}, f32[2048]{0:T(1024)S(1)}, u32[]{:S(2)}, u32[]{:S(2)}) collective-permute-start(f32[2048]{0:T(1024)S(1)} %bitcast.56), channel_id=1, source_target_pairs={{0,3},{1,2},{2,1},{3,0},{4,7},{5,6},{6,5},{7,4},{8,11},{9,10},{10,... | collective-permute-start | bytes 24584 | tf_op jit(solution)/shard_map/ppermute | solution.py:386
  23.7 5.2 %copy-start.2 = (bf16[2048,512]{1,0:T(8,128)(2,1)}, bf16[2048,512]{1,0:T(8,128)(2,1)S(1)}, u32[]{:S(2)}) copy-start(bf16[2048,512]{1,0:T(8,128)(2,1)S(1)} %multiply_convert_fusion) | copy-start | bytes 6291460
  26.2 2.7 collective-permute-start.3
  31.4 8.4 %collective-permute-start.4 = (f16[256,512]{1,0:T(8,128)(2,1)S(1)}, f16[256,512]{1,0:T(8,128)(2,1)S(1)}, u32[]{:S(2)}, u32[]{:S(2)}) collective-permute-start(f16[256,512]{1,0:T(8,128)(2,1)S(1)} %get-tuple-element.60), channel_id=1, source_target_pairs={{0,8},{4,12},{8,0},{12,4},{16,24},{20,28},{24,16},{28,20},{1,9},{5... | collective-permute-start | bytes 786440 | tf_op jit(solution)/shard_map/ppermute | solution.py:392
  33.0 8.1 %collective-permute-start.5 = (f16[256,512]{1,0:T(8,128)(2,1)S(1)}, f16[256,512]{1,0:T(8,128)(2,1)S(1)}, u32[]{:S(2)}, u32[]{:S(2)}) collective-permute-start(f16[256,512]{1,0:T(8,128)(2,1)S(1)} %get-tuple-element.59), channel_id=1, source_target_pairs={{0,16},{4,20},{8,24},{12,28},{16,0},{20,4},{24,8},{28,12},{1,17},{... | collective-permute-start | bytes 786440 | tf_op jit(solution)/shard_map/ppermute | solution.py:392
  41.3 5.0 %collective-permute-start.6 = (f16[128,512]{1,0:T(8,128)(2,1)S(1)}, f16[128,512]{1,0:T(8,128)(2,1)S(1)}, u32[]{:S(2)}, u32[]{:S(2)}) collective-permute-start(f16[128,512]{1,0:T(8,128)(2,1)S(1)} %slice_convert_fusion.1), channel_id=1, source_target_pairs={{0,16},{4,20},{8,24},{12,28},{16,0},{20,4},{24,8},{28,12},{1,17},{... | collective-permute-start | bytes 393224 | tf_op jit(solution)/shard_map/ppermute | solution.py:392
  42.9 34.6 %copy-start.1 = (bf16[2048,512]{1,0:T(8,128)(2,1)S(1)}, bf16[2048,512]{1,0:T(8,128)(2,1)}, u32[]{:S(2)}) copy-start(bf16[2048,512]{1,0:T(8,128)(2,1)} %param.7) | copy-start | bytes 6291460
  42.9 5.0 %collective-permute-start.7 = (f16[128,512]{1,0:T(8,128)(2,1)S(1)}, f16[128,512]{1,0:T(8,128)(2,1)S(1)}, u32[]{:S(2)}, u32[]{:S(2)}) collective-permute-start(f16[128,512]{1,0:T(8,128)(2,1)S(1)} %slice_convert_fusion), channel_id=1, source_target_pairs={{0,8},{4,12},{8,0},{12,4},{16,24},{20,28},{24,16},{28,20},{1,9},{5... | collective-permute-start | bytes 393224 | tf_op jit(solution)/shard_map/ppermute | solution.py:392
  48.0 8.1 %collective-permute-start.10 = (bf16[128,512]{1,0:T(8,128)(2,1)S(1)}, bf16[128,512]{1,0:T(8,128)(2,1)S(1)}, u32[]{:S(2)}, u32[]{:S(2)}) collective-permute-start(bf16[128,512]{1,0:T(8,128)(2,1)S(1)} %fusion.22), channel_id=1, source_target_pairs={{0,3},{1,2},{2,1},{3,0},{4,7},{5,6},{6,5},{7,4},{8,11},{9,10},{10,... | collective-permute-start | bytes 393224 | tf_op jit(solution)/shard_map/ppermute | solution.py:386
  48.4 7.6 %collective-permute-start.8 = (bf16[128,512]{1,0:T(8,128)(2,1)S(1)}, bf16[128,512]{1,0:T(8,128)(2,1)S(1)}, u32[]{:S(2)}, u32[]{:S(2)}) collective-permute-start(bf16[128,512]{1,0:T(8,128)(2,1)S(1)} %fusion.22), channel_id=1, source_target_pairs={{0,1},{1,0},{2,3},{3,2},{4,5},{5,4},{6,7},{7,6},{8,9},{9,8},{10,11... | collective-permute-start | bytes 393224 | tf_op jit(solution)/shard_map/ppermute | solution.py:386
  48.4 11.1 %collective-permute-start.9 = (bf16[128,512]{1,0:T(8,128)(2,1)S(1)}, bf16[128,512]{1,0:T(8,128)(2,1)S(1)}, u32[]{:S(2)}, u32[]{:S(2)}) collective-permute-start(bf16[128,512]{1,0:T(8,128)(2,1)S(1)} %fusion.22), channel_id=1, source_target_pairs={{0,2},{1,3},{2,0},{3,1},{4,6},{5,7},{6,4},{7,5},{8,10},{9,11},{10,... | collective-permute-start | bytes 393224 | tf_op jit(solution)/shard_map/ppermute | solution.py:386
  60.4 18.0 %copy-start.3 = (f32[512]{0:T(512)S(1)}, f32[512]{0:T(512)}, u32[]{:S(2)}) copy-start(f32[512]{0:T(512)} %param.8) | copy-start | bytes 6148
  60.4 72.5 %all-gather.7.cloned.1.call-start = ((), (), s32[]{:S(2)}) async-start(), calls=%async_computation.2 | async-start | bytes 4718592 | tf_op jit(solution)/shard_map/all_gather | solution.py:461
  60.5 5.1 %collective-permute-start.11 = (bf16[128,512]{1,0:T(8,128)(2,1)S(1)}, bf16[128,512]{1,0:T(8,128)(2,1)S(1)}, u32[]{:S(2)}, u32[]{:S(2)}) collective-permute-start(bf16[128,512]{1,0:T(8,128)(2,1)S(1)} %fusion.20), channel_id=1, source_target_pairs={{0,1},{1,0},{2,3},{3,2},{4,5},{5,4},{6,7},{7,6},{8,9},{9,8},{10,11... | collective-permute-start | bytes 393224 | tf_op jit(solution)/shard_map/ppermute | solution.py:386
  60.5 11.6 %collective-permute-start.12 = (bf16[128,512]{1,0:T(8,128)(2,1)S(1)}, bf16[128,512]{1,0:T(8,128)(2,1)S(1)}, u32[]{:S(2)}, u32[]{:S(2)}) collective-permute-start(bf16[128,512]{1,0:T(8,128)(2,1)S(1)} %fusion.20), channel_id=1, source_target_pairs={{0,2},{1,3},{2,0},{3,1},{4,6},{5,7},{6,4},{7,5},{8,10},{9,11},{10,... | collective-permute-start | bytes 393224 | tf_op jit(solution)/shard_map/ppermute | solution.py:386
  62.1 10.1 %collective-permute-start.13 = (bf16[128,512]{1,0:T(8,128)(2,1)S(1)}, bf16[128,512]{1,0:T(8,128)(2,1)S(1)}, u32[]{:S(2)}, u32[]{:S(2)}) collective-permute-start(bf16[128,512]{1,0:T(8,128)(2,1)S(1)} %fusion.20), channel_id=1, source_target_pairs={{0,3},{1,2},{2,1},{3,0},{4,7},{5,6},{6,5},{7,4},{8,11},{9,10},{10,... | collective-permute-start | bytes 393224 | tf_op jit(solution)/shard_map/ppermute | solution.py:386
  73.0 52.6 %all-to-all-start = ((bf16[4,512,512]{2,1,0:T(8,128)(2,1)}), bf16[4,512,512]{2,1,0:T(8,128)(2,1)}, u32[]{:S(2)}, u32[]{:S(2)}) async-start(bf16[4,512,512]{2,1,0:T(8,128)(2,1)} %bitcast.42), calls=%async_computation | async-start | bytes 4194304 | tf_op jit(solution)/shard_map/all_to_all | solution.py:471
  78.7 1.2 collective-permute-start.14
  80.0 3.9 %collective-permute-start.15 = (f32[1,2048]{1,0:T(1,128)S(1)}, f32[1,2048]{1,0:T(1,128)S(1)}, u32[]{:S(2)}, u32[]{:S(2)}) collective-permute-start(f32[1,2048]{1,0:T(1,128)S(1)} %add.147), channel_id=1, source_target_pairs={{0,8},{4,12},{8,0},{12,4},{16,24},{20,28},{24,16},{28,20},{1,9},{5... | collective-permute-start | bytes 24584 | tf_op jit(solution)/shard_map/ppermute | solution.py:433
  83.9 3.9 %collective-permute-start.16 = (f32[1,2048]{1,0:T(1,128)S(1)}, f32[1,2048]{1,0:T(1,128)S(1)}, u32[]{:S(2)}, u32[]{:S(2)}) collective-permute-start(f32[1,2048]{1,0:T(1,128)S(1)} %add.148), channel_id=1, source_target_pairs={{0,16},{4,20},{8,24},{12,28},{16,0},{20,4},{24,8},{28,12},{1,17},{... | collective-permute-start | bytes 24584 | tf_op jit(solution)/shard_map/ppermute | solution.py:433
  87.7 22.6 %collective-permute-start.17 = (f32[1,2048]{1,0:T(1,128)S(1)}, f32[1,2048]{1,0:T(1,128)S(1)}, u32[]{:S(2)}, u32[]{:S(2)}) collective-permute-start(f32[1,2048]{1,0:T(1,128)S(1)} %add.149), channel_id=1, source_target_pairs={{0,1},{1,0},{2,3},{3,2},{4,5},{5,4},{6,7},{7,6},{8,9},{9,8},{10,11... | collective-permute-start | bytes 24584 | tf_op jit(solution)/shard_map/ppermute | solution.py:433
  110.3 15.3 %collective-permute-start.18 = (f32[1,2048]{1,0:T(1,128)S(1)}, f32[1,2048]{1,0:T(1,128)S(1)}, u32[]{:S(2)}, u32[]{:S(2)}) collective-permute-start(f32[1,2048]{1,0:T(1,128)S(1)} %add.150), channel_id=1, source_target_pairs={{0,2},{1,3},{2,0},{3,1},{4,6},{5,7},{6,4},{7,5},{8,10},{9,11},{10,... | collective-permute-start | bytes 24584 | tf_op jit(solution)/shard_map/ppermute | solution.py:433
  261.6 1.2 collective-permute-start.19
  262.8 3.7 %collective-permute-start.20 = (f32[1,2048]{1,0:T(1,128)S(1)}, f32[1,2048]{1,0:T(1,128)S(1)}, u32[]{:S(2)}, u32[]{:S(2)}) collective-permute-start(f32[1,2048]{1,0:T(1,128)S(1)} %add.152), channel_id=1, source_target_pairs={{0,8},{4,12},{8,0},{12,4},{16,24},{20,28},{24,16},{28,20},{1,9},{5... | collective-permute-start | bytes 24584 | tf_op jit(solution)/shard_map/ppermute | solution.py:433
  266.6 3.7 %collective-permute-start.21 = (f32[1,2048]{1,0:T(1,128)S(1)}, f32[1,2048]{1,0:T(1,128)S(1)}, u32[]{:S(2)}, u32[]{:S(2)}) collective-permute-start(f32[1,2048]{1,0:T(1,128)S(1)} %add.153), channel_id=1, source_target_pairs={{0,16},{4,20},{8,24},{12,28},{16,0},{20,4},{24,8},{28,12},{1,17},{... | collective-permute-start | bytes 24584 | tf_op jit(solution)/shard_map/ppermute | solution.py:433
  270.3 3.7 %collective-permute-start.22 = (f32[1,2048]{1,0:T(1,128)S(1)}, f32[1,2048]{1,0:T(1,128)S(1)}, u32[]{:S(2)}, u32[]{:S(2)}) collective-permute-start(f32[1,2048]{1,0:T(1,128)S(1)} %add.154), channel_id=1, source_target_pairs={{0,1},{1,0},{2,3},{3,2},{4,5},{5,4},{6,7},{7,6},{8,9},{9,8},{10,11... | collective-permute-start | bytes 24584 | tf_op jit(solution)/shard_map/ppermute | solution.py:433
  274.0 4.6 %collective-permute-start.23 = (f32[1,2048]{1,0:T(1,128)S(1)}, f32[1,2048]{1,0:T(1,128)S(1)}, u32[]{:S(2)}, u32[]{:S(2)}) collective-permute-start(f32[1,2048]{1,0:T(1,128)S(1)} %add.155), channel_id=1, source_target_pairs={{0,2},{1,3},{2,0},{3,1},{4,6},{5,7},{6,4},{7,5},{8,10},{9,11},{10,... | collective-permute-start | bytes 24584 | tf_op jit(solution)/shard_map/ppermute | solution.py:433
  283.6 1.2 collective-permute-start.24
  284.7 3.7 %collective-permute-start.25 = (f32[1,2048]{1,0:T(1,128)S(1)}, f32[1,2048]{1,0:T(1,128)S(1)}, u32[]{:S(2)}, u32[]{:S(2)}) collective-permute-start(f32[1,2048]{1,0:T(1,128)S(1)} %add.157), channel_id=1, source_target_pairs={{0,8},{4,12},{8,0},{12,4},{16,24},{20,28},{24,16},{28,20},{1,9},{5... | collective-permute-start | bytes 24584 | tf_op jit(solution)/shard_map/ppermute | solution.py:433
  288.5 3.7 %collective-permute-start.26 = (f32[1,2048]{1,0:T(1,128)S(1)}, f32[1,2048]{1,0:T(1,128)S(1)}, u32[]{:S(2)}, u32[]{:S(2)}) collective-permute-start(f32[1,2048]{1,0:T(1,128)S(1)} %add.158), channel_id=1, source_target_pairs={{0,16},{4,20},{8,24},{12,28},{16,0},{20,4},{24,8},{28,12},{1,17},{... | collective-permute-start | bytes 24584 | tf_op jit(solution)/shard_map/ppermute | solution.py:433
  292.2 3.7 %collective-permute-start.27 = (f32[1,2048]{1,0:T(1,128)S(1)}, f32[1,2048]{1,0:T(1,128)S(1)}, u32[]{:S(2)}, u32[]{:S(2)}) collective-permute-start(f32[1,2048]{1,0:T(1,128)S(1)} %add.159), channel_id=1, source_target_pairs={{0,1},{1,0},{2,3},{3,2},{4,5},{5,4},{6,7},{7,6},{8,9},{9,8},{10,11... | collective-permute-start | bytes 24584 | tf_op jit(solution)/shard_map/ppermute | solution.py:433
  295.9 4.6 %collective-permute-start.28 = (f32[1,2048]{1,0:T(1,128)S(1)}, f32[1,2048]{1,0:T(1,128)S(1)}, u32[]{:S(2)}, u32[]{:S(2)}) collective-permute-start(f32[1,2048]{1,0:T(1,128)S(1)} %add.160), channel_id=1, source_target_pairs={{0,2},{1,3},{2,0},{3,1},{4,6},{5,7},{6,4},{7,5},{8,10},{9,11},{10,... | collective-permute-start | bytes 24584 | tf_op jit(solution)/shard_map/ppermute | solution.py:433
  305.4 1.2 collective-permute-start.29
  306.6 3.7 %collective-permute-start.30 = (f32[1,2048]{1,0:T(1,128)S(1)}, f32[1,2048]{1,0:T(1,128)S(1)}, u32[]{:S(2)}, u32[]{:S(2)}) collective-permute-start(f32[1,2048]{1,0:T(1,128)S(1)} %add.162), channel_id=1, source_target_pairs={{0,8},{4,12},{8,0},{12,4},{16,24},{20,28},{24,16},{28,20},{1,9},{5... | collective-permute-start | bytes 24584 | tf_op jit(solution)/shard_map/ppermute | solution.py:433
  310.4 3.7 %collective-permute-start.31 = (f32[1,2048]{1,0:T(1,128)S(1)}, f32[1,2048]{1,0:T(1,128)S(1)}, u32[]{:S(2)}, u32[]{:S(2)}) collective-permute-start(f32[1,2048]{1,0:T(1,128)S(1)} %add.163), channel_id=1, source_target_pairs={{0,16},{4,20},{8,24},{12,28},{16,0},{20,4},{24,8},{28,12},{1,17},{... | collective-permute-start | bytes 24584 | tf_op jit(solution)/shard_map/ppermute | solution.py:433
  314.1 3.7 %collective-permute-start.32 = (f32[1,2048]{1,0:T(1,128)S(1)}, f32[1,2048]{1,0:T(1,128)S(1)}, u32[]{:S(2)}, u32[]{:S(2)}) collective-permute-start(f32[1,2048]{1,0:T(1,128)S(1)} %add.164), channel_id=1, source_target_pairs={{0,1},{1,0},{2,3},{3,2},{4,5},{5,4},{6,7},{7,6},{8,9},{9,8},{10,11... | collective-permute-start | bytes 24584 | tf_op jit(solution)/shard_map/ppermute | solution.py:433
  317.8 4.6 %collective-permute-start.33 = (f32[1,2048]{1,0:T(1,128)S(1)}, f32[1,2048]{1,0:T(1,128)S(1)}, u32[]{:S(2)}, u32[]{:S(2)}) collective-permute-start(f32[1,2048]{1,0:T(1,128)S(1)} %add.165), channel_id=1, source_target_pairs={{0,2},{1,3},{2,0},{3,1},{4,6},{5,7},{6,4},{7,5},{8,10},{9,11},{10,... | collective-permute-start | bytes 24584 | tf_op jit(solution)/shard_map/ppermute | solution.py:433
  327.5 1.2 collective-permute-start.34
  328.7 3.7 %collective-permute-start.35 = (f32[1,2048]{1,0:T(1,128)S(1)}, f32[1,2048]{1,0:T(1,128)S(1)}, u32[]{:S(2)}, u32[]{:S(2)}) collective-permute-start(f32[1,2048]{1,0:T(1,128)S(1)} %add.167), channel_id=1, source_target_pairs={{0,8},{4,12},{8,0},{12,4},{16,24},{20,28},{24,16},{28,20},{1,9},{5... | collective-permute-start | bytes 24584 | tf_op jit(solution)/shard_map/ppermute | solution.py:433
  332.4 3.7 %collective-permute-start.36 = (f32[1,2048]{1,0:T(1,128)S(1)}, f32[1,2048]{1,0:T(1,128)S(1)}, u32[]{:S(2)}, u32[]{:S(2)}) collective-permute-start(f32[1,2048]{1,0:T(1,128)S(1)} %add.168), channel_id=1, source_target_pairs={{0,16},{4,20},{8,24},{12,28},{16,0},{20,4},{24,8},{28,12},{1,17},{... | collective-permute-start | bytes 24584 | tf_op jit(solution)/shard_map/ppermute | solution.py:433
  336.1 3.7 %collective-permute-start.37 = (f32[1,2048]{1,0:T(1,128)S(1)}, f32[1,2048]{1,0:T(1,128)S(1)}, u32[]{:S(2)}, u32[]{:S(2)}) collective-permute-start(f32[1,2048]{1,0:T(1,128)S(1)} %add.169), channel_id=1, source_target_pairs={{0,1},{1,0},{2,3},{3,2},{4,5},{5,4},{6,7},{7,6},{8,9},{9,8},{10,11... | collective-permute-start | bytes 24584 | tf_op jit(solution)/shard_map/ppermute | solution.py:433
  339.8 4.6 %collective-permute-start.38 = (f32[1,2048]{1,0:T(1,128)S(1)}, f32[1,2048]{1,0:T(1,128)S(1)}, u32[]{:S(2)}, u32[]{:S(2)}) collective-permute-start(f32[1,2048]{1,0:T(1,128)S(1)} %add.170), channel_id=1, source_target_pairs={{0,2},{1,3},{2,0},{3,1},{4,6},{5,7},{6,4},{7,5},{8,10},{9,11},{10,... | collective-permute-start | bytes 24584 | tf_op jit(solution)/shard_map/ppermute | solution.py:433
Sparse Core Ops, SparseCore 0:
  60.5 33.6 all-gather.4
  96.1 36.7 all-gather.6

commit v2 on v1

--- a/solution.py
+++ b/solution.py
@@ -23,14 +23,9 @@
     return high, low
 
 
-def reciprocal(value):
-    guess = pl.reciprocal(value, approx=True)
-    guess = guess * (2.0 - value * guess)
-    return guess * (2.0 - value * guess)
-
-
 def invert_block(block, pieces=()):
     tiles = BLOCK // PIVOTS
+    slots = BLOCK // 2
     lane = lax.broadcasted_iota(jnp.int32, (PIVOTS, BLOCK), 1)
     sub = lax.broadcasted_iota(jnp.int32, (PIVOTS, BLOCK), 0)
     shape = (PIVOTS, BLOCK)
@@ -62,7 +57,10 @@
         pairs = []
         for j in range(0, PIVOTS, 2):
             a, b, d = cell[j, j], cell[j + 1, j], cell[j + 1, j + 1]
-            inverse = reciprocal(a * d - b * b)
+            inverse = 1.0 / (a * d - b * b)
+            slot = (step * PIVOTS + j) // 2
+            for piece in pieces[slot * len(pieces) // slots : (slot + 1) * len(pieces) // slots]:
+                piece()
             pairs.append((a * inverse, b * inverse, d * inverse))
             for i in range(j + 2, PIVOTS):
                 one, two = cell[i, j], cell[i, j + 1]
@@ -103,8 +101,6 @@
         for j in range(1, PIVOTS):
             rows = jnp.where(sub == j, line[j], rows)
         scaled_rows.append(jnp.where(before, rows, 0.0))
-        for piece in pieces[step * len(pieces) // tiles : (step + 1) * len(pieces) // tiles]:
-            piece()
     high, low = split(jnp.concatenate(plain, axis=0))
     left = jnp.concatenate([high, low, high, low], axis=0)
     high, low = split(jnp.concatenate(scaled_rows, axis=0))
@@ -114,27 +110,24 @@
     )
 
 
-def factor_kernel(feat, upper, lower, work, inv_ref, sketch, right, wide, left, sem):
+def factor_kernel(feat, pieces, work, inv_ref, sketch, right, wide, left, sem):
     size = work.shape[0]
     blocks = size // BLOCK
-    feat_count = upper.shape[1]
+    feat_count = pieces.shape[1]
     width = size // feat_count
     copies = []
-    for group, pieces in enumerate((upper, lower)):
-        for mask in range(feat_count):
-            start = pl.multiple_of((feat[0] ^ mask) * width, width)
-            copies.append(
-                pltpu.make_async_copy(
-                    pieces.at[:, mask],
-                    sketch.at[group, :, :, pl.ds(start, width)],
-                    sem.at[group, mask],
-                )
+    for mask in range(feat_count):
+        start = pl.multiple_of((feat[0] ^ mask) * width, width)
+        copies.append(
+            pltpu.make_async_copy(
+                pieces.at[:, mask], sketch.at[:, :, pl.ds(start, width)], sem.at[mask]
             )
+        )
     for copy in copies:
         copy.start()
     for copy in copies:
         copy.wait()
-    samples = sketch.shape[0] * sketch.shape[1] * sketch.shape[2]
+    samples = sketch.shape[0] * sketch.shape[1]
     chunks = size // CHUNK
 
     def chunk(c):
@@ -148,8 +141,8 @@
             @pl.when(c >= m)
             def _():
                 product = lax.dot_general(
-                    sketch[:, :, :, here].reshape(samples, CHUNK),
-                    sketch[:, :, :, chunk(c)].reshape(samples, CHUNK),
+                    sketch[:, :, here].reshape(samples, CHUNK),
+                    sketch[:, :, chunk(c)].reshape(samples, CHUNK),
                     (((0,), (0,)), ((), ())),
                     preferred_element_type=jnp.float32,
                 )
@@ -235,14 +228,13 @@
 VMEM = pl.BlockSpec(memory_space=pltpu.VMEM)
 
 
-def factor(feat, upper, lower, interpret=False):
-    ex_count, feat_count, rows, width = upper.shape
+def factor(feat, pieces, interpret=False):
+    ex_count, feat_count, rows, width = pieces.shape
     size = feat_count * width
     return pl.pallas_call(
         factor_kernel,
         in_specs=[
             pl.BlockSpec(memory_space=pltpu.SMEM),
-            pl.BlockSpec(memory_space=pl.ANY),
             pl.BlockSpec(memory_space=pl.ANY),
         ],
         out_specs=[VMEM, VMEM],
@@ -251,15 +243,15 @@
             pltpu.VMEM((size, BLOCK), jnp.float32),
         ],
         scratch_shapes=[
-            pltpu.VMEM((2, ex_count, rows, size), jnp.bfloat16),
+            pltpu.VMEM((ex_count, rows, size), jnp.bfloat16),
             pltpu.VMEM((4 * BLOCK, size), jnp.bfloat16),
             pltpu.VMEM((size, 4 * BLOCK), jnp.bfloat16),
             pltpu.VMEM((size, 4 * BLOCK), jnp.bfloat16),
-            pltpu.SemaphoreType.DMA((2, feat_count)),
+            pltpu.SemaphoreType.DMA((feat_count,)),
         ],
         compiler_params=pltpu.CompilerParams(vmem_limit_bytes=36 * 2**20),
         interpret=interpret,
-    )(feat, upper, lower)
+    )(feat, pieces)
 
 
 def apply_inverse(lower, inverses, residual, column):
@@ -425,13 +417,11 @@
     return parts
 
 
-def butterfly(value):
-    for axis in ("ex", "feat"):
+def butterfly(value, axes=("ex", "feat")):
+    for axis in axes:
         count = lax.axis_size(axis)
-        mask = 1
-        while mask < count:
-            value = value + lax.ppermute(value, axis, [(s, s ^ mask) for s in range(count)])
-            mask = mask * 2
+        for bit in range(count.bit_length() - 1):
+            value = value + swap(value, axis, bit)
     return value
 
 
@@ -445,21 +435,17 @@
     total_rows = row_count * ex_count
     sample_count = samples.shape[0]
     dense = features.astype(jnp.float32)
-    margins = sum(exchange(jnp.dot(dense, weights, precision=highest), "feat"))
+    margins = butterfly(jnp.dot(dense, weights, precision=highest), ("feat",))
     probability = 1.0 / (1.0 + jnp.exp(-margins))
     curvature = probability * (1.0 - probability)
     weighted = (jnp.sqrt(curvature)[:, None] * dense).astype(jnp.bfloat16)
     signed = weighted * signs.astype(jnp.bfloat16)[:, None]
     places = ex_index * row_count + lax.iota(jnp.int32, row_count)
     scale = 1.0 / math.sqrt(total_rows * sample_count)
-    upper, lower = [
-        (part * scale).astype(jnp.bfloat16) for part in sampled_mix(samples, places, signed)
-    ]
-    upper = jnp.stack(exchange(upper, "feat"))
-    upper, lower = lax.optimization_barrier((upper, lower))
-    lower = jnp.stack(exchange(lower, "feat"))
-    upper, lower = [lax.all_gather(value, "ex", axis=0) for value in (upper, lower)]
-    lower, inverses = factor(feat_index.astype(jnp.int32)[None], upper, lower)
+    sketch = (jnp.concatenate(sampled_mix(samples, places, signed)) * scale).astype(jnp.bfloat16)
+    wide_sketch = jnp.stack(exchange(sketch, "feat"))
+    pieces = lax.all_gather(wide_sketch, "ex", axis=0)
+    lower, inverses = factor(feat_index.astype(jnp.int32)[None], pieces)
 
     grad_part = jnp.dot(probability - labels.astype(jnp.float32), dense, precision=highest)
     own_weights = jnp.where(ex_index == 0, REG / D, 0.0) * weights

time: 360 us -> 351 us (0.975)
  starting transfers between devices: 59.4 us -> 36.4 us
  waiting for transfers between devices: 115 us -> 135 us
  other arithmetic: 7.07 us -> 2.86 us
    ppermute x5 -> x32, waiting for transfers between devices: 13.6 us -> 119 us  [swap(): lax.ppermute(value, axis, [(s, s ^ mask) for s in range(lax.axis_size(axi...]
    ppermute x25 -> x0, waiting for transfers between devices: 78.8 us -> none  [butterfly(): lax.ppermute(value, axis, [(s, s ^ mask) for s in range(count)])]
    ppermute x25 -> x0, starting transfers between devices: 35.1 us -> none  [butterfly(): lax.ppermute(value, axis, [(s, s ^ mask) for s in range(count)])]
    ppermute x5 -> x32, starting transfers between devices: 5.33 us -> 24 us  [swap(): lax.ppermute(value, axis, [(s, s ^ mask) for s in range(lax.axis_size(axi...]
    ppermute x9 -> x3, starting transfers between devices: 14.5 us -> 4.23 us  [exchange(): lax.ppermute(value, axis, [(s, s ^ mask) for s in range(count)])]
    all_gather x2 -> x1, waiting for transfers between devices: 5.29 us -> 0.02 us  [local(): pieces = lax.all_gather(wide_sketch, 'ex', axis=0)]
    all_to_all x1, starting transfers between devices: 4.45 us -> 8.11 us  [local(): lax.all_to_all(weighted, 'feat', split_axis=0, concat_axis=1, tiled=True)]
    ppermute x9 -> x3, waiting for transfers between devices: 17.7 us -> 15.4 us  [exchange(): lax.ppermute(value, axis, [(s, s ^ mask) for s in range(count)])]
  transfers between devices with their start and end apart: 42 -> 37, of which waited for: 36 -> 34; matrix products, arithmetic and copies ran while one was open for 2% -> 1% of each run, Pallas kernels for 0% -> 0%
where the time goes in v2:
time: 351 us; the launch traced here: 344 us
  Pallas kernels  144 us (41%)
  waiting for transfers between devices  135 us (38%)
  starting transfers between devices  36.4 us (10%)
  between operations  14.6 us (4%)
  matrix products  9.22 us (3%)
    pallas_call x1, Pallas kernels, factor(): pl.pallas_call(factor_kernel, in_specs=[pl.BlockSpec(memory_space=pltpu.S...  123 us
    ppermute x32, waiting for transfers between devices, swap(): lax.ppermute(value, axis, [(s, s ^ mask) for s in range(lax.axis_size(axi...  119 us
    ppermute x32, starting transfers between devices, swap(): lax.ppermute(value, axis, [(s, s ^ mask) for s in range(lax.axis_size(axi...  24 us
    pallas_call x5, Pallas kernels, call(): pl.pallas_call(kernel, in_specs=[VMEM] * len(args), out_specs=[VMEM] * le...  20.7 us
    ppermute x3, waiting for transfers between devices, exchange(): lax.ppermute(value, axis, [(s, s ^ mask) for s in range(count)])  15.4 us
    all_to_all x1, starting transfers between devices, local(): lax.all_to_all(weighted, 'feat', split_axis=0, concat_axis=1, tiled=True)  8.11 us
  transfers between devices with their start and end apart: 37, of which 34 were waited for; matrix products, arithmetic and copies ran while one was open for 1% of the time, Pallas kernels for 0%

profile of v2, /device:TPU:0, one launch (start us, length us, event | category | flops | bytes accessed | tf_op | source)
XLA Modules:
  0.0 344.2 jit_solution(12773953347726672111)
XLA Ops:
  6.6 3.5 %fusion.29 = f32[1,2048]{1,0:T(1,128)S(1)} fusion(bf16[2048,512]{1,0:T(8,128)(2,1)} %param.7, f32[512,1]{0,1:T(1,128)} %bitcast.51), kind=kOutput, calls=%fused_computation.50 | convolution fusion | flops 12582912 | bytes 2107392 | tf_op jit(solution)/shard_map/dot_general | solution.py:438
  10.1 3.0 collective-permute-start
  13.1 0.6 gather_fusion
  13.7 1.0 collective-permute-done
  14.7 3.0 collective-permute-start.1
  17.8 1.6 collective-permute-done.1
  19.4 0.5 multiply_convert_fusion
  19.9 2.4 fusion.14
  22.4 2.6 collective-permute-done.2
  25.1 2.4 fusion.28
  27.6 1.9 collective-permute-start.3
  29.5 1.5 collective-permute-start.4
  31.0 5.1 %collective-permute-done.3 = f16[256,512]{1,0:T(8,128)(2,1)S(1)} collective-permute-done((f16[256,512]{1,0:T(8,128)(2,1)S(1)}, f16[256,512]{1,0:T(8,128)(2,1)S(1)}, u32[]{:S(2)}, u32[]{:S(2)}) %collective-permute-start.3) | collective-permute-done | bytes 262176 | tf_op jit(solution)/shard_map/ppermute | solution.py:384
  36.1 1.5 collective-permute-done.4
  37.8 1.6 collective-permute-start.5
  39.4 0.6 collective-permute-start.6
  40.0 2.8 collective-permute-done.5
  42.8 1.6 collective-permute-done.6
  44.6 2.6 collective-permute-start.8
  47.2 1.3 collective-permute-start.9
  48.8 15.1 %collective-permute-done.8 = bf16[256,512]{1,0:T(8,128)(2,1)S(1)} collective-permute-done((bf16[256,512]{1,0:T(8,128)(2,1)S(1)}, bf16[256,512]{1,0:T(8,128)(2,1)S(1)}, u32[]{:S(2)}, u32[]{:S(2)}) %collective-permute-start.8) | collective-permute-done | bytes 262176 | tf_op jit(solution)/shard_map/ppermute | solution.py:378
  64.2 1.1 pad_maximum_fusion
  65.4 8.1 %all-to-all-start = ((bf16[4,512,512]{2,1,0:T(8,128)(2,1)}), bf16[4,512,512]{2,1,0:T(8,128)(2,1)}, u32[]{:S(2)}, u32[]{:S(2)}) async-start(bf16[4,512,512]{2,1,0:T(8,128)(2,1)} %bitcast.39), calls=%async_computation | async-start | bytes 4194304 | tf_op jit(solution)/shard_map/all_to_all | solution.py:457
  73.5 0.9 fusion.30
  74.8 1.2 collective-permute-done.10
  75.9 0.6 collective-permute-start.11
  76.6 3.1 collective-permute-done.11
  79.9 3.6 %collective-permute-done.12 = f32[1,2048]{1,0:T(1,128)S(1)} collective-permute-done((f32[1,2048]{1,0:T(1,128)S(1)}, f32[1,2048]{1,0:T(1,128)S(1)}, u32[]{:S(2)}, u32[]{:S(2)}) %collective-permute-start.12) | collective-permute-done | bytes 8224 | tf_op jit(solution)/shard_map/ppermute | solution.py:384
  83.5 2.1 collective-permute-start.13
  85.6 22.1 %collective-permute-done.13 = f32[1,2048]{1,0:T(1,128)S(1)} collective-permute-done((f32[1,2048]{1,0:T(1,128)S(1)}, f32[1,2048]{1,0:T(1,128)S(1)}, u32[]{:S(2)}, u32[]{:S(2)}) %collective-permute-start.13) | collective-permute-done | bytes 8224 | tf_op jit(solution)/shard_map/ppermute | solution.py:384
  107.7 4.7 %collective-permute-start.14 = (f32[1,2048]{1,0:T(1,128)S(1)}, f32[1,2048]{1,0:T(1,128)S(1)}, u32[]{:S(2)}, u32[]{:S(2)}) collective-permute-start(f32[1,2048]{1,0:T(1,128)S(1)} %add.146), channel_id=1, source_target_pairs={{0,2},{1,3},{2,0},{3,1},{4,6},{5,7},{6,4},{7,5},{8,10},{9,11},{10,... | collective-permute-start | bytes 24584 | tf_op jit(solution)/shard_map/ppermute | solution.py:384
  112.4 10.6 %collective-permute-done.14 = f32[1,2048]{1,0:T(1,128)S(1)} collective-permute-done((f32[1,2048]{1,0:T(1,128)S(1)}, f32[1,2048]{1,0:T(1,128)S(1)}, u32[]{:S(2)}, u32[]{:S(2)}) %collective-permute-start.14) | collective-permute-done | bytes 8224 | tf_op jit(solution)/shard_map/ppermute | solution.py:384
  123.0 1.9 copy.10
  124.9 122.9 %shard_map.73 = (f32[2048,2048]{1,0:T(8,128)S(1)}, f32[2048,128]{1,0:T(8,128)S(1)}) custom-call(s32[1]{0:T(128)} %bitcast.feat, bf16[8,4,256,512]{3,2,1,0:T(8,128)(2,1)} %bitcast.38), custom_call_target="tpu_custom_call" | custom-call | tf_op jit(solution)/shard_map/pallas_call | solution.py:234
  247.8 4.6 %shard_map.74 = (f32[1,2048]{1,0:T(1,128)S(1)}, f32[1,1]{1,0:T(1,128)}, f32[1,2048]{1,0:T(1,128)S(1)}) custom-call(f32[2048,2048]{1,0:T(8,128)S(1)} %get-tuple-element.32.lower, f32[2048,128]{1,0:T(8,128)S(1)} %get-tuple-element.33.inverses, bf16[512,2048]{1,0:T(8,128)(2,1)S(1)} %bitcast.34, f32[1,2048]{1,0:T(1,128)S(1)} %add_negate_fusion.residual), custom_call_target="tpu_custom_call" | custom-call | tf_op jit(solution)/shard_map/pallas_call | solution.py:364
  252.4 1.2 collective-permute-done.15
  253.6 0.7 collective-permute-start.16
  254.2 3.0 collective-permute-done.16
  257.6 3.5 %collective-permute-done.17 = f32[1,2048]{1,0:T(1,128)S(1)} collective-permute-done((f32[1,2048]{1,0:T(1,128)S(1)}, f32[1,2048]{1,0:T(1,128)S(1)}, u32[]{:S(2)}, u32[]{:S(2)}) %collective-permute-start.17) | collective-permute-done | bytes 8224 | tf_op jit(solution)/shard_map/ppermute | solution.py:384
  261.1 3.6 %collective-permute-done.18 = f32[1,2048]{1,0:T(1,128)S(1)} collective-permute-done((f32[1,2048]{1,0:T(1,128)S(1)}, f32[1,2048]{1,0:T(1,128)S(1)}, u32[]{:S(2)}, u32[]{:S(2)}) %collective-permute-start.18) | collective-permute-done | bytes 8224 | tf_op jit(solution)/shard_map/ppermute | solution.py:384
  264.9 4.5 %collective-permute-done.19 = f32[1,2048]{1,0:T(1,128)S(1)} collective-permute-done((f32[1,2048]{1,0:T(1,128)S(1)}, f32[1,2048]{1,0:T(1,128)S(1)}, u32[]{:S(2)}, u32[]{:S(2)}) %collective-permute-start.19) | collective-permute-done | bytes 8224 | tf_op jit(solution)/shard_map/ppermute | solution.py:384
  269.4 5.1 %shard_map.75 = (f32[1,2048]{1,0:T(1,128)S(1)}, f32[1,2048]{1,0:T(1,128)S(1)}, f32[1,2048]{1,0:T(1,128)S(1)}, f32[1,1]{1,0:T(1,128)}, f32[1,2048]{1,0:T(1,128)S(1)}) custom-call(f32[2048,2048]{1,0:T(8,128)S(1)} %get-tuple-element.32.lower, f32[2048,128]{1,0:T(8,128)S(1)} %get-tuple-element.33.inverses, bf16[512,2048]{1,0:T(8,128)(2,1)S(1)} %bitcast.35, ...), custom_call_target="tpu_custom_call" | custom-call | tf_op jit(solution)/shard_map/pallas_call | solution.py:364
  274.5 1.2 collective-permute-done.20
  275.6 0.7 collective-permute-start.21
  276.3 3.0 collective-permute-done.21
  279.6 3.5 %collective-permute-done.22 = f32[1,2048]{1,0:T(1,128)S(1)} collective-permute-done((f32[1,2048]{1,0:T(1,128)S(1)}, f32[1,2048]{1,0:T(1,128)S(1)}, u32[]{:S(2)}, u32[]{:S(2)}) %collective-permute-start.22) | collective-permute-done | bytes 8224 | tf_op jit(solution)/shard_map/ppermute | solution.py:384
  283.2 3.6 %collective-permute-done.23 = f32[1,2048]{1,0:T(1,128)S(1)} collective-permute-done((f32[1,2048]{1,0:T(1,128)S(1)}, f32[1,2048]{1,0:T(1,128)S(1)}, u32[]{:S(2)}, u32[]{:S(2)}) %collective-permute-start.23) | collective-permute-done | bytes 8224 | tf_op jit(solution)/shard_map/ppermute | solution.py:384
  287.0 4.5 %collective-permute-done.24 = f32[1,2048]{1,0:T(1,128)S(1)} collective-permute-done((f32[1,2048]{1,0:T(1,128)S(1)}, f32[1,2048]{1,0:T(1,128)S(1)}, u32[]{:S(2)}, u32[]{:S(2)}) %collective-permute-start.24) | collective-permute-done | bytes 8224 | tf_op jit(solution)/shard_map/ppermute | solution.py:384
  291.5 5.0 %shard_map.76 = (f32[1,2048]{1,0:T(1,128)S(1)}, f32[1,2048]{1,0:T(1,128)S(1)}, f32[1,2048]{1,0:T(1,128)S(1)}, f32[1,1]{1,0:T(1,128)}, f32[1,2048]{1,0:T(1,128)S(1)}) custom-call(f32[2048,2048]{1,0:T(8,128)S(1)} %get-tuple-element.32.lower, f32[2048,128]{1,0:T(8,128)S(1)} %get-tuple-element.33.inverses, bf16[512,2048]{1,0:T(8,128)(2,1)S(1)} %bitcast.36, ...), custom_call_target="tpu_custom_call" | custom-call | tf_op jit(solution)/shard_map/pallas_call | solution.py:364
  296.5 1.2 collective-permute-done.25
  297.7 0.7 collective-permute-start.26
  298.4 3.0 collective-permute-done.26
  301.7 3.5 %collective-permute-done.27 = f32[1,2048]{1,0:T(1,128)S(1)} collective-permute-done((f32[1,2048]{1,0:T(1,128)S(1)}, f32[1,2048]{1,0:T(1,128)S(1)}, u32[]{:S(2)}, u32[]{:S(2)}) %collective-permute-start.27) | collective-permute-done | bytes 8224 | tf_op jit(solution)/shard_map/ppermute | solution.py:384
  305.2 3.6 %collective-permute-done.28 = f32[1,2048]{1,0:T(1,128)S(1)} collective-permute-done((f32[1,2048]{1,0:T(1,128)S(1)}, f32[1,2048]{1,0:T(1,128)S(1)}, u32[]{:S(2)}, u32[]{:S(2)}) %collective-permute-start.28) | collective-permute-done | bytes 8224 | tf_op jit(solution)/shard_map/ppermute | solution.py:384
  309.0 4.5 %collective-permute-done.29 = f32[1,2048]{1,0:T(1,128)S(1)} collective-permute-done((f32[1,2048]{1,0:T(1,128)S(1)}, f32[1,2048]{1,0:T(1,128)S(1)}, u32[]{:S(2)}, u32[]{:S(2)}) %collective-permute-start.29) | collective-permute-done | bytes 8224 | tf_op jit(solution)/shard_map/ppermute | solution.py:384
  313.5 5.1 %shard_map.77 = (f32[1,2048]{1,0:T(1,128)S(1)}, f32[1,2048]{1,0:T(1,128)}, f32[1,2048]{1,0:T(1,128)S(1)}, f32[1,1]{1,0:T(1,128)}, f32[1,2048]{1,0:T(1,128)S(1)}) custom-call(f32[2048,2048]{1,0:T(8,128)S(1)} %get-tuple-element.32.lower, f32[2048,128]{1,0:T(8,128)S(1)} %get-tuple-element.33.inverses, bf16[512,2048]{1,0:T(8,128)(2,1)S(1)} %bitcast.37, ...), custom_call_target="tpu_custom_call" | custom-call | tf_op jit(solution)/shard_map/pallas_call | solution.py:364
  318.6 1.2 collective-permute-done.30
  319.8 0.7 collective-permute-start.31
  320.5 3.0 collective-permute-done.31
  323.8 3.5 %collective-permute-done.32 = f32[1,2048]{1,0:T(1,128)S(1)} collective-permute-done((f32[1,2048]{1,0:T(1,128)S(1)}, f32[1,2048]{1,0:T(1,128)S(1)}, u32[]{:S(2)}, u32[]{:S(2)}) %collective-permute-start.32) | collective-permute-done | bytes 8224 | tf_op jit(solution)/shard_map/ppermute | solution.py:384
  327.4 3.6 %collective-permute-done.33 = f32[1,2048]{1,0:T(1,128)S(1)} collective-permute-done((f32[1,2048]{1,0:T(1,128)S(1)}, f32[1,2048]{1,0:T(1,128)S(1)}, u32[]{:S(2)}, u32[]{:S(2)}) %collective-permute-start.33) | collective-permute-done | bytes 8224 | tf_op jit(solution)/shard_map/ppermute | solution.py:384
  331.8 3.8 %collective-permute-done.34 = f32[1,2048]{1,0:T(1,128)S(1)} collective-permute-done((f32[1,2048]{1,0:T(1,128)S(1)}, f32[1,2048]{1,0:T(1,128)S(1)}, u32[]{:S(2)}, u32[]{:S(2)}) %collective-permute-start.34) | collective-permute-done | bytes 8224 | tf_op jit(solution)/shard_map/ppermute | solution.py:384
  335.6 0.9 shard_map.78
  336.5 0.6 add.169
  (87 shorter events, 4.0 us)
Async XLA Ops:
  6.5 6.6 %copy-start = (s32[2048]{0:T(1024)S(1)}, s32[2048]{0:T(1024)}, u32[]{:S(2)}) copy-start(s32[2048]{0:T(1024)} %param.11) | copy-start | bytes 24580
  6.5 6.6 %copy-start.6 = (s32[16,1]{0,1:T(1,128)S(1)}, s32[16,1]{0,1:T(1,128)}, u32[]{:S(2)}) copy-start(s32[16,1]{0,1:T(1,128)} %constant.42) | copy-start | bytes 196
  6.5 6.6 %copy-start.7 = (s32[16,1]{0,1:T(1,128)S(1)}, s32[16,1]{0,1:T(1,128)}, u32[]{:S(2)}) copy-start(s32[16,1]{0,1:T(1,128)} %constant.43) | copy-start | bytes 196
  6.5 12.9 %copy-start.1 = (bf16[2048,512]{1,0:T(8,128)(2,1)S(1)}, bf16[2048,512]{1,0:T(8,128)(2,1)}, u32[]{:S(2)}) copy-start(bf16[2048,512]{1,0:T(8,128)(2,1)} %param.7) | copy-start | bytes 6291460
  6.5 11.2 %copy-start.5 = (s32[2048]{0:T(1024)S(1)}, s32[2048]{0:T(1024)}, u32[]{:S(2)}) copy-start(s32[2048]{0:T(1024)} %param.10) | copy-start | bytes 24580
  6.5 12.9 %copy-start.4 = (s32[2048]{0:T(1024)S(1)}, s32[2048]{0:T(1024)}, u32[]{:S(2)}) copy-start(s32[2048]{0:T(1024)} %param.9) | copy-start | bytes 24580
  6.6 118.4 %all-gather.3.cloned.1.call-start = ((), (), s32[]{:S(2)}) async-start(), calls=%async_computation.1 | async-start | bytes 9437184 | tf_op jit(solution)/shard_map/all_gather | solution.py:447
  10.1 4.7 %collective-permute-start = (f32[2048]{0:T(1024)S(1)}, f32[2048]{0:T(1024)S(1)}, u32[]{:S(2)}, u32[]{:S(2)}) collective-permute-start(f32[2048]{0:T(1024)S(1)} %bitcast.46), channel_id=1, source_target_pairs={{0,1},{1,0},{2,3},{3,2},{4,5},{5,4},{6,7},{7,6},{8,9},{9,8},{10,11... | collective-permute-start | bytes 24584 | tf_op jit(solution)/shard_map/ppermute | solution.py:384
  14.7 4.7 %collective-permute-start.1 = (f32[2048]{0:T(1024)S(1)}, f32[2048]{0:T(1024)S(1)}, u32[]{:S(2)}, u32[]{:S(2)}) collective-permute-start(f32[2048]{0:T(1024)S(1)} %add.133), channel_id=1, source_target_pairs={{0,2},{1,3},{2,0},{3,1},{4,6},{5,7},{6,4},{7,5},{8,10},{9,11},{10,... | collective-permute-start | bytes 24584 | tf_op jit(solution)/shard_map/ppermute | solution.py:384
  19.9 5.2 %copy-start.2 = (bf16[2048,512]{1,0:T(8,128)(2,1)}, bf16[2048,512]{1,0:T(8,128)(2,1)S(1)}, u32[]{:S(2)}) copy-start(bf16[2048,512]{1,0:T(8,128)(2,1)S(1)} %multiply_convert_fusion) | copy-start | bytes 6291460
  22.3 2.7 collective-permute-start.2
  27.6 8.5 %collective-permute-start.3 = (f16[256,512]{1,0:T(8,128)(2,1)S(1)}, f16[256,512]{1,0:T(8,128)(2,1)S(1)}, u32[]{:S(2)}, u32[]{:S(2)}) collective-permute-start(f16[256,512]{1,0:T(8,128)(2,1)S(1)} %get-tuple-element.54), channel_id=1, source_target_pairs={{0,8},{4,12},{8,0},{12,4},{16,24},{20,28},{24,16},{28,20},{1,9},{5... | collective-permute-start | bytes 786440 | tf_op jit(solution)/shard_map/ppermute | solution.py:384
  29.5 8.1 %collective-permute-start.4 = (f16[256,512]{1,0:T(8,128)(2,1)S(1)}, f16[256,512]{1,0:T(8,128)(2,1)S(1)}, u32[]{:S(2)}, u32[]{:S(2)}) collective-permute-start(f16[256,512]{1,0:T(8,128)(2,1)S(1)} %get-tuple-element.53), channel_id=1, source_target_pairs={{0,16},{4,20},{8,24},{12,28},{16,0},{20,4},{24,8},{28,12},{1,17},{... | collective-permute-start | bytes 786440 | tf_op jit(solution)/shard_map/ppermute | solution.py:384
  37.8 5.0 %collective-permute-start.5 = (f16[128,512]{1,0:T(8,128)(2,1)S(1)}, f16[128,512]{1,0:T(8,128)(2,1)S(1)}, u32[]{:S(2)}, u32[]{:S(2)}) collective-permute-start(f16[128,512]{1,0:T(8,128)(2,1)S(1)} %slice_convert_fusion.1), channel_id=1, source_target_pairs={{0,16},{4,20},{8,24},{12,28},{16,0},{20,4},{24,8},{28,12},{1,17},{... | collective-permute-start | bytes 393224 | tf_op jit(solution)/shard_map/ppermute | solution.py:384
  39.4 5.0 %collective-permute-start.6 = (f16[128,512]{1,0:T(8,128)(2,1)S(1)}, f16[128,512]{1,0:T(8,128)(2,1)S(1)}, u32[]{:S(2)}, u32[]{:S(2)}) collective-permute-start(f16[128,512]{1,0:T(8,128)(2,1)S(1)} %slice_convert_fusion), channel_id=1, source_target_pairs={{0,8},{4,12},{8,0},{12,4},{16,24},{20,28},{24,16},{28,20},{1,9},{5... | collective-permute-start | bytes 393224 | tf_op jit(solution)/shard_map/ppermute | solution.py:384
  44.6 19.4 %collective-permute-start.8 = (bf16[256,512]{1,0:T(8,128)(2,1)S(1)}, bf16[256,512]{1,0:T(8,128)(2,1)S(1)}, u32[]{:S(2)}, u32[]{:S(2)}) collective-permute-start(bf16[256,512]{1,0:T(8,128)(2,1)S(1)} %fusion.20), channel_id=1, source_target_pairs={{0,2},{1,3},{2,0},{3,1},{4,6},{5,7},{6,4},{7,5},{8,10},{9,11},{10,... | collective-permute-start | bytes 786440 | tf_op jit(solution)/shard_map/ppermute | solution.py:378
  47.2 16.8 %collective-permute-start.9 = (bf16[256,512]{1,0:T(8,128)(2,1)S(1)}, bf16[256,512]{1,0:T(8,128)(2,1)S(1)}, u32[]{:S(2)}, u32[]{:S(2)}) collective-permute-start(bf16[256,512]{1,0:T(8,128)(2,1)S(1)} %fusion.20), channel_id=1, source_target_pairs={{0,3},{1,2},{2,1},{3,0},{4,7},{5,6},{6,5},{7,4},{8,11},{9,10},{10,... | collective-permute-start | bytes 786440 | tf_op jit(solution)/shard_map/ppermute | solution.py:378
  48.6 15.7 %collective-permute-start.7 = (bf16[256,512]{1,0:T(8,128)(2,1)S(1)}, bf16[256,512]{1,0:T(8,128)(2,1)S(1)}, u32[]{:S(2)}, u32[]{:S(2)}) collective-permute-start(bf16[256,512]{1,0:T(8,128)(2,1)S(1)} %fusion.20), channel_id=1, source_target_pairs={{0,1},{1,0},{2,3},{3,2},{4,5},{5,4},{6,7},{7,6},{8,9},{9,8},{10,11... | collective-permute-start | bytes 786440 | tf_op jit(solution)/shard_map/ppermute | solution.py:378
  65.4 57.7 %all-to-all-start = ((bf16[4,512,512]{2,1,0:T(8,128)(2,1)}), bf16[4,512,512]{2,1,0:T(8,128)(2,1)}, u32[]{:S(2)}, u32[]{:S(2)}) async-start(bf16[4,512,512]{2,1,0:T(8,128)(2,1)} %bitcast.39), calls=%async_computation | async-start | bytes 4194304 | tf_op jit(solution)/shard_map/all_to_all | solution.py:457
  73.5 0.9 copy-start.3
  74.7 1.2 collective-permute-start.10
  75.9 3.7 %collective-permute-start.11 = (f32[1,2048]{1,0:T(1,128)S(1)}, f32[1,2048]{1,0:T(1,128)S(1)}, u32[]{:S(2)}, u32[]{:S(2)}) collective-permute-start(f32[1,2048]{1,0:T(1,128)S(1)} %add.143), channel_id=1, source_target_pairs={{0,8},{4,12},{8,0},{12,4},{16,24},{20,28},{24,16},{28,20},{1,9},{5... | collective-permute-start | bytes 24584 | tf_op jit(solution)/shard_map/ppermute | solution.py:384
  79.7 3.9 %collective-permute-start.12 = (f32[1,2048]{1,0:T(1,128)S(1)}, f32[1,2048]{1,0:T(1,128)S(1)}, u32[]{:S(2)}, u32[]{:S(2)}) collective-permute-start(f32[1,2048]{1,0:T(1,128)S(1)} %add.144), channel_id=1, source_target_pairs={{0,16},{4,20},{8,24},{12,28},{16,0},{20,4},{24,8},{28,12},{1,17},{... | collective-permute-start | bytes 24584 | tf_op jit(solution)/shard_map/ppermute | solution.py:384
  83.5 24.2 %collective-permute-start.13 = (f32[1,2048]{1,0:T(1,128)S(1)}, f32[1,2048]{1,0:T(1,128)S(1)}, u32[]{:S(2)}, u32[]{:S(2)}) collective-permute-start(f32[1,2048]{1,0:T(1,128)S(1)} %add.145), channel_id=1, source_target_pairs={{0,1},{1,0},{2,3},{3,2},{4,5},{5,4},{6,7},{7,6},{8,9},{9,8},{10,11... | collective-permute-start | bytes 24584 | tf_op jit(solution)/shard_map/ppermute | solution.py:384
  107.7 15.3 %collective-permute-start.14 = (f32[1,2048]{1,0:T(1,128)S(1)}, f32[1,2048]{1,0:T(1,128)S(1)}, u32[]{:S(2)}, u32[]{:S(2)}) collective-permute-start(f32[1,2048]{1,0:T(1,128)S(1)} %add.146), channel_id=1, source_target_pairs={{0,2},{1,3},{2,0},{3,1},{4,6},{5,7},{6,4},{7,5},{8,10},{9,11},{10,... | collective-permute-start | bytes 24584 | tf_op jit(solution)/shard_map/ppermute | solution.py:384
  252.4 1.2 collective-permute-start.15
  253.6 3.7 %collective-permute-start.16 = (f32[1,2048]{1,0:T(1,128)S(1)}, f32[1,2048]{1,0:T(1,128)S(1)}, u32[]{:S(2)}, u32[]{:S(2)}) collective-permute-start(f32[1,2048]{1,0:T(1,128)S(1)} %add.148), channel_id=1, source_target_pairs={{0,8},{4,12},{8,0},{12,4},{16,24},{20,28},{24,16},{28,20},{1,9},{5... | collective-permute-start | bytes 24584 | tf_op jit(solution)/shard_map/ppermute | solution.py:384
  257.3 3.7 %collective-permute-start.17 = (f32[1,2048]{1,0:T(1,128)S(1)}, f32[1,2048]{1,0:T(1,128)S(1)}, u32[]{:S(2)}, u32[]{:S(2)}) collective-permute-start(f32[1,2048]{1,0:T(1,128)S(1)} %add.149), channel_id=1, source_target_pairs={{0,16},{4,20},{8,24},{12,28},{16,0},{20,4},{24,8},{28,12},{1,17},{... | collective-permute-start | bytes 24584 | tf_op jit(solution)/shard_map/ppermute | solution.py:384
  261.0 3.7 %collective-permute-start.18 = (f32[1,2048]{1,0:T(1,128)S(1)}, f32[1,2048]{1,0:T(1,128)S(1)}, u32[]{:S(2)}, u32[]{:S(2)}) collective-permute-start(f32[1,2048]{1,0:T(1,128)S(1)} %add.150), channel_id=1, source_target_pairs={{0,1},{1,0},{2,3},{3,2},{4,5},{5,4},{6,7},{7,6},{8,9},{9,8},{10,11... | collective-permute-start | bytes 24584 | tf_op jit(solution)/shard_map/ppermute | solution.py:384
  264.8 4.6 %collective-permute-start.19 = (f32[1,2048]{1,0:T(1,128)S(1)}, f32[1,2048]{1,0:T(1,128)S(1)}, u32[]{:S(2)}, u32[]{:S(2)}) collective-permute-start(f32[1,2048]{1,0:T(1,128)S(1)} %add.151), channel_id=1, source_target_pairs={{0,2},{1,3},{2,0},{3,1},{4,6},{5,7},{6,4},{7,5},{8,10},{9,11},{10,... | collective-permute-start | bytes 24584 | tf_op jit(solution)/shard_map/ppermute | solution.py:384
  274.5 1.2 collective-permute-start.20
  275.6 3.7 %collective-permute-start.21 = (f32[1,2048]{1,0:T(1,128)S(1)}, f32[1,2048]{1,0:T(1,128)S(1)}, u32[]{:S(2)}, u32[]{:S(2)}) collective-permute-start(f32[1,2048]{1,0:T(1,128)S(1)} %add.153), channel_id=1, source_target_pairs={{0,8},{4,12},{8,0},{12,4},{16,24},{20,28},{24,16},{28,20},{1,9},{5... | collective-permute-start | bytes 24584 | tf_op jit(solution)/shard_map/ppermute | solution.py:384
  279.4 3.7 %collective-permute-start.22 = (f32[1,2048]{1,0:T(1,128)S(1)}, f32[1,2048]{1,0:T(1,128)S(1)}, u32[]{:S(2)}, u32[]{:S(2)}) collective-permute-start(f32[1,2048]{1,0:T(1,128)S(1)} %add.154), channel_id=1, source_target_pairs={{0,16},{4,20},{8,24},{12,28},{16,0},{20,4},{24,8},{28,12},{1,17},{... | collective-permute-start | bytes 24584 | tf_op jit(solution)/shard_map/ppermute | solution.py:384
  283.1 3.7 %collective-permute-start.23 = (f32[1,2048]{1,0:T(1,128)S(1)}, f32[1,2048]{1,0:T(1,128)S(1)}, u32[]{:S(2)}, u32[]{:S(2)}) collective-permute-start(f32[1,2048]{1,0:T(1,128)S(1)} %add.155), channel_id=1, source_target_pairs={{0,1},{1,0},{2,3},{3,2},{4,5},{5,4},{6,7},{7,6},{8,9},{9,8},{10,11... | collective-permute-start | bytes 24584 | tf_op jit(solution)/shard_map/ppermute | solution.py:384
  286.8 4.6 %collective-permute-start.24 = (f32[1,2048]{1,0:T(1,128)S(1)}, f32[1,2048]{1,0:T(1,128)S(1)}, u32[]{:S(2)}, u32[]{:S(2)}) collective-permute-start(f32[1,2048]{1,0:T(1,128)S(1)} %add.156), channel_id=1, source_target_pairs={{0,2},{1,3},{2,0},{3,1},{4,6},{5,7},{6,4},{7,5},{8,10},{9,11},{10,... | collective-permute-start | bytes 24584 | tf_op jit(solution)/shard_map/ppermute | solution.py:384
  296.5 1.2 collective-permute-start.25
  297.7 3.7 %collective-permute-start.26 = (f32[1,2048]{1,0:T(1,128)S(1)}, f32[1,2048]{1,0:T(1,128)S(1)}, u32[]{:S(2)}, u32[]{:S(2)}) collective-permute-start(f32[1,2048]{1,0:T(1,128)S(1)} %add.158), channel_id=1, source_target_pairs={{0,8},{4,12},{8,0},{12,4},{16,24},{20,28},{24,16},{28,20},{1,9},{5... | collective-permute-start | bytes 24584 | tf_op jit(solution)/shard_map/ppermute | solution.py:384
  301.4 3.7 %collective-permute-start.27 = (f32[1,2048]{1,0:T(1,128)S(1)}, f32[1,2048]{1,0:T(1,128)S(1)}, u32[]{:S(2)}, u32[]{:S(2)}) collective-permute-start(f32[1,2048]{1,0:T(1,128)S(1)} %add.159), channel_id=1, source_target_pairs={{0,16},{4,20},{8,24},{12,28},{16,0},{20,4},{24,8},{28,12},{1,17},{... | collective-permute-start | bytes 24584 | tf_op jit(solution)/shard_map/ppermute | solution.py:384
  305.2 3.7 %collective-permute-start.28 = (f32[1,2048]{1,0:T(1,128)S(1)}, f32[1,2048]{1,0:T(1,128)S(1)}, u32[]{:S(2)}, u32[]{:S(2)}) collective-permute-start(f32[1,2048]{1,0:T(1,128)S(1)} %add.160), channel_id=1, source_target_pairs={{0,1},{1,0},{2,3},{3,2},{4,5},{5,4},{6,7},{7,6},{8,9},{9,8},{10,11... | collective-permute-start | bytes 24584 | tf_op jit(solution)/shard_map/ppermute | solution.py:384
  308.9 4.6 %collective-permute-start.29 = (f32[1,2048]{1,0:T(1,128)S(1)}, f32[1,2048]{1,0:T(1,128)S(1)}, u32[]{:S(2)}, u32[]{:S(2)}) collective-permute-start(f32[1,2048]{1,0:T(1,128)S(1)} %add.161), channel_id=1, source_target_pairs={{0,2},{1,3},{2,0},{3,1},{4,6},{5,7},{6,4},{7,5},{8,10},{9,11},{10,... | collective-permute-start | bytes 24584 | tf_op jit(solution)/shard_map/ppermute | solution.py:384
  318.6 1.2 collective-permute-start.30
  319.8 3.7 %collective-permute-start.31 = (f32[1,2048]{1,0:T(1,128)S(1)}, f32[1,2048]{1,0:T(1,128)S(1)}, u32[]{:S(2)}, u32[]{:S(2)}) collective-permute-start(f32[1,2048]{1,0:T(1,128)S(1)} %add.163), channel_id=1, source_target_pairs={{0,8},{4,12},{8,0},{12,4},{16,24},{20,28},{24,16},{28,20},{1,9},{5... | collective-permute-start | bytes 24584 | tf_op jit(solution)/shard_map/ppermute | solution.py:384
  323.5 3.7 %collective-permute-start.32 = (f32[1,2048]{1,0:T(1,128)S(1)}, f32[1,2048]{1,0:T(1,128)S(1)}, u32[]{:S(2)}, u32[]{:S(2)}) collective-permute-start(f32[1,2048]{1,0:T(1,128)S(1)} %add.164), channel_id=1, source_target_pairs={{0,16},{4,20},{8,24},{12,28},{16,0},{20,4},{24,8},{28,12},{1,17},{... | collective-permute-start | bytes 24584 | tf_op jit(solution)/shard_map/ppermute | solution.py:384
  327.3 3.7 %collective-permute-start.33 = (f32[1,2048]{1,0:T(1,128)S(1)}, f32[1,2048]{1,0:T(1,128)S(1)}, u32[]{:S(2)}, u32[]{:S(2)}) collective-permute-start(f32[1,2048]{1,0:T(1,128)S(1)} %add.165), channel_id=1, source_target_pairs={{0,1},{1,0},{2,3},{3,2},{4,5},{5,4},{6,7},{7,6},{8,9},{9,8},{10,11... | collective-permute-start | bytes 24584 | tf_op jit(solution)/shard_map/ppermute | solution.py:384
  331.0 4.6 %collective-permute-start.34 = (f32[1,2048]{1,0:T(1,128)S(1)}, f32[1,2048]{1,0:T(1,128)S(1)}, u32[]{:S(2)}, u32[]{:S(2)}) collective-permute-start(f32[1,2048]{1,0:T(1,128)S(1)} %add.166), channel_id=1, source_target_pairs={{0,2},{1,3},{2,0},{3,1},{4,6},{5,7},{6,4},{7,5},{8,10},{9,11},{10,... | collective-permute-start | bytes 24584 | tf_op jit(solution)/shard_map/ppermute | solution.py:384
Sparse Core Ops, SparseCore 0:
  65.5 57.1 all-gather.2

commit v3 on v2

--- a/solution.py
+++ b/solution.py
@@ -110,7 +110,7 @@
     )
 
 
-def factor_kernel(feat, pieces, work, inv_ref, sketch, right, wide, left, sem):
+def factor_kernel(feat, pieces, work, inv_ref, sketch, turned, right, left, sem):
     size = work.shape[0]
     blocks = size // BLOCK
     feat_count = pieces.shape[1]
@@ -136,14 +136,14 @@
     def gram(m, _):
         start = pl.multiple_of(m * CHUNK, CHUNK)
         here = pl.ds(start, CHUNK)
+        turned[...] = sketch[:, :, here].reshape(samples, CHUNK).T
         for c in range(chunks):
 
             @pl.when(c >= m)
             def _():
-                product = lax.dot_general(
-                    sketch[:, :, here].reshape(samples, CHUNK),
+                product = jnp.dot(
+                    turned[...],
                     sketch[:, :, chunk(c)].reshape(samples, CHUNK),
-                    (((0,), (0,)), ((), ())),
                     preferred_element_type=jnp.float32,
                 )
                 row = start + lax.broadcasted_iota(jnp.int32, product.shape, 0)
@@ -154,33 +154,31 @@
 
     lax.fori_loop(0, chunks, gram, 0)
 
-    def stage(k, c, lowest):
+    eye = (
+        lax.broadcasted_iota(jnp.int32, (BLOCK, BLOCK), 0)
+        == lax.broadcasted_iota(jnp.int32, (BLOCK, BLOCK), 1)
+    ).astype(jnp.float32)
+
+    def prepare(k, inverse, lowest):
         here = pl.ds(pl.multiple_of(k * BLOCK, BLOCK), BLOCK)
-        panel = work[here, chunk(c)]
-        if lowest <= c <= lowest + GROUP * BLOCK // CHUNK:
-            row = lax.broadcasted_iota(jnp.int32, panel.shape, 0)
-            col = c * CHUNK - k * BLOCK + lax.broadcasted_iota(jnp.int32, panel.shape, 1)
-            unit = jnp.where(row == col, 1.0, 0.0)
-            panel = jnp.where((col >= 0) & (col < BLOCK), unit, panel)
-            work[here, chunk(c)] = panel
-        high, low = split(panel)
-        right[0:BLOCK, chunk(c)] = high
-        right[BLOCK : 2 * BLOCK, chunk(c)] = high
-        right[2 * BLOCK : 3 * BLOCK, chunk(c)] = low
-        right[3 * BLOCK : 4 * BLOCK, chunk(c)] = low
-        if c >= lowest:
-            high, low = split(panel.T)
-            wide[chunk(c), :] = jnp.concatenate([high, low, high, low], axis=1)
-
-    def finish(k, inverse, lowest):
-        inv_ref[pl.ds(pl.multiple_of(k * BLOCK, BLOCK), BLOCK), :] = inverse
+        inv_ref[here, :] = inverse
         high, low = split(inverse)
         diag = jnp.concatenate([high, high, low, low], axis=0)
-        for c in range(lowest, chunks):
-            scaled = jnp.dot(wide[chunk(c), :], diag, preferred_element_type=jnp.float32)
-            place = c * CHUNK + lax.broadcasted_iota(jnp.int32, (CHUNK, BLOCK), 0)
-            high, low = split(jnp.where(place >= (k + 1) * BLOCK, scaled, 0.0))
-            left[chunk(c), :] = jnp.concatenate([high, low, high, low], axis=1)
+        work[here, here] = eye
+        for c in range(chunks):
+            panel = work[here, chunk(c)]
+            high, low = split(panel)
+            right[0:BLOCK, chunk(c)] = high
+            right[BLOCK : 2 * BLOCK, chunk(c)] = high
+            right[2 * BLOCK : 3 * BLOCK, chunk(c)] = low
+            right[3 * BLOCK : 4 * BLOCK, chunk(c)] = low
+            if c >= lowest:
+                high, low = split(panel.T)
+                wide = jnp.concatenate([high, low, high, low], axis=1)
+                scaled = jnp.dot(wide, diag, preferred_element_type=jnp.float32)
+                place = c * CHUNK + lax.broadcasted_iota(jnp.int32, (CHUNK, BLOCK), 0)
+                high, low = split(jnp.where(place >= (k + 1) * BLOCK, scaled, 0.0))
+                left[chunk(c), :] = jnp.concatenate([high, low, high, low], axis=1)
 
     def update(k, m, c, lowest):
         product = jnp.dot(
@@ -194,26 +192,23 @@
             value = jnp.where(fresh, 0.0, value)
         work[chunk(m), chunk(c)] = value - product
 
-    inverse = invert_block(work[0:BLOCK, 0:BLOCK])
-    for c in range(chunks):
-        stage(0, c, 0)
-    finish(0, inverse, 0)
+    prepare(0, invert_block(work[0:BLOCK, 0:BLOCK]), 0)
     for first in range(0, blocks, GROUP):
         lowest = first * BLOCK // CHUNK
         settled = lowest + GROUP * BLOCK // CHUNK
+        wanted = [
+            (m, c) for m in range(lowest, chunks) for c in range(chunks) if c < settled or c >= m
+        ]
 
         def outer(k, _):
             following = pl.ds(pl.multiple_of((k + 1) * BLOCK, BLOCK), BLOCK)
             block = work[following, following] - jnp.dot(
                 left[following, :], right[:, following], preferred_element_type=jnp.float32
             )
-            pieces = []
-            for c in range(chunks):
-                for m in range(lowest, chunks):
-                    if c < settled or c >= m:
-                        pieces.append(functools.partial(update, k, m, c, lowest))
-                pieces.append(functools.partial(stage, k + 1, c, lowest))
-            finish(k + 1, invert_block(block, pieces), lowest)
+            inverse = invert_block(
+                block, [functools.partial(update, k, m, c, lowest) for m, c in wanted]
+            )
+            prepare(k + 1, inverse, lowest)
             return 0
 
         lax.fori_loop(first, min(first + GROUP, blocks - 1), outer, 0)
@@ -244,8 +239,8 @@
         ],
         scratch_shapes=[
             pltpu.VMEM((ex_count, rows, size), jnp.bfloat16),
+            pltpu.VMEM((CHUNK, ex_count * rows), jnp.bfloat16),
             pltpu.VMEM((4 * BLOCK, size), jnp.bfloat16),
-            pltpu.VMEM((size, 4 * BLOCK), jnp.bfloat16),
             pltpu.VMEM((size, 4 * BLOCK), jnp.bfloat16),
             pltpu.SemaphoreType.DMA((feat_count,)),
         ],

time: 351 us -> 345 us (0.983)
  Pallas kernels: 144 us -> 137 us
    pallas_call x1, Pallas kernels: 123 us -> 116 us  [factor(): pl.pallas_call(factor_kernel, in_specs=[pl.BlockSpec(memory_space=pltpu.S...]
where the time goes in v3:
time: 345 us; the launch traced here: 338 us
  Pallas kernels  137 us (40%)
  waiting for transfers between devices  134 us (39%)
  starting transfers between devices  37.1 us (11%)
  between operations  14.9 us (4%)
  matrix products  9.23 us (3%)
    ppermute x32, waiting for transfers between devices, swap(): lax.ppermute(value, axis, [(s, s ^ mask) for s in range(lax.axis_size(axi...  119 us
    pallas_call x1, Pallas kernels, factor(): pl.pallas_call(factor_kernel, in_specs=[pl.BlockSpec(memory_space=pltpu.S...  116 us
    ppermute x32, starting transfers between devices, swap(): lax.ppermute(value, axis, [(s, s ^ mask) for s in range(lax.axis_size(axi...  24.7 us
    pallas_call x5, Pallas kernels, call(): pl.pallas_call(kernel, in_specs=[VMEM] * len(args), out_specs=[VMEM] * le...  21 us
    ppermute x3, waiting for transfers between devices, exchange(): lax.ppermute(value, axis, [(s, s ^ mask) for s in range(count)])  15.4 us
    all_to_all x1, starting transfers between devices, local(): lax.all_to_all(weighted, 'feat', split_axis=0, concat_axis=1, tiled=True)  8.15 us
  transfers between devices with their start and end apart: 37, of which 34 were waited for; matrix products, arithmetic and copies ran while one was open for 1% of the time, Pallas kernels for 0%

profile of v3, /device:TPU:0, one launch (start us, length us, event | category | flops | bytes accessed | tf_op | source)
XLA Modules:
  0.0 338.4 jit_solution(7912726590667118792)
XLA Ops:
  6.6 3.5 %fusion.29 = f32[1,2048]{1,0:T(1,128)S(1)} fusion(bf16[2048,512]{1,0:T(8,128)(2,1)} %param.7, f32[512,1]{0,1:T(1,128)} %bitcast.51), kind=kOutput, calls=%fused_computation.50 | convolution fusion | flops 12582912 | bytes 2107392 | tf_op jit(solution)/shard_map/dot_general | solution.py:433
  10.1 3.0 collective-permute-start
  13.1 0.6 gather_fusion
  13.7 1.0 collective-permute-done
  14.7 3.0 collective-permute-start.1
  17.8 1.6 collective-permute-done.1
  19.4 0.5 multiply_convert_fusion
  19.9 2.4 fusion.14
  22.4 2.6 collective-permute-done.2
  25.1 2.4 fusion.28
  27.6 1.9 collective-permute-start.3
  29.5 1.5 collective-permute-start.4
  31.0 5.1 %collective-permute-done.3 = f16[256,512]{1,0:T(8,128)(2,1)S(1)} collective-permute-done((f16[256,512]{1,0:T(8,128)(2,1)S(1)}, f16[256,512]{1,0:T(8,128)(2,1)S(1)}, u32[]{:S(2)}, u32[]{:S(2)}) %collective-permute-start.3) | collective-permute-done | bytes 262176 | tf_op jit(solution)/shard_map/ppermute | solution.py:379
  36.1 1.5 collective-permute-done.4
  37.8 1.6 collective-permute-start.5
  39.4 0.6 collective-permute-start.6
  40.0 2.8 collective-permute-done.5
  42.8 1.6 collective-permute-done.6
  44.6 2.7 collective-permute-start.8
  47.2 1.3 collective-permute-start.9
  48.8 15.1 %collective-permute-done.8 = bf16[256,512]{1,0:T(8,128)(2,1)S(1)} collective-permute-done((bf16[256,512]{1,0:T(8,128)(2,1)S(1)}, bf16[256,512]{1,0:T(8,128)(2,1)S(1)}, u32[]{:S(2)}, u32[]{:S(2)}) %collective-permute-start.8) | collective-permute-done | bytes 262176 | tf_op jit(solution)/shard_map/ppermute | solution.py:373
  64.2 1.1 pad_maximum_fusion
  65.3 8.2 %all-to-all-start = ((bf16[4,512,512]{2,1,0:T(8,128)(2,1)}), bf16[4,512,512]{2,1,0:T(8,128)(2,1)}, u32[]{:S(2)}, u32[]{:S(2)}) async-start(bf16[4,512,512]{2,1,0:T(8,128)(2,1)} %bitcast.39), calls=%async_computation | async-start | bytes 4194304 | tf_op jit(solution)/shard_map/all_to_all | solution.py:452
  73.5 0.9 fusion.30
  74.7 1.2 collective-permute-done.10
  75.9 0.6 collective-permute-start.11
  76.6 3.1 collective-permute-done.11
  79.9 3.6 %collective-permute-done.12 = f32[1,2048]{1,0:T(1,128)S(1)} collective-permute-done((f32[1,2048]{1,0:T(1,128)S(1)}, f32[1,2048]{1,0:T(1,128)S(1)}, u32[]{:S(2)}, u32[]{:S(2)}) %collective-permute-start.12) | collective-permute-done | bytes 8224 | tf_op jit(solution)/shard_map/ppermute | solution.py:379
  83.5 2.1 collective-permute-start.13
  85.6 22.1 %collective-permute-done.13 = f32[1,2048]{1,0:T(1,128)S(1)} collective-permute-done((f32[1,2048]{1,0:T(1,128)S(1)}, f32[1,2048]{1,0:T(1,128)S(1)}, u32[]{:S(2)}, u32[]{:S(2)}) %collective-permute-start.13) | collective-permute-done | bytes 8224 | tf_op jit(solution)/shard_map/ppermute | solution.py:379
  107.7 4.7 %collective-permute-start.14 = (f32[1,2048]{1,0:T(1,128)S(1)}, f32[1,2048]{1,0:T(1,128)S(1)}, u32[]{:S(2)}, u32[]{:S(2)}) collective-permute-start(f32[1,2048]{1,0:T(1,128)S(1)} %add.146), channel_id=1, source_target_pairs={{0,2},{1,3},{2,0},{3,1},{4,6},{5,7},{6,4},{7,5},{8,10},{9,11},{10,... | collective-permute-start | bytes 24584 | tf_op jit(solution)/shard_map/ppermute | solution.py:379
  112.4 10.6 %collective-permute-done.14 = f32[1,2048]{1,0:T(1,128)S(1)} collective-permute-done((f32[1,2048]{1,0:T(1,128)S(1)}, f32[1,2048]{1,0:T(1,128)S(1)}, u32[]{:S(2)}, u32[]{:S(2)}) %collective-permute-start.14) | collective-permute-done | bytes 8224 | tf_op jit(solution)/shard_map/ppermute | solution.py:379
  123.0 1.9 copy.10
  124.9 116.4 %shard_map.73 = (f32[2048,2048]{1,0:T(8,128)S(1)}, f32[2048,128]{1,0:T(8,128)S(1)}) custom-call(s32[1]{0:T(128)} %bitcast.feat, bf16[8,4,256,512]{3,2,1,0:T(8,128)(2,1)} %bitcast.38), custom_call_target="tpu_custom_call" | custom-call | tf_op jit(solution)/shard_map/pallas_call | solution.py:229
  241.4 4.6 %shard_map.74 = (f32[1,2048]{1,0:T(1,128)S(1)}, f32[1,1]{1,0:T(1,128)}, f32[1,2048]{1,0:T(1,128)S(1)}) custom-call(f32[2048,2048]{1,0:T(8,128)S(1)} %get-tuple-element.32.lower, f32[2048,128]{1,0:T(8,128)S(1)} %get-tuple-element.33.inverses, bf16[512,2048]{1,0:T(8,128)(2,1)S(1)} %bitcast.34, f32[1,2048]{1,0:T(1,128)S(1)} %add_negate_fusion.residual), custom_call_target="tpu_custom_call" | custom-call | tf_op jit(solution)/shard_map/pallas_call | solution.py:359
  246.0 1.1 collective-permute-done.15
  247.2 0.7 collective-permute-start.16
  247.8 3.1 collective-permute-done.16
  251.2 3.4 %collective-permute-done.17 = f32[1,2048]{1,0:T(1,128)S(1)} collective-permute-done((f32[1,2048]{1,0:T(1,128)S(1)}, f32[1,2048]{1,0:T(1,128)S(1)}, u32[]{:S(2)}, u32[]{:S(2)}) %collective-permute-start.17) | collective-permute-done | bytes 8224 | tf_op jit(solution)/shard_map/ppermute | solution.py:379
  254.7 3.6 %collective-permute-done.18 = f32[1,2048]{1,0:T(1,128)S(1)} collective-permute-done((f32[1,2048]{1,0:T(1,128)S(1)}, f32[1,2048]{1,0:T(1,128)S(1)}, u32[]{:S(2)}, u32[]{:S(2)}) %collective-permute-start.18) | collective-permute-done | bytes 8224 | tf_op jit(solution)/shard_map/ppermute | solution.py:379
  258.6 4.4 %collective-permute-done.19 = f32[1,2048]{1,0:T(1,128)S(1)} collective-permute-done((f32[1,2048]{1,0:T(1,128)S(1)}, f32[1,2048]{1,0:T(1,128)S(1)}, u32[]{:S(2)}, u32[]{:S(2)}) %collective-permute-start.19) | collective-permute-done | bytes 8224 | tf_op jit(solution)/shard_map/ppermute | solution.py:379
  263.0 5.3 %shard_map.75 = (f32[1,2048]{1,0:T(1,128)S(1)}, f32[1,2048]{1,0:T(1,128)S(1)}, f32[1,2048]{1,0:T(1,128)S(1)}, f32[1,1]{1,0:T(1,128)}, f32[1,2048]{1,0:T(1,128)S(1)}) custom-call(f32[2048,2048]{1,0:T(8,128)S(1)} %get-tuple-element.32.lower, f32[2048,128]{1,0:T(8,128)S(1)} %get-tuple-element.33.inverses, bf16[512,2048]{1,0:T(8,128)(2,1)S(1)} %bitcast.35, ...), custom_call_target="tpu_custom_call" | custom-call | tf_op jit(solution)/shard_map/pallas_call | solution.py:359
  268.3 1.2 collective-permute-done.20
  269.5 0.7 collective-permute-start.21
  270.2 3.1 collective-permute-done.21
  273.5 3.4 %collective-permute-done.22 = f32[1,2048]{1,0:T(1,128)S(1)} collective-permute-done((f32[1,2048]{1,0:T(1,128)S(1)}, f32[1,2048]{1,0:T(1,128)S(1)}, u32[]{:S(2)}, u32[]{:S(2)}) %collective-permute-start.22) | collective-permute-done | bytes 8224 | tf_op jit(solution)/shard_map/ppermute | solution.py:379
  277.1 3.6 %collective-permute-done.23 = f32[1,2048]{1,0:T(1,128)S(1)} collective-permute-done((f32[1,2048]{1,0:T(1,128)S(1)}, f32[1,2048]{1,0:T(1,128)S(1)}, u32[]{:S(2)}, u32[]{:S(2)}) %collective-permute-start.23) | collective-permute-done | bytes 8224 | tf_op jit(solution)/shard_map/ppermute | solution.py:379
  281.0 4.3 %collective-permute-done.24 = f32[1,2048]{1,0:T(1,128)S(1)} collective-permute-done((f32[1,2048]{1,0:T(1,128)S(1)}, f32[1,2048]{1,0:T(1,128)S(1)}, u32[]{:S(2)}, u32[]{:S(2)}) %collective-permute-start.24) | collective-permute-done | bytes 8224 | tf_op jit(solution)/shard_map/ppermute | solution.py:379
  285.3 5.0 %shard_map.76 = (f32[1,2048]{1,0:T(1,128)S(1)}, f32[1,2048]{1,0:T(1,128)S(1)}, f32[1,2048]{1,0:T(1,128)S(1)}, f32[1,1]{1,0:T(1,128)}, f32[1,2048]{1,0:T(1,128)S(1)}) custom-call(f32[2048,2048]{1,0:T(8,128)S(1)} %get-tuple-element.32.lower, f32[2048,128]{1,0:T(8,128)S(1)} %get-tuple-element.33.inverses, bf16[512,2048]{1,0:T(8,128)(2,1)S(1)} %bitcast.36, ...), custom_call_target="tpu_custom_call" | custom-call | tf_op jit(solution)/shard_map/pallas_call | solution.py:359
  290.4 1.2 collective-permute-done.25
  291.6 0.7 collective-permute-start.26
  292.2 3.1 collective-permute-done.26
  295.6 3.4 %collective-permute-done.27 = f32[1,2048]{1,0:T(1,128)S(1)} collective-permute-done((f32[1,2048]{1,0:T(1,128)S(1)}, f32[1,2048]{1,0:T(1,128)S(1)}, u32[]{:S(2)}, u32[]{:S(2)}) %collective-permute-start.27) | collective-permute-done | bytes 8224 | tf_op jit(solution)/shard_map/ppermute | solution.py:379
  299.1 3.6 %collective-permute-done.28 = f32[1,2048]{1,0:T(1,128)S(1)} collective-permute-done((f32[1,2048]{1,0:T(1,128)S(1)}, f32[1,2048]{1,0:T(1,128)S(1)}, u32[]{:S(2)}, u32[]{:S(2)}) %collective-permute-start.28) | collective-permute-done | bytes 8224 | tf_op jit(solution)/shard_map/ppermute | solution.py:379
  303.1 4.3 %collective-permute-done.29 = f32[1,2048]{1,0:T(1,128)S(1)} collective-permute-done((f32[1,2048]{1,0:T(1,128)S(1)}, f32[1,2048]{1,0:T(1,128)S(1)}, u32[]{:S(2)}, u32[]{:S(2)}) %collective-permute-start.29) | collective-permute-done | bytes 8224 | tf_op jit(solution)/shard_map/ppermute | solution.py:379
  307.4 5.1 %shard_map.77 = (f32[1,2048]{1,0:T(1,128)S(1)}, f32[1,2048]{1,0:T(1,128)}, f32[1,2048]{1,0:T(1,128)S(1)}, f32[1,1]{1,0:T(1,128)}, f32[1,2048]{1,0:T(1,128)S(1)}) custom-call(f32[2048,2048]{1,0:T(8,128)S(1)} %get-tuple-element.32.lower, f32[2048,128]{1,0:T(8,128)S(1)} %get-tuple-element.33.inverses, bf16[512,2048]{1,0:T(8,128)(2,1)S(1)} %bitcast.37, ...), custom_call_target="tpu_custom_call" | custom-call | tf_op jit(solution)/shard_map/pallas_call | solution.py:359
  312.5 1.2 collective-permute-done.30
  313.7 0.7 collective-permute-start.31
  314.4 3.1 collective-permute-done.31
  317.7 3.4 %collective-permute-done.32 = f32[1,2048]{1,0:T(1,128)S(1)} collective-permute-done((f32[1,2048]{1,0:T(1,128)S(1)}, f32[1,2048]{1,0:T(1,128)S(1)}, u32[]{:S(2)}, u32[]{:S(2)}) %collective-permute-start.32) | collective-permute-done | bytes 8224 | tf_op jit(solution)/shard_map/ppermute | solution.py:379
  321.2 3.6 %collective-permute-done.33 = f32[1,2048]{1,0:T(1,128)S(1)} collective-permute-done((f32[1,2048]{1,0:T(1,128)S(1)}, f32[1,2048]{1,0:T(1,128)S(1)}, u32[]{:S(2)}, u32[]{:S(2)}) %collective-permute-start.33) | collective-permute-done | bytes 8224 | tf_op jit(solution)/shard_map/ppermute | solution.py:379
  325.9 3.6 %collective-permute-done.34 = f32[1,2048]{1,0:T(1,128)S(1)} collective-permute-done((f32[1,2048]{1,0:T(1,128)S(1)}, f32[1,2048]{1,0:T(1,128)S(1)}, u32[]{:S(2)}, u32[]{:S(2)}) %collective-permute-start.34) | collective-permute-done | bytes 8224 | tf_op jit(solution)/shard_map/ppermute | solution.py:379
  329.5 0.9 shard_map.78
  330.4 0.6 add.169
  (87 shorter events, 4.6 us)
Async XLA Ops:
  6.5 6.6 %copy-start = (s32[2048]{0:T(1024)S(1)}, s32[2048]{0:T(1024)}, u32[]{:S(2)}) copy-start(s32[2048]{0:T(1024)} %param.11) | copy-start | bytes 24580
  6.5 6.6 %copy-start.6 = (s32[16,1]{0,1:T(1,128)S(1)}, s32[16,1]{0,1:T(1,128)}, u32[]{:S(2)}) copy-start(s32[16,1]{0,1:T(1,128)} %constant.42) | copy-start | bytes 196
  6.5 6.6 %copy-start.7 = (s32[16,1]{0,1:T(1,128)S(1)}, s32[16,1]{0,1:T(1,128)}, u32[]{:S(2)}) copy-start(s32[16,1]{0,1:T(1,128)} %constant.43) | copy-start | bytes 196
  6.5 12.9 %copy-start.1 = (bf16[2048,512]{1,0:T(8,128)(2,1)S(1)}, bf16[2048,512]{1,0:T(8,128)(2,1)}, u32[]{:S(2)}) copy-start(bf16[2048,512]{1,0:T(8,128)(2,1)} %param.7) | copy-start | bytes 6291460
  6.5 11.2 %copy-start.5 = (s32[2048]{0:T(1024)S(1)}, s32[2048]{0:T(1024)}, u32[]{:S(2)}) copy-start(s32[2048]{0:T(1024)} %param.10) | copy-start | bytes 24580
  6.5 12.9 %copy-start.4 = (s32[2048]{0:T(1024)S(1)}, s32[2048]{0:T(1024)}, u32[]{:S(2)}) copy-start(s32[2048]{0:T(1024)} %param.9) | copy-start | bytes 24580
  6.6 118.4 %all-gather.3.cloned.1.call-start = ((), (), s32[]{:S(2)}) async-start(), calls=%async_computation.1 | async-start | bytes 9437184 | tf_op jit(solution)/shard_map/all_gather | solution.py:442
  10.1 4.7 %collective-permute-start = (f32[2048]{0:T(1024)S(1)}, f32[2048]{0:T(1024)S(1)}, u32[]{:S(2)}, u32[]{:S(2)}) collective-permute-start(f32[2048]{0:T(1024)S(1)} %bitcast.46), channel_id=1, source_target_pairs={{0,1},{1,0},{2,3},{3,2},{4,5},{5,4},{6,7},{7,6},{8,9},{9,8},{10,11... | collective-permute-start | bytes 24584 | tf_op jit(solution)/shard_map/ppermute | solution.py:379
  14.7 4.7 %collective-permute-start.1 = (f32[2048]{0:T(1024)S(1)}, f32[2048]{0:T(1024)S(1)}, u32[]{:S(2)}, u32[]{:S(2)}) collective-permute-start(f32[2048]{0:T(1024)S(1)} %add.133), channel_id=1, source_target_pairs={{0,2},{1,3},{2,0},{3,1},{4,6},{5,7},{6,4},{7,5},{8,10},{9,11},{10,... | collective-permute-start | bytes 24584 | tf_op jit(solution)/shard_map/ppermute | solution.py:379
  19.9 5.2 %copy-start.2 = (bf16[2048,512]{1,0:T(8,128)(2,1)}, bf16[2048,512]{1,0:T(8,128)(2,1)S(1)}, u32[]{:S(2)}) copy-start(bf16[2048,512]{1,0:T(8,128)(2,1)S(1)} %multiply_convert_fusion) | copy-start | bytes 6291460
  22.3 2.7 collective-permute-start.2
  27.6 8.5 %collective-permute-start.3 = (f16[256,512]{1,0:T(8,128)(2,1)S(1)}, f16[256,512]{1,0:T(8,128)(2,1)S(1)}, u32[]{:S(2)}, u32[]{:S(2)}) collective-permute-start(f16[256,512]{1,0:T(8,128)(2,1)S(1)} %get-tuple-element.54), channel_id=1, source_target_pairs={{0,8},{4,12},{8,0},{12,4},{16,24},{20,28},{24,16},{28,20},{1,9},{5... | collective-permute-start | bytes 786440 | tf_op jit(solution)/shard_map/ppermute | solution.py:379
  29.5 8.1 %collective-permute-start.4 = (f16[256,512]{1,0:T(8,128)(2,1)S(1)}, f16[256,512]{1,0:T(8,128)(2,1)S(1)}, u32[]{:S(2)}, u32[]{:S(2)}) collective-permute-start(f16[256,512]{1,0:T(8,128)(2,1)S(1)} %get-tuple-element.53), channel_id=1, source_target_pairs={{0,16},{4,20},{8,24},{12,28},{16,0},{20,4},{24,8},{28,12},{1,17},{... | collective-permute-start | bytes 786440 | tf_op jit(solution)/shard_map/ppermute | solution.py:379
  37.8 5.0 %collective-permute-start.5 = (f16[128,512]{1,0:T(8,128)(2,1)S(1)}, f16[128,512]{1,0:T(8,128)(2,1)S(1)}, u32[]{:S(2)}, u32[]{:S(2)}) collective-permute-start(f16[128,512]{1,0:T(8,128)(2,1)S(1)} %slice_convert_fusion.1), channel_id=1, source_target_pairs={{0,16},{4,20},{8,24},{12,28},{16,0},{20,4},{24,8},{28,12},{1,17},{... | collective-permute-start | bytes 393224 | tf_op jit(solution)/shard_map/ppermute | solution.py:379
  39.4 5.0 %collective-permute-start.6 = (f16[128,512]{1,0:T(8,128)(2,1)S(1)}, f16[128,512]{1,0:T(8,128)(2,1)S(1)}, u32[]{:S(2)}, u32[]{:S(2)}) collective-permute-start(f16[128,512]{1,0:T(8,128)(2,1)S(1)} %slice_convert_fusion), channel_id=1, source_target_pairs={{0,8},{4,12},{8,0},{12,4},{16,24},{20,28},{24,16},{28,20},{1,9},{5... | collective-permute-start | bytes 393224 | tf_op jit(solution)/shard_map/ppermute | solution.py:379
  44.6 19.4 %collective-permute-start.8 = (bf16[256,512]{1,0:T(8,128)(2,1)S(1)}, bf16[256,512]{1,0:T(8,128)(2,1)S(1)}, u32[]{:S(2)}, u32[]{:S(2)}) collective-permute-start(bf16[256,512]{1,0:T(8,128)(2,1)S(1)} %fusion.20), channel_id=1, source_target_pairs={{0,2},{1,3},{2,0},{3,1},{4,6},{5,7},{6,4},{7,5},{8,10},{9,11},{10,... | collective-permute-start | bytes 786440 | tf_op jit(solution)/shard_map/ppermute | solution.py:373
  47.2 16.8 %collective-permute-start.9 = (bf16[256,512]{1,0:T(8,128)(2,1)S(1)}, bf16[256,512]{1,0:T(8,128)(2,1)S(1)}, u32[]{:S(2)}, u32[]{:S(2)}) collective-permute-start(bf16[256,512]{1,0:T(8,128)(2,1)S(1)} %fusion.20), channel_id=1, source_target_pairs={{0,3},{1,2},{2,1},{3,0},{4,7},{5,6},{6,5},{7,4},{8,11},{9,10},{10,... | collective-permute-start | bytes 786440 | tf_op jit(solution)/shard_map/ppermute | solution.py:373
  48.6 15.6 %collective-permute-start.7 = (bf16[256,512]{1,0:T(8,128)(2,1)S(1)}, bf16[256,512]{1,0:T(8,128)(2,1)S(1)}, u32[]{:S(2)}, u32[]{:S(2)}) collective-permute-start(bf16[256,512]{1,0:T(8,128)(2,1)S(1)} %fusion.20), channel_id=1, source_target_pairs={{0,1},{1,0},{2,3},{3,2},{4,5},{5,4},{6,7},{7,6},{8,9},{9,8},{10,11... | collective-permute-start | bytes 786440 | tf_op jit(solution)/shard_map/ppermute | solution.py:373
  65.3 57.7 %all-to-all-start = ((bf16[4,512,512]{2,1,0:T(8,128)(2,1)}), bf16[4,512,512]{2,1,0:T(8,128)(2,1)}, u32[]{:S(2)}, u32[]{:S(2)}) async-start(bf16[4,512,512]{2,1,0:T(8,128)(2,1)} %bitcast.39), calls=%async_computation | async-start | bytes 4194304 | tf_op jit(solution)/shard_map/all_to_all | solution.py:452
  73.5 0.9 copy-start.3
  74.7 1.2 collective-permute-start.10
  75.9 3.7 %collective-permute-start.11 = (f32[1,2048]{1,0:T(1,128)S(1)}, f32[1,2048]{1,0:T(1,128)S(1)}, u32[]{:S(2)}, u32[]{:S(2)}) collective-permute-start(f32[1,2048]{1,0:T(1,128)S(1)} %add.143), channel_id=1, source_target_pairs={{0,8},{4,12},{8,0},{12,4},{16,24},{20,28},{24,16},{28,20},{1,9},{5... | collective-permute-start | bytes 24584 | tf_op jit(solution)/shard_map/ppermute | solution.py:379
  79.6 3.9 %collective-permute-start.12 = (f32[1,2048]{1,0:T(1,128)S(1)}, f32[1,2048]{1,0:T(1,128)S(1)}, u32[]{:S(2)}, u32[]{:S(2)}) collective-permute-start(f32[1,2048]{1,0:T(1,128)S(1)} %add.144), channel_id=1, source_target_pairs={{0,16},{4,20},{8,24},{12,28},{16,0},{20,4},{24,8},{28,12},{1,17},{... | collective-permute-start | bytes 24584 | tf_op jit(solution)/shard_map/ppermute | solution.py:379
  83.5 24.2 %collective-permute-start.13 = (f32[1,2048]{1,0:T(1,128)S(1)}, f32[1,2048]{1,0:T(1,128)S(1)}, u32[]{:S(2)}, u32[]{:S(2)}) collective-permute-start(f32[1,2048]{1,0:T(1,128)S(1)} %add.145), channel_id=1, source_target_pairs={{0,1},{1,0},{2,3},{3,2},{4,5},{5,4},{6,7},{7,6},{8,9},{9,8},{10,11... | collective-permute-start | bytes 24584 | tf_op jit(solution)/shard_map/ppermute | solution.py:379
  107.7 15.3 %collective-permute-start.14 = (f32[1,2048]{1,0:T(1,128)S(1)}, f32[1,2048]{1,0:T(1,128)S(1)}, u32[]{:S(2)}, u32[]{:S(2)}) collective-permute-start(f32[1,2048]{1,0:T(1,128)S(1)} %add.146), channel_id=1, source_target_pairs={{0,2},{1,3},{2,0},{3,1},{4,6},{5,7},{6,4},{7,5},{8,10},{9,11},{10,... | collective-permute-start | bytes 24584 | tf_op jit(solution)/shard_map/ppermute | solution.py:379
  246.0 1.2 collective-permute-start.15
  247.2 3.7 %collective-permute-start.16 = (f32[1,2048]{1,0:T(1,128)S(1)}, f32[1,2048]{1,0:T(1,128)S(1)}, u32[]{:S(2)}, u32[]{:S(2)}) collective-permute-start(f32[1,2048]{1,0:T(1,128)S(1)} %add.148), channel_id=1, source_target_pairs={{0,8},{4,12},{8,0},{12,4},{16,24},{20,28},{24,16},{28,20},{1,9},{5... | collective-permute-start | bytes 24584 | tf_op jit(solution)/shard_map/ppermute | solution.py:379
  250.9 3.7 %collective-permute-start.17 = (f32[1,2048]{1,0:T(1,128)S(1)}, f32[1,2048]{1,0:T(1,128)S(1)}, u32[]{:S(2)}, u32[]{:S(2)}) collective-permute-start(f32[1,2048]{1,0:T(1,128)S(1)} %add.149), channel_id=1, source_target_pairs={{0,16},{4,20},{8,24},{12,28},{16,0},{20,4},{24,8},{28,12},{1,17},{... | collective-permute-start | bytes 24584 | tf_op jit(solution)/shard_map/ppermute | solution.py:379
  254.6 3.7 %collective-permute-start.18 = (f32[1,2048]{1,0:T(1,128)S(1)}, f32[1,2048]{1,0:T(1,128)S(1)}, u32[]{:S(2)}, u32[]{:S(2)}) collective-permute-start(f32[1,2048]{1,0:T(1,128)S(1)} %add.150), channel_id=1, source_target_pairs={{0,1},{1,0},{2,3},{3,2},{4,5},{5,4},{6,7},{7,6},{8,9},{9,8},{10,11... | collective-permute-start | bytes 24584 | tf_op jit(solution)/shard_map/ppermute | solution.py:379
  258.4 4.6 %collective-permute-start.19 = (f32[1,2048]{1,0:T(1,128)S(1)}, f32[1,2048]{1,0:T(1,128)S(1)}, u32[]{:S(2)}, u32[]{:S(2)}) collective-permute-start(f32[1,2048]{1,0:T(1,128)S(1)} %add.151), channel_id=1, source_target_pairs={{0,2},{1,3},{2,0},{3,1},{4,6},{5,7},{6,4},{7,5},{8,10},{9,11},{10,... | collective-permute-start | bytes 24584 | tf_op jit(solution)/shard_map/ppermute | solution.py:379
  268.3 1.2 collective-permute-start.20
  269.5 3.7 %collective-permute-start.21 = (f32[1,2048]{1,0:T(1,128)S(1)}, f32[1,2048]{1,0:T(1,128)S(1)}, u32[]{:S(2)}, u32[]{:S(2)}) collective-permute-start(f32[1,2048]{1,0:T(1,128)S(1)} %add.153), channel_id=1, source_target_pairs={{0,8},{4,12},{8,0},{12,4},{16,24},{20,28},{24,16},{28,20},{1,9},{5... | collective-permute-start | bytes 24584 | tf_op jit(solution)/shard_map/ppermute | solution.py:379
  273.3 3.7 %collective-permute-start.22 = (f32[1,2048]{1,0:T(1,128)S(1)}, f32[1,2048]{1,0:T(1,128)S(1)}, u32[]{:S(2)}, u32[]{:S(2)}) collective-permute-start(f32[1,2048]{1,0:T(1,128)S(1)} %add.154), channel_id=1, source_target_pairs={{0,16},{4,20},{8,24},{12,28},{16,0},{20,4},{24,8},{28,12},{1,17},{... | collective-permute-start | bytes 24584 | tf_op jit(solution)/shard_map/ppermute | solution.py:379
  277.0 3.7 %collective-permute-start.23 = (f32[1,2048]{1,0:T(1,128)S(1)}, f32[1,2048]{1,0:T(1,128)S(1)}, u32[]{:S(2)}, u32[]{:S(2)}) collective-permute-start(f32[1,2048]{1,0:T(1,128)S(1)} %add.155), channel_id=1, source_target_pairs={{0,1},{1,0},{2,3},{3,2},{4,5},{5,4},{6,7},{7,6},{8,9},{9,8},{10,11... | collective-permute-start | bytes 24584 | tf_op jit(solution)/shard_map/ppermute | solution.py:379
  280.7 4.6 %collective-permute-start.24 = (f32[1,2048]{1,0:T(1,128)S(1)}, f32[1,2048]{1,0:T(1,128)S(1)}, u32[]{:S(2)}, u32[]{:S(2)}) collective-permute-start(f32[1,2048]{1,0:T(1,128)S(1)} %add.156), channel_id=1, source_target_pairs={{0,2},{1,3},{2,0},{3,1},{4,6},{5,7},{6,4},{7,5},{8,10},{9,11},{10,... | collective-permute-start | bytes 24584 | tf_op jit(solution)/shard_map/ppermute | solution.py:379
  290.4 1.2 collective-permute-start.25
  291.6 3.7 %collective-permute-start.26 = (f32[1,2048]{1,0:T(1,128)S(1)}, f32[1,2048]{1,0:T(1,128)S(1)}, u32[]{:S(2)}, u32[]{:S(2)}) collective-permute-start(f32[1,2048]{1,0:T(1,128)S(1)} %add.158), channel_id=1, source_target_pairs={{0,8},{4,12},{8,0},{12,4},{16,24},{20,28},{24,16},{28,20},{1,9},{5... | collective-permute-start | bytes 24584 | tf_op jit(solution)/shard_map/ppermute | solution.py:379
  295.3 3.7 %collective-permute-start.27 = (f32[1,2048]{1,0:T(1,128)S(1)}, f32[1,2048]{1,0:T(1,128)S(1)}, u32[]{:S(2)}, u32[]{:S(2)}) collective-permute-start(f32[1,2048]{1,0:T(1,128)S(1)} %add.159), channel_id=1, source_target_pairs={{0,16},{4,20},{8,24},{12,28},{16,0},{20,4},{24,8},{28,12},{1,17},{... | collective-permute-start | bytes 24584 | tf_op jit(solution)/shard_map/ppermute | solution.py:379
  299.0 3.7 %collective-permute-start.28 = (f32[1,2048]{1,0:T(1,128)S(1)}, f32[1,2048]{1,0:T(1,128)S(1)}, u32[]{:S(2)}, u32[]{:S(2)}) collective-permute-start(f32[1,2048]{1,0:T(1,128)S(1)} %add.160), channel_id=1, source_target_pairs={{0,1},{1,0},{2,3},{3,2},{4,5},{5,4},{6,7},{7,6},{8,9},{9,8},{10,11... | collective-permute-start | bytes 24584 | tf_op jit(solution)/shard_map/ppermute | solution.py:379
  302.8 4.6 %collective-permute-start.29 = (f32[1,2048]{1,0:T(1,128)S(1)}, f32[1,2048]{1,0:T(1,128)S(1)}, u32[]{:S(2)}, u32[]{:S(2)}) collective-permute-start(f32[1,2048]{1,0:T(1,128)S(1)} %add.161), channel_id=1, source_target_pairs={{0,2},{1,3},{2,0},{3,1},{4,6},{5,7},{6,4},{7,5},{8,10},{9,11},{10,... | collective-permute-start | bytes 24584 | tf_op jit(solution)/shard_map/ppermute | solution.py:379
  312.5 1.2 collective-permute-start.30
  313.7 3.7 %collective-permute-start.31 = (f32[1,2048]{1,0:T(1,128)S(1)}, f32[1,2048]{1,0:T(1,128)S(1)}, u32[]{:S(2)}, u32[]{:S(2)}) collective-permute-start(f32[1,2048]{1,0:T(1,128)S(1)} %add.163), channel_id=1, source_target_pairs={{0,8},{4,12},{8,0},{12,4},{16,24},{20,28},{24,16},{28,20},{1,9},{5... | collective-permute-start | bytes 24584 | tf_op jit(solution)/shard_map/ppermute | solution.py:379
  317.4 3.7 %collective-permute-start.32 = (f32[1,2048]{1,0:T(1,128)S(1)}, f32[1,2048]{1,0:T(1,128)S(1)}, u32[]{:S(2)}, u32[]{:S(2)}) collective-permute-start(f32[1,2048]{1,0:T(1,128)S(1)} %add.164), channel_id=1, source_target_pairs={{0,16},{4,20},{8,24},{12,28},{16,0},{20,4},{24,8},{28,12},{1,17},{... | collective-permute-start | bytes 24584 | tf_op jit(solution)/shard_map/ppermute | solution.py:379
  321.2 3.7 %collective-permute-start.33 = (f32[1,2048]{1,0:T(1,128)S(1)}, f32[1,2048]{1,0:T(1,128)S(1)}, u32[]{:S(2)}, u32[]{:S(2)}) collective-permute-start(f32[1,2048]{1,0:T(1,128)S(1)} %add.165), channel_id=1, source_target_pairs={{0,1},{1,0},{2,3},{3,2},{4,5},{5,4},{6,7},{7,6},{8,9},{9,8},{10,11... | collective-permute-start | bytes 24584 | tf_op jit(solution)/shard_map/ppermute | solution.py:379
  324.9 4.6 %collective-permute-start.34 = (f32[1,2048]{1,0:T(1,128)S(1)}, f32[1,2048]{1,0:T(1,128)S(1)}, u32[]{:S(2)}, u32[]{:S(2)}) collective-permute-start(f32[1,2048]{1,0:T(1,128)S(1)} %add.166), channel_id=1, source_target_pairs={{0,2},{1,3},{2,0},{3,1},{4,6},{5,7},{6,4},{7,5},{8,10},{9,11},{10,... | collective-permute-start | bytes 24584 | tf_op jit(solution)/shard_map/ppermute | solution.py:379
Sparse Core Ops, SparseCore 0:
  65.4 57.1 all-gather.2

commit v4 on v3

--- a/solution.py
+++ b/solution.py
@@ -290,13 +290,15 @@
 
 
 def curve(rows_ref, direction):
-    count, size = rows_ref.shape
+    parts, count, width = rows_ref.shape
+    size = parts * width
     blocks = size // BLOCK
     high = 16
 
     def step(i, total):
         here = pl.ds(pl.multiple_of(i * high, high), high)
-        tile = rows_ref[here, :].astype(jnp.float32)
+        tile = jnp.concatenate([rows_ref[q, here, :] for q in range(parts)], axis=1)
+        tile = tile.astype(jnp.float32)
         sums = jnp.zeros((high, BLOCK), jnp.float32)
         for c in range(blocks):
             cols = slice(c * BLOCK, (c + 1) * BLOCK)
@@ -449,7 +451,9 @@
         wide, (grad_part / total_rows + own_weights)[None], feat_index, 0
     )
     residual = -butterfly(wide.reshape(1, D))
-    own_rows = lax.all_to_all(weighted, "feat", split_axis=0, concat_axis=1, tiled=True)
+    own_rows = lax.all_to_all(
+        weighted.reshape(feat_count, -1, feat_width), "feat", split_axis=0, concat_axis=0, tiled=True
+    )
 
     row, one = (1, D), (1, 1)
     scratch = [pltpu.VMEM((D, BLOCK), jnp.float32)]

time: 345 us -> 357 us (1.035)
  waiting for transfers between devices: 134 us -> 109 us
  starting transfers between devices: 37.1 us -> 59.1 us
  local copies, waits for them, and re-layouts: 2.83 us -> 12.5 us
  other arithmetic: 2.86 us -> 6.5 us
    ppermute x32, waiting for transfers between devices: 119 us -> 92.7 us  [swap(): lax.ppermute(value, axis, [(s, s ^ mask) for s in range(lax.axis_size(axi...]
    ppermute x32, starting transfers between devices: 24.7 us -> 46.7 us  [swap(): lax.ppermute(value, axis, [(s, s ^ mask) for s in range(lax.axis_size(axi...]
    unnamed x17 -> x13, local copies, waits for them, and re-layouts: 0.04 us -> 11.6 us
  transfers between devices with their start and end apart: 37 -> 37, of which waited for: 34 -> 35; matrix products, arithmetic and copies ran while one was open for 1% -> 1% of each run, Pallas kernels for 0% -> 33%
where the time goes in v4:
time: 357 us; the launch traced here: 350 us
  Pallas kernels  138 us (39%)
  waiting for transfers between devices  109 us (31%)
  starting transfers between devices  59.1 us (17%)
  between operations  14.8 us (4%)
  local copies, waits for them, and re-layouts  12.5 us (4%)
  matrix products  10.9 us (3%)
  other arithmetic  6.5 us (2%)
    pallas_call x1, Pallas kernels, factor(): pl.pallas_call(factor_kernel, in_specs=[pl.BlockSpec(memory_space=pltpu.S...  116 us
    ppermute x32, waiting for transfers between devices, swap(): lax.ppermute(value, axis, [(s, s ^ mask) for s in range(lax.axis_size(axi...  92.7 us
    ppermute x32, starting transfers between devices, swap(): lax.ppermute(value, axis, [(s, s ^ mask) for s in range(lax.axis_size(axi...  46.7 us
    pallas_call x5, Pallas kernels, call(): pl.pallas_call(kernel, in_specs=[VMEM] * len(args), out_specs=[VMEM] * le...  21.4 us
    ppermute x3, waiting for transfers between devices, exchange(): lax.ppermute(value, axis, [(s, s ^ mask) for s in range(count)])  15.4 us
    unnamed x13, local copies, waits for them, and re-layouts  11.6 us
    all_to_all x1, starting transfers between devices, local(): lax.all_to_all(weighted.reshape(feat_count, -1, feat_width), 'feat', spli...  8.15 us
  transfers between devices with their start and end apart: 37, of which 35 were waited for; matrix products, arithmetic and copies ran while one was open for 1% of the time, Pallas kernels for 33%

profile of v4, /device:TPU:0, one launch (start us, length us, event | category | flops | bytes accessed | tf_op | source)
XLA Modules:
  0.0 350.2 jit_solution(16880143087312178758)
XLA Ops:
  6.5 3.3 fusion.29
  9.9 3.0 collective-permute-start
  14.5 3.0 collective-permute-start.1
  19.9 2.0 multiply_convert_fusion
  22.0 2.4 fusion.14
  24.5 2.6 collective-permute-done.2
  27.1 2.4 fusion.28
  29.7 1.9 collective-permute-start.3
  31.6 1.5 collective-permute-start.4
  33.1 5.1 %collective-permute-done.3 = f16[256,512]{1,0:T(8,128)(2,1)S(1)} collective-permute-done((f16[256,512]{1,0:T(8,128)(2,1)S(1)}, f16[256,512]{1,0:T(8,128)(2,1)S(1)}, u32[]{:S(2)}, u32[]{:S(2)}) %collective-permute-start.3) | collective-permute-done | bytes 262176 | tf_op jit(solution)/shard_map/ppermute | solution.py:381
  38.2 1.5 collective-permute-done.4
  39.9 1.6 collective-permute-start.5
  42.1 2.8 collective-permute-done.5
  44.9 1.6 collective-permute-done.6
  46.6 2.7 collective-permute-start.8
  49.3 1.3 collective-permute-start.9
  50.9 15.1 %collective-permute-done.8 = bf16[256,512]{1,0:T(8,128)(2,1)S(1)} collective-permute-done((bf16[256,512]{1,0:T(8,128)(2,1)S(1)}, bf16[256,512]{1,0:T(8,128)(2,1)S(1)}, u32[]{:S(2)}, u32[]{:S(2)}) %collective-permute-start.8) | collective-permute-done | bytes 262176 | tf_op jit(solution)/shard_map/ppermute | solution.py:375
  67.4 8.2 %all-to-all-start = ((bf16[4,512,512]{2,1,0:T(8,128)(2,1)}), bf16[4,512,512]{2,1,0:T(8,128)(2,1)S(1)}, u32[]{:S(2)}, u32[]{:S(2)}) async-start(bf16[4,512,512]{2,1,0:T(8,128)(2,1)} %bitcast.32), calls=%async_computation | async-start | bytes 4194304 | tf_op jit(solution)/shard_map/all_to_all | solution.py:454
  75.6 2.7 fusion.30
  80.2 3.4 collective-permute-done.11
  83.8 3.8 %collective-permute-done.12 = f32[1,2048]{1,0:T(1,128)S(1)} collective-permute-done((f32[1,2048]{1,0:T(1,128)S(1)}, f32[1,2048]{1,0:T(1,128)S(1)}, u32[]{:S(2)}, u32[]{:S(2)}) %collective-permute-start.12) | collective-permute-done | bytes 8224 | tf_op jit(solution)/shard_map/ppermute | solution.py:381
  87.6 2.1 collective-permute-start.13
  89.7 20.2 %collective-permute-done.13 = f32[1,2048]{1,0:T(1,128)S(1)} collective-permute-done((f32[1,2048]{1,0:T(1,128)S(1)}, f32[1,2048]{1,0:T(1,128)S(1)}, u32[]{:S(2)}, u32[]{:S(2)}) %collective-permute-start.13) | collective-permute-done | bytes 8224 | tf_op jit(solution)/shard_map/ppermute | solution.py:381
  109.8 4.7 %collective-permute-start.14 = (f32[1,2048]{1,0:T(1,128)S(1)}, f32[1,2048]{1,0:T(1,128)S(1)}, u32[]{:S(2)}, u32[]{:S(2)}) collective-permute-start(f32[1,2048]{1,0:T(1,128)S(1)} %add.146), channel_id=1, source_target_pairs={{0,2},{1,3},{2,0},{3,1},{4,6},{5,7},{6,4},{7,5},{8,10},{9,11},{10,... | collective-permute-start | bytes 24584 | tf_op jit(solution)/shard_map/ppermute | solution.py:381
  114.5 9.8 %collective-permute-done.14 = f32[1,2048]{1,0:T(1,128)S(1)} collective-permute-done((f32[1,2048]{1,0:T(1,128)S(1)}, f32[1,2048]{1,0:T(1,128)S(1)}, u32[]{:S(2)}, u32[]{:S(2)}) %collective-permute-start.14) | collective-permute-done | bytes 8224 | tf_op jit(solution)/shard_map/ppermute | solution.py:381
  124.8 116.4 %shard_map.73 = (f32[2048,2048]{1,0:T(8,128)S(1)}, f32[2048,128]{1,0:T(8,128)S(1)}) custom-call(s32[1]{0:T(128)} %bitcast.feat, bf16[8,4,256,512]{3,2,1,0:T(8,128)(2,1)} %bitcast.31), custom_call_target="tpu_custom_call" | custom-call | tf_op jit(solution)/shard_map/pallas_call | solution.py:229
  241.3 5.8 %copy-done.1 = f32[2048,2048]{1,0:T(8,128)} copy-done((f32[2048,2048]{1,0:T(8,128)}, f32[2048,2048]{1,0:T(8,128)S(1)}, u32[]{:S(2)}) %copy-start.1) | copy-done | bytes 16777240
  247.1 5.8 %copy-done.2 = f32[2048,2048]{1,0:T(8,128)S(1)} copy-done((f32[2048,2048]{1,0:T(8,128)S(1)}, f32[2048,2048]{1,0:T(8,128)}, u32[]{:S(2)}) %copy-start.2) | copy-done | bytes 16777240
  252.8 4.7 %shard_map.74 = (f32[1,2048]{1,0:T(1,128)S(1)}, f32[1,1]{1,0:T(1,128)}, f32[1,2048]{1,0:T(1,128)S(1)}) custom-call(f32[2048,2048]{1,0:T(8,128)S(1)} %copy-done.2, f32[2048,128]{1,0:T(8,128)S(1)} %get-tuple-element.33.inverses, bf16[4,512,512]{2,1,0:T(8,128)(2,1)S(1)} %all-to-all-done.rows, f32[1,2048]{1,0:T(1,128)S(1)} %add_negate_fusion.residual), custom_call_target="tpu_custom_call" | custom-call | tf_op jit(solution)/shard_map/pallas_call | solution.py:361
  258.7 1.5 collective-permute-start.16
  260.2 2.2 collective-permute-done.16
  262.4 1.2 collective-permute-start.17
  263.7 2.5 collective-permute-done.17
  266.2 1.6 collective-permute-start.18
  267.7 2.2 collective-permute-done.18
  269.9 2.5 collective-permute-start.19
  272.4 2.1 collective-permute-done.19
  274.6 5.5 %shard_map.75 = (f32[1,2048]{1,0:T(1,128)S(1)}, f32[1,2048]{1,0:T(1,128)S(1)}, f32[1,2048]{1,0:T(1,128)S(1)}, f32[1,1]{1,0:T(1,128)}, f32[1,2048]{1,0:T(1,128)S(1)}) custom-call(f32[2048,2048]{1,0:T(8,128)S(1)} %copy-done.3, f32[2048,128]{1,0:T(8,128)S(1)} %get-tuple-element.33.inverses, bf16[4,512,512]{2,1,0:T(8,128)(2,1)S(1)} %all-to-all-done.rows, ...), custom_call_target="tpu_custom_call" | custom-call | tf_op jit(solution)/shard_map/pallas_call | solution.py:361
  281.2 1.5 collective-permute-start.21
  282.7 2.2 collective-permute-done.21
  284.9 1.2 collective-permute-start.22
  286.2 2.5 collective-permute-done.22
  288.7 1.6 collective-permute-start.23
  290.2 2.2 collective-permute-done.23
  292.4 2.5 collective-permute-start.24
  294.9 2.1 collective-permute-done.24
  297.0 5.1 %shard_map.76 = (f32[1,2048]{1,0:T(1,128)S(1)}, f32[1,2048]{1,0:T(1,128)S(1)}, f32[1,2048]{1,0:T(1,128)S(1)}, f32[1,1]{1,0:T(1,128)}, f32[1,2048]{1,0:T(1,128)S(1)}) custom-call(f32[2048,2048]{1,0:T(8,128)S(1)} %copy-done.3, f32[2048,128]{1,0:T(8,128)S(1)} %get-tuple-element.33.inverses, bf16[4,512,512]{2,1,0:T(8,128)(2,1)S(1)} %all-to-all-done.rows, ...), custom_call_target="tpu_custom_call" | custom-call | tf_op jit(solution)/shard_map/pallas_call | solution.py:361
  303.4 1.5 collective-permute-start.26
  304.9 2.2 collective-permute-done.26
  307.1 1.2 collective-permute-start.27
  308.3 2.5 collective-permute-done.27
  310.8 1.6 collective-permute-start.28
  312.4 2.2 collective-permute-done.28
  314.5 2.5 collective-permute-start.29
  317.1 2.1 collective-permute-done.29
  319.2 5.1 %shard_map.77 = (f32[1,2048]{1,0:T(1,128)S(1)}, f32[1,2048]{1,0:T(1,128)}, f32[1,2048]{1,0:T(1,128)S(1)}, f32[1,1]{1,0:T(1,128)}, f32[1,2048]{1,0:T(1,128)S(1)}) custom-call(f32[2048,2048]{1,0:T(8,128)S(1)} %copy-done.3, f32[2048,128]{1,0:T(8,128)S(1)} %get-tuple-element.33.inverses, bf16[4,512,512]{2,1,0:T(8,128)(2,1)S(1)} %all-to-all-done.rows, ...), custom_call_target="tpu_custom_call" | custom-call | tf_op jit(solution)/shard_map/pallas_call | solution.py:361
  325.5 1.5 collective-permute-start.31
  327.0 2.2 collective-permute-done.31
  329.2 1.2 collective-permute-start.32
  330.4 2.5 collective-permute-done.32
  332.9 1.6 collective-permute-start.33
  334.5 2.2 collective-permute-done.33
  336.7 2.5 collective-permute-start.34
  339.8 1.5 collective-permute-done.34
  (82 shorter events, 15.8 us)
Async XLA Ops:
  6.5 7.1 %copy-start = (s32[2048]{0:T(1024)S(1)}, s32[2048]{0:T(1024)}, u32[]{:S(2)}) copy-start(s32[2048]{0:T(1024)} %param.11) | copy-start | bytes 24580
  6.5 118.3 %all-gather.3.cloned.1.call-start = ((), (), s32[]{:S(2)}) async-start(), calls=%async_computation.1 | async-start | bytes 9437184 | tf_op jit(solution)/shard_map/all_gather | solution.py:444
  9.9 4.7 %collective-permute-start = (f32[2048]{0:T(1024)S(1)}, f32[2048]{0:T(1024)S(1)}, u32[]{:S(2)}, u32[]{:S(2)}) collective-permute-start(f32[2048]{0:T(1024)S(1)} %bitcast.39), channel_id=1, source_target_pairs={{0,1},{1,0},{2,3},{3,2},{4,5},{5,4},{6,7},{7,6},{8,9},{9,8},{10,11... | collective-permute-start | bytes 24584 | tf_op jit(solution)/shard_map/ppermute | solution.py:381
  14.5 4.7 %collective-permute-start.1 = (f32[2048]{0:T(1024)S(1)}, f32[2048]{0:T(1024)S(1)}, u32[]{:S(2)}, u32[]{:S(2)}) collective-permute-start(f32[2048]{0:T(1024)S(1)} %add.133), channel_id=1, source_target_pairs={{0,2},{1,3},{2,0},{3,1},{4,6},{5,7},{6,4},{7,5},{8,10},{9,11},{10,... | collective-permute-start | bytes 24584 | tf_op jit(solution)/shard_map/ppermute | solution.py:381
  22.0 5.2 %copy-start.4 = (bf16[2048,512]{1,0:T(8,128)(2,1)}, bf16[2048,512]{1,0:T(8,128)(2,1)S(1)}, u32[]{:S(2)}) copy-start(bf16[2048,512]{1,0:T(8,128)(2,1)S(1)} %multiply_convert_fusion) | copy-start | bytes 6291460
  24.4 2.7 collective-permute-start.2
  29.7 8.5 %collective-permute-start.3 = (f16[256,512]{1,0:T(8,128)(2,1)S(1)}, f16[256,512]{1,0:T(8,128)(2,1)S(1)}, u32[]{:S(2)}, u32[]{:S(2)}) collective-permute-start(f16[256,512]{1,0:T(8,128)(2,1)S(1)} %get-tuple-element.54), channel_id=1, source_target_pairs={{0,8},{4,12},{8,0},{12,4},{16,24},{20,28},{24,16},{28,20},{1,9},{5... | collective-permute-start | bytes 786440 | tf_op jit(solution)/shard_map/ppermute | solution.py:381
  31.6 8.1 %collective-permute-start.4 = (f16[256,512]{1,0:T(8,128)(2,1)S(1)}, f16[256,512]{1,0:T(8,128)(2,1)S(1)}, u32[]{:S(2)}, u32[]{:S(2)}) collective-permute-start(f16[256,512]{1,0:T(8,128)(2,1)S(1)} %get-tuple-element.53), channel_id=1, source_target_pairs={{0,16},{4,20},{8,24},{12,28},{16,0},{20,4},{24,8},{28,12},{1,17},{... | collective-permute-start | bytes 786440 | tf_op jit(solution)/shard_map/ppermute | solution.py:381
  39.9 5.0 %collective-permute-start.5 = (f16[128,512]{1,0:T(8,128)(2,1)S(1)}, f16[128,512]{1,0:T(8,128)(2,1)S(1)}, u32[]{:S(2)}, u32[]{:S(2)}) collective-permute-start(f16[128,512]{1,0:T(8,128)(2,1)S(1)} %slice_convert_fusion.1), channel_id=1, source_target_pairs={{0,16},{4,20},{8,24},{12,28},{16,0},{20,4},{24,8},{28,12},{1,17},{... | collective-permute-start | bytes 393224 | tf_op jit(solution)/shard_map/ppermute | solution.py:381
  41.5 5.0 %collective-permute-start.6 = (f16[128,512]{1,0:T(8,128)(2,1)S(1)}, f16[128,512]{1,0:T(8,128)(2,1)S(1)}, u32[]{:S(2)}, u32[]{:S(2)}) collective-permute-start(f16[128,512]{1,0:T(8,128)(2,1)S(1)} %slice_convert_fusion), channel_id=1, source_target_pairs={{0,8},{4,12},{8,0},{12,4},{16,24},{20,28},{24,16},{28,20},{1,9},{5... | collective-permute-start | bytes 393224 | tf_op jit(solution)/shard_map/ppermute | solution.py:381
  46.6 19.4 %collective-permute-start.8 = (bf16[256,512]{1,0:T(8,128)(2,1)S(1)}, bf16[256,512]{1,0:T(8,128)(2,1)S(1)}, u32[]{:S(2)}, u32[]{:S(2)}) collective-permute-start(bf16[256,512]{1,0:T(8,128)(2,1)S(1)} %fusion.20), channel_id=1, source_target_pairs={{0,2},{1,3},{2,0},{3,1},{4,6},{5,7},{6,4},{7,5},{8,10},{9,11},{10,... | collective-permute-start | bytes 786440 | tf_op jit(solution)/shard_map/ppermute | solution.py:375
  49.3 16.8 %collective-permute-start.9 = (bf16[256,512]{1,0:T(8,128)(2,1)S(1)}, bf16[256,512]{1,0:T(8,128)(2,1)S(1)}, u32[]{:S(2)}, u32[]{:S(2)}) collective-permute-start(bf16[256,512]{1,0:T(8,128)(2,1)S(1)} %fusion.20), channel_id=1, source_target_pairs={{0,3},{1,2},{2,1},{3,0},{4,7},{5,6},{6,5},{7,4},{8,11},{9,10},{10,... | collective-permute-start | bytes 786440 | tf_op jit(solution)/shard_map/ppermute | solution.py:375
  50.6 15.7 %collective-permute-start.7 = (bf16[256,512]{1,0:T(8,128)(2,1)S(1)}, bf16[256,512]{1,0:T(8,128)(2,1)S(1)}, u32[]{:S(2)}, u32[]{:S(2)}) collective-permute-start(bf16[256,512]{1,0:T(8,128)(2,1)S(1)} %fusion.20), channel_id=1, source_target_pairs={{0,1},{1,0},{2,3},{3,2},{4,5},{5,4},{6,7},{7,6},{8,9},{9,8},{10,11... | collective-permute-start | bytes 786440 | tf_op jit(solution)/shard_map/ppermute | solution.py:375
  67.4 10.9 %copy-start.5 = (f32[512]{0:T(512)S(1)}, f32[512]{0:T(512)}, u32[]{:S(2)}) copy-start(f32[512]{0:T(512)} %param.8) | copy-start | bytes 6148
  67.4 179.6 %all-to-all-start = ((bf16[4,512,512]{2,1,0:T(8,128)(2,1)}), bf16[4,512,512]{2,1,0:T(8,128)(2,1)S(1)}, u32[]{:S(2)}, u32[]{:S(2)}) async-start(bf16[4,512,512]{2,1,0:T(8,128)(2,1)} %bitcast.32), calls=%async_computation | async-start | bytes 4194304 | tf_op jit(solution)/shard_map/all_to_all | solution.py:454
  78.6 1.2 collective-permute-start.10
  79.8 3.9 %collective-permute-start.11 = (f32[1,2048]{1,0:T(1,128)S(1)}, f32[1,2048]{1,0:T(1,128)S(1)}, u32[]{:S(2)}, u32[]{:S(2)}) collective-permute-start(f32[1,2048]{1,0:T(1,128)S(1)} %add.143), channel_id=1, source_target_pairs={{0,8},{4,12},{8,0},{12,4},{16,24},{20,28},{24,16},{28,20},{1,9},{5... | collective-permute-start | bytes 24584 | tf_op jit(solution)/shard_map/ppermute | solution.py:381
  83.7 3.9 %collective-permute-start.12 = (f32[1,2048]{1,0:T(1,128)S(1)}, f32[1,2048]{1,0:T(1,128)S(1)}, u32[]{:S(2)}, u32[]{:S(2)}) collective-permute-start(f32[1,2048]{1,0:T(1,128)S(1)} %add.144), channel_id=1, source_target_pairs={{0,16},{4,20},{8,24},{12,28},{16,0},{20,4},{24,8},{28,12},{1,17},{... | collective-permute-start | bytes 24584 | tf_op jit(solution)/shard_map/ppermute | solution.py:381
  87.6 22.3 %collective-permute-start.13 = (f32[1,2048]{1,0:T(1,128)S(1)}, f32[1,2048]{1,0:T(1,128)S(1)}, u32[]{:S(2)}, u32[]{:S(2)}) collective-permute-start(f32[1,2048]{1,0:T(1,128)S(1)} %add.145), channel_id=1, source_target_pairs={{0,1},{1,0},{2,3},{3,2},{4,5},{5,4},{6,7},{7,6},{8,9},{9,8},{10,11... | collective-permute-start | bytes 24584 | tf_op jit(solution)/shard_map/ppermute | solution.py:381
  109.8 14.4 %collective-permute-start.14 = (f32[1,2048]{1,0:T(1,128)S(1)}, f32[1,2048]{1,0:T(1,128)S(1)}, u32[]{:S(2)}, u32[]{:S(2)}) collective-permute-start(f32[1,2048]{1,0:T(1,128)S(1)} %add.146), channel_id=1, source_target_pairs={{0,2},{1,3},{2,0},{3,1},{4,6},{5,7},{6,4},{7,5},{8,10},{9,11},{10,... | collective-permute-start | bytes 24584 | tf_op jit(solution)/shard_map/ppermute | solution.py:381
  241.3 5.8 %copy-start.1 = (f32[2048,2048]{1,0:T(8,128)}, f32[2048,2048]{1,0:T(8,128)S(1)}, u32[]{:S(2)}) copy-start(f32[2048,2048]{1,0:T(8,128)S(1)} %get-tuple-element.32.lower) | copy-start | bytes 50331652
  247.1 5.8 %copy-start.2 = (f32[2048,2048]{1,0:T(8,128)S(1)}, f32[2048,2048]{1,0:T(8,128)}, u32[]{:S(2)}) copy-start(f32[2048,2048]{1,0:T(8,128)} %copy-done.1) | copy-start | bytes 50331652
  252.8 21.7 %copy-start.3 = (f32[2048,2048]{1,0:T(8,128)S(1)}, f32[2048,2048]{1,0:T(8,128)}, u32[]{:S(2)}) copy-start(f32[2048,2048]{1,0:T(8,128)} %copy-done.1) | copy-start | bytes 50331652
  257.5 1.2 collective-permute-start.15
  258.7 3.7 %collective-permute-start.16 = (f32[1,2048]{1,0:T(1,128)S(1)}, f32[1,2048]{1,0:T(1,128)S(1)}, u32[]{:S(2)}, u32[]{:S(2)}) collective-permute-start(f32[1,2048]{1,0:T(1,128)S(1)} %add.148), channel_id=1, source_target_pairs={{0,8},{4,12},{8,0},{12,4},{16,24},{20,28},{24,16},{28,20},{1,9},{5... | collective-permute-start | bytes 24584 | tf_op jit(solution)/shard_map/ppermute | solution.py:381
  262.4 3.7 %collective-permute-start.17 = (f32[1,2048]{1,0:T(1,128)S(1)}, f32[1,2048]{1,0:T(1,128)S(1)}, u32[]{:S(2)}, u32[]{:S(2)}) collective-permute-start(f32[1,2048]{1,0:T(1,128)S(1)} %add.149), channel_id=1, source_target_pairs={{0,16},{4,20},{8,24},{12,28},{16,0},{20,4},{24,8},{28,12},{1,17},{... | collective-permute-start | bytes 24584 | tf_op jit(solution)/shard_map/ppermute | solution.py:381
  266.2 3.7 %collective-permute-start.18 = (f32[1,2048]{1,0:T(1,128)S(1)}, f32[1,2048]{1,0:T(1,128)S(1)}, u32[]{:S(2)}, u32[]{:S(2)}) collective-permute-start(f32[1,2048]{1,0:T(1,128)S(1)} %add.150), channel_id=1, source_target_pairs={{0,1},{1,0},{2,3},{3,2},{4,5},{5,4},{6,7},{7,6},{8,9},{9,8},{10,11... | collective-permute-start | bytes 24584 | tf_op jit(solution)/shard_map/ppermute | solution.py:381
  269.9 4.6 %collective-permute-start.19 = (f32[1,2048]{1,0:T(1,128)S(1)}, f32[1,2048]{1,0:T(1,128)S(1)}, u32[]{:S(2)}, u32[]{:S(2)}) collective-permute-start(f32[1,2048]{1,0:T(1,128)S(1)} %add.151), channel_id=1, source_target_pairs={{0,2},{1,3},{2,0},{3,1},{4,6},{5,7},{6,4},{7,5},{8,10},{9,11},{10,... | collective-permute-start | bytes 24584 | tf_op jit(solution)/shard_map/ppermute | solution.py:381
  280.0 1.2 collective-permute-start.20
  281.2 3.7 %collective-permute-start.21 = (f32[1,2048]{1,0:T(1,128)S(1)}, f32[1,2048]{1,0:T(1,128)S(1)}, u32[]{:S(2)}, u32[]{:S(2)}) collective-permute-start(f32[1,2048]{1,0:T(1,128)S(1)} %add.153), channel_id=1, source_target_pairs={{0,8},{4,12},{8,0},{12,4},{16,24},{20,28},{24,16},{28,20},{1,9},{5... | collective-permute-start | bytes 24584 | tf_op jit(solution)/shard_map/ppermute | solution.py:381
  284.9 3.7 %collective-permute-start.22 = (f32[1,2048]{1,0:T(1,128)S(1)}, f32[1,2048]{1,0:T(1,128)S(1)}, u32[]{:S(2)}, u32[]{:S(2)}) collective-permute-start(f32[1,2048]{1,0:T(1,128)S(1)} %add.154), channel_id=1, source_target_pairs={{0,16},{4,20},{8,24},{12,28},{16,0},{20,4},{24,8},{28,12},{1,17},{... | collective-permute-start | bytes 24584 | tf_op jit(solution)/shard_map/ppermute | solution.py:381
  288.7 3.7 %collective-permute-start.23 = (f32[1,2048]{1,0:T(1,128)S(1)}, f32[1,2048]{1,0:T(1,128)S(1)}, u32[]{:S(2)}, u32[]{:S(2)}) collective-permute-start(f32[1,2048]{1,0:T(1,128)S(1)} %add.155), channel_id=1, source_target_pairs={{0,1},{1,0},{2,3},{3,2},{4,5},{5,4},{6,7},{7,6},{8,9},{9,8},{10,11... | collective-permute-start | bytes 24584 | tf_op jit(solution)/shard_map/ppermute | solution.py:381
  292.4 4.6 %collective-permute-start.24 = (f32[1,2048]{1,0:T(1,128)S(1)}, f32[1,2048]{1,0:T(1,128)S(1)}, u32[]{:S(2)}, u32[]{:S(2)}) collective-permute-start(f32[1,2048]{1,0:T(1,128)S(1)} %add.156), channel_id=1, source_target_pairs={{0,2},{1,3},{2,0},{3,1},{4,6},{5,7},{6,4},{7,5},{8,10},{9,11},{10,... | collective-permute-start | bytes 24584 | tf_op jit(solution)/shard_map/ppermute | solution.py:381
  302.2 1.2 collective-permute-start.25
  303.4 3.7 %collective-permute-start.26 = (f32[1,2048]{1,0:T(1,128)S(1)}, f32[1,2048]{1,0:T(1,128)S(1)}, u32[]{:S(2)}, u32[]{:S(2)}) collective-permute-start(f32[1,2048]{1,0:T(1,128)S(1)} %add.158), channel_id=1, source_target_pairs={{0,8},{4,12},{8,0},{12,4},{16,24},{20,28},{24,16},{28,20},{1,9},{5... | collective-permute-start | bytes 24584 | tf_op jit(solution)/shard_map/ppermute | solution.py:381
  307.1 3.7 %collective-permute-start.27 = (f32[1,2048]{1,0:T(1,128)S(1)}, f32[1,2048]{1,0:T(1,128)S(1)}, u32[]{:S(2)}, u32[]{:S(2)}) collective-permute-start(f32[1,2048]{1,0:T(1,128)S(1)} %add.159), channel_id=1, source_target_pairs={{0,16},{4,20},{8,24},{12,28},{16,0},{20,4},{24,8},{28,12},{1,17},{... | collective-permute-start | bytes 24584 | tf_op jit(solution)/shard_map/ppermute | solution.py:381
  310.8 3.7 %collective-permute-start.28 = (f32[1,2048]{1,0:T(1,128)S(1)}, f32[1,2048]{1,0:T(1,128)S(1)}, u32[]{:S(2)}, u32[]{:S(2)}) collective-permute-start(f32[1,2048]{1,0:T(1,128)S(1)} %add.160), channel_id=1, source_target_pairs={{0,1},{1,0},{2,3},{3,2},{4,5},{5,4},{6,7},{7,6},{8,9},{9,8},{10,11... | collective-permute-start | bytes 24584 | tf_op jit(solution)/shard_map/ppermute | solution.py:381
  314.5 4.6 %collective-permute-start.29 = (f32[1,2048]{1,0:T(1,128)S(1)}, f32[1,2048]{1,0:T(1,128)S(1)}, u32[]{:S(2)}, u32[]{:S(2)}) collective-permute-start(f32[1,2048]{1,0:T(1,128)S(1)} %add.161), channel_id=1, source_target_pairs={{0,2},{1,3},{2,0},{3,1},{4,6},{5,7},{6,4},{7,5},{8,10},{9,11},{10,... | collective-permute-start | bytes 24584 | tf_op jit(solution)/shard_map/ppermute | solution.py:381
  324.3 1.2 collective-permute-start.30
  325.5 3.7 %collective-permute-start.31 = (f32[1,2048]{1,0:T(1,128)S(1)}, f32[1,2048]{1,0:T(1,128)S(1)}, u32[]{:S(2)}, u32[]{:S(2)}) collective-permute-start(f32[1,2048]{1,0:T(1,128)S(1)} %add.163), channel_id=1, source_target_pairs={{0,8},{4,12},{8,0},{12,4},{16,24},{20,28},{24,16},{28,20},{1,9},{5... | collective-permute-start | bytes 24584 | tf_op jit(solution)/shard_map/ppermute | solution.py:381
  329.2 3.7 %collective-permute-start.32 = (f32[1,2048]{1,0:T(1,128)S(1)}, f32[1,2048]{1,0:T(1,128)S(1)}, u32[]{:S(2)}, u32[]{:S(2)}) collective-permute-start(f32[1,2048]{1,0:T(1,128)S(1)} %add.164), channel_id=1, source_target_pairs={{0,16},{4,20},{8,24},{12,28},{16,0},{20,4},{24,8},{28,12},{1,17},{... | collective-permute-start | bytes 24584 | tf_op jit(solution)/shard_map/ppermute | solution.py:381
  332.9 3.7 %collective-permute-start.33 = (f32[1,2048]{1,0:T(1,128)S(1)}, f32[1,2048]{1,0:T(1,128)S(1)}, u32[]{:S(2)}, u32[]{:S(2)}) collective-permute-start(f32[1,2048]{1,0:T(1,128)S(1)} %add.165), channel_id=1, source_target_pairs={{0,1},{1,0},{2,3},{3,2},{4,5},{5,4},{6,7},{7,6},{8,9},{9,8},{10,11... | collective-permute-start | bytes 24584 | tf_op jit(solution)/shard_map/ppermute | solution.py:381
  336.7 4.6 %collective-permute-start.34 = (f32[1,2048]{1,0:T(1,128)S(1)}, f32[1,2048]{1,0:T(1,128)S(1)}, u32[]{:S(2)}, u32[]{:S(2)}) collective-permute-start(f32[1,2048]{1,0:T(1,128)S(1)} %add.166), channel_id=1, source_target_pairs={{0,2},{1,3},{2,0},{3,1},{4,6},{5,7},{6,4},{7,5},{8,10},{9,11},{10,... | collective-permute-start | bytes 24584 | tf_op jit(solution)/shard_map/ppermute | solution.py:381
Sparse Core Ops, SparseCore 0:
  67.5 57.2 all-gather.2
